TPU v7x, 32 devices: a whole 2x2x4 slice. The times are simulated.
32 devices in a mesh: expert: 8 (over z, core), shard: 4 (over y, x).
Axes of the slice: x: 2, y: 2, z: 4, core: 2. Of those that a mesh axis runs over, the one named last changes fastest.
Arguments:
- tokens: bfloat16 [16384, 1024], P(('expert', 'shard')), may hold values from -6 to 6
- gain_attn: bfloat16 [1024], P('shard'), may hold values from 0.099609375 to 1.8984375
- w_query: bfloat16 [1024, 1024], P('shard'), may hold values from -0.1875 to 0.1875
- key_weight: bfloat16 [1024, 512], P('shard'), may hold values from -0.1875 to 0.1875
- value_weight: bfloat16 [1024, 512], P('shard'), may hold values from -0.1875 to 0.1875
- w_out: bfloat16 [1024, 1024], P('shard'), may hold values from -1.5 to 1.5
- gain_mix: bfloat16 [1024], P('shard'), may hold values from 0.099609375 to 1.8984375
- router: bfloat16 [1024, 16], P('shard'), may hold values from -0.09375 to 0.09375
- w_gate: bfloat16 [16, 1024, 512], P('expert', 'shard'), may hold values from -0.1875 to 0.1875
- w_up: bfloat16 [16, 1024, 512], P('expert', 'shard'), may hold values from -0.1875 to 0.1875
- w_down: bfloat16 [16, 512, 1024], P('expert', 'shard'), may hold values from -0.75 to 0.75
- routes: int32 [16384, 8], P(('expert', 'shard')), may hold values from 0 to 15, all different within a row; in each aligned block of 512 rows (0 to 511, 512 to 1023, ...) at most 384 rows name the same one
- lengths: int32 [32, 4], P(('expert', 'shard')), may hold values from 1 to 256, 512 in all within a row
- cotangent: bfloat16 [16384, 1024], P(('expert', 'shard')), may hold values from -6 to 6
Outputs:
- out_tokens: bfloat16 [16384, 1024], P(('expert', 'shard'))
- grad_tokens: bfloat16 [16384, 1024], P(('expert', 'shard'))
- grad_gain_attn: float32 [1024], P('shard')
- grad_w_query: float32 [1024, 1024], P('shard')
- grad_w_key: float32 [1024, 512], P('shard')
- grad_w_value: float32 [1024, 512], P('shard')
- grad_w_out: float32 [1024, 1024], P('shard')
- grad_gain_mix: float32 [1024], P('shard')
- grad_router: float32 [1024, 16], P('shard')
- grad_w_gate: float32 [16, 1024, 512], P('expert', 'shard')
- grad_w_up: float32 [16, 1024, 512], P('expert', 'shard')
- grad_w_down: float32 [16, 512, 1024], P('expert', 'shard')
Inputs may be any that keep to these rules, and one draw needn't show every extreme that they name: `routes`: each row names 8 different experts. The 512 rows of one device name no expert more than 384 times, and in every draw some device's rows name some expert exactly 384 times. Row b holds, in order, the lengths of the 4 documents of token block b; each row sums to 512 and its longest is exactly 256.
All inputs are finite; a program needn't handle non-finite values.
Results may differ from a plain program's by a relative error of at most 0.02.
Values may be sent and summed in bfloat16 or wider, within the bound.
No kernel may reach another device: no remote copies, remote signals or barrier semaphores. Data moves between devices by JAX's collectives and lax.ppermute only.
A program may use at most 256 MiB of HBM per device.

v0:
```python
import math

import jax
import jax.numpy as jnp
from jax import lax
from jax.sharding import PartitionSpec as P

QUERY_HEADS = 16
KEY_VALUE_HEADS = 8
HEAD_DIM = 64


def normalize(values, gain_vector):
    return (
        values * lax.rsqrt(jnp.mean(values * values, axis=-1, keepdims=True) + 1e-06) * gain_vector
    )


def apply_rotary(values, cosine_table, sine_lookup):
    half_width = values.shape[-1] // 2
    first_half = values[..., :half_width]
    second_half = values[..., half_width:]
    return jnp.concatenate(
        [
            first_half * cosine_table - second_half * sine_lookup,
            second_half * cosine_table + first_half * sine_lookup,
        ],
        axis=-1,
    )


def place_tables(lengths_row, total_rows, head_width):
    doc_ends = jnp.cumsum(lengths_row)
    token_index = jnp.arange(total_rows, dtype=jnp.int32)
    past_end = token_index[:, None] >= doc_ends[None, :]
    document = jnp.sum(past_end.astype(jnp.int32), axis=1)
    doc_start = jnp.sum(jnp.where(past_end, lengths_row[None, :], 0), axis=1)
    position = (token_index - doc_start).astype(jnp.float32)
    half_width = head_width // 2
    inverse = 10000.0 ** (-(jnp.arange(half_width, dtype=jnp.float32) * 2.0 / head_width))
    angles = position[:, None] * inverse[None, :]
    allowed = (document[:, None] == document[None, :]) & (
        token_index[None, :] <= token_index[:, None]
    )
    return (jnp.cos(angles)[:, None, :], jnp.sin(angles)[:, None, :], allowed)


def matrix_product(left_side, right_side):
    return jnp.dot(left_side, right_side, preferred_element_type=jnp.float32)


def product_tn(left_side, right_side):
    return lax.dot_general(
        left_side, right_side, (((0,), (0,)), ((), ())), preferred_element_type=jnp.float32
    )


def product_transposed_right(left_side, right_side):
    return lax.dot_general(
        left_side, right_side, (((1,), (1,)), ((), ())), preferred_element_type=jnp.float32
    )


def per_device(
    tokens,
    gain_attn,
    w_query,
    key_weight,
    value_weight,
    w_out,
    gain_mix,
    router,
    w_gate,
    w_up,
    w_down,
    routes,
    lengths,
    cotangent,
):
    gain_one, query_w, key_matrix, value_matrix, output_matrix, gain_two, router_w = (
        lax.all_gather(gain_attn, "shard", axis=0, tiled=True),
        lax.all_gather(w_query, "shard", axis=0, tiled=True),
        lax.all_gather(key_weight, "shard", axis=0, tiled=True),
        lax.all_gather(value_weight, "shard", axis=0, tiled=True),
        lax.all_gather(w_out, "shard", axis=0, tiled=True),
        lax.all_gather(gain_mix, "shard", axis=0, tiled=True),
        lax.all_gather(router, "shard", axis=0, tiled=True),
    )
    gate_w, up_w, down_w = (
        lax.all_gather(w_gate, "shard", axis=1, tiled=True),
        lax.all_gather(w_up, "shard", axis=1, tiled=True),
        lax.all_gather(w_down, "shard", axis=1, tiled=True),
    )
    total_rows, model_width = tokens.shape
    query_group_width = QUERY_HEADS // KEY_VALUE_HEADS
    route_count = routes.shape[1]
    experts = router_w.shape[1]
    local_experts = gate_w.shape[0]
    peer_count = lax.axis_size("expert")
    capacity = 3 * total_rows * route_count // (2 * experts)
    score_scale = 1.0 / math.sqrt(HEAD_DIM)
    inputs = tokens.astype(jnp.float32)
    gain_first = gain_one.astype(jnp.float32)
    gain_second = gain_two.astype(jnp.float32)
    normalized_input = normalize(inputs, gain_first).astype(jnp.bfloat16)
    cosine_table, sine_lookup, allowed = place_tables(lengths[0], total_rows, HEAD_DIM)
    query_raw = matrix_product(normalized_input, query_w).reshape(total_rows, QUERY_HEADS, HEAD_DIM)
    unrotated_keys = matrix_product(normalized_input, key_matrix).reshape(
        total_rows, KEY_VALUE_HEADS, HEAD_DIM
    )
    query_rows = (
        apply_rotary(query_raw, cosine_table, sine_lookup)
        .astype(jnp.bfloat16)
        .reshape(total_rows, KEY_VALUE_HEADS, query_group_width, HEAD_DIM)
    )
    key_matrix_rows = apply_rotary(unrotated_keys, cosine_table, sine_lookup).astype(jnp.bfloat16)
    value_matrix_rows = (
        matrix_product(normalized_input, value_matrix)
        .astype(jnp.bfloat16)
        .reshape(total_rows, KEY_VALUE_HEADS, HEAD_DIM)
    )

    def score_table():
        raw_scores = (
            jnp.einsum(
                "vuol,mul->uovm", query_rows, key_matrix_rows, preferred_element_type=jnp.float32
            )
            * score_scale
        )
        return jnp.where(allowed[None, None], raw_scores, -1e30)

    scores = score_table()
    top_score = jnp.max(scores, axis=-1, keepdims=True)
    weights = jnp.exp(scores - top_score)
    sum_weights = jnp.sum(weights, axis=-1, keepdims=True)
    probability = weights / sum_weights
    log_total = top_score + jnp.log(sum_weights)
    lower_probabilities = probability.astype(jnp.bfloat16)
    attended = (
        jnp.einsum(
            "yjvu,uyw->vyjw",
            lower_probabilities,
            value_matrix_rows,
            preferred_element_type=jnp.float32,
        )
        .astype(jnp.bfloat16)
        .reshape(total_rows, QUERY_HEADS * HEAD_DIM)
    )
    hidden_state = inputs + matrix_product(attended, output_matrix)
    mixed_in = normalize(hidden_state, gain_second).astype(jnp.bfloat16)
    logits = matrix_product(mixed_in, router_w)
    gate_probs = jax.nn.softmax(jnp.take_along_axis(logits, routes, axis=1), axis=-1)
    flat_routes = routes.reshape(-1)
    expert_ids = jnp.arange(experts, dtype=jnp.int32)
    onehot = (flat_routes[:, None] == expert_ids[None, :]).astype(jnp.int32)
    earlier = jnp.sum((jnp.cumsum(onehot, axis=0) - onehot) * onehot, axis=1)
    slot_index = flat_routes * capacity + earlier
    owner_rows = jnp.repeat(mixed_in, route_count, axis=0)
    outgoing = (
        jnp.zeros((experts * capacity, model_width), jnp.bfloat16).at[slot_index].set(owner_rows)
    )
    outgoing = outgoing.reshape(peer_count, local_experts, capacity, model_width)
    arrived = lax.all_to_all(outgoing, "expert", split_axis=0, concat_axis=0, tiled=True)
    gate_val = jnp.einsum("sjcd,jdf->sjcf", arrived, gate_w, preferred_element_type=jnp.float32)
    up_val = jnp.einsum("sjcd,jdf->sjcf", arrived, up_w, preferred_element_type=jnp.float32)
    inner_act = (jax.nn.silu(gate_val) * up_val).astype(jnp.bfloat16)
    result = jnp.einsum(
        "sjcf,jfd->sjcd", inner_act, down_w, preferred_element_type=jnp.float32
    ).astype(jnp.bfloat16)
    returned = lax.all_to_all(result, "expert", split_axis=0, concat_axis=0, tiled=True)
    returned, arrived = (returned, arrived)
    expert_out = returned.reshape(experts * capacity, model_width)[slot_index].reshape(
        total_rows, route_count, model_width
    )
    output = hidden_state + jnp.sum(gate_probs[:, :, None] * expert_out.astype(jnp.float32), axis=1)
    upstream = cotangent.astype(jnp.float32)
    gate_grad = jnp.sum(upstream[:, None, :] * expert_out.astype(jnp.float32), axis=2)
    slot_grad = (
        (gate_probs[:, :, None] * upstream[:, None, :])
        .astype(jnp.bfloat16)
        .reshape(total_rows * route_count, model_width)
    )
    grad_slots = (
        jnp.zeros((experts * capacity, model_width), jnp.bfloat16).at[slot_index].set(slot_grad)
    )
    grad_slots = grad_slots.reshape(peer_count, local_experts, capacity, model_width)
    arrived_grad = lax.all_to_all(grad_slots, "expert", split_axis=0, concat_axis=0, tiled=True)
    gate_val = jnp.einsum("sjcd,jdf->sjcf", arrived, gate_w, preferred_element_type=jnp.float32)
    up_val = jnp.einsum("sjcd,jdf->sjcf", arrived, up_w, preferred_element_type=jnp.float32)
    sigmoid_gate = jax.nn.sigmoid(gate_val)
    swish_gate = gate_val * sigmoid_gate
    inner_act = (swish_gate * up_val).astype(jnp.bfloat16)
    inner_grad = jnp.einsum(
        "sjcd,jfd->sjcf", arrived_grad, down_w, preferred_element_type=jnp.float32
    )
    gate_back = (
        inner_grad * up_val * sigmoid_gate * (1.0 + gate_val * (1.0 - sigmoid_gate))
    ).astype(jnp.bfloat16)
    up_back = (inner_grad * swish_gate).astype(jnp.bfloat16)
    down_grad_w = jnp.einsum(
        "sjcf,sjcd->jfd", inner_act, arrived_grad, preferred_element_type=jnp.float32
    )
    gate_grad_w = jnp.einsum(
        "sjcd,sjcf->jdf", arrived, gate_back, preferred_element_type=jnp.float32
    )
    up_grad_w = jnp.einsum("sjcd,sjcf->jdf", arrived, up_back, preferred_element_type=jnp.float32)
    row_grad = jnp.einsum("sjcf,jdf->sjcd", gate_back, gate_w, preferred_element_type=jnp.float32)
    row_grad = (
        row_grad + jnp.einsum("sjcf,jdf->sjcd", up_back, up_w, preferred_element_type=jnp.float32)
    ).astype(jnp.bfloat16)
    row_back = lax.all_to_all(row_grad, "expert", split_axis=0, concat_axis=0, tiled=True)
    expert_gate_sum, expert_up_sum, expert_down_sum = (
        lax.psum_scatter(
            gate_grad_w.astype(jnp.bfloat16), "shard", scatter_dimension=1, tiled=True
        ).astype(jnp.float32),
        lax.psum_scatter(
            up_grad_w.astype(jnp.bfloat16), "shard", scatter_dimension=1, tiled=True
        ).astype(jnp.float32),
        lax.psum_scatter(
            down_grad_w.astype(jnp.bfloat16), "shard", scatter_dimension=1, tiled=True
        ).astype(jnp.float32),
    )
    chosen_grad = gate_probs * (gate_grad - jnp.sum(gate_probs * gate_grad, axis=1, keepdims=True))
    matches = routes[:, :, None] == expert_ids[None, None, :]
    logit_grad = jnp.sum(jnp.where(matches, chosen_grad[:, :, None], 0.0), axis=1).astype(
        jnp.bfloat16
    )
    router_grad = product_tn(mixed_in, logit_grad)
    returned_rows = row_back.reshape(experts * capacity, model_width)[slot_index].reshape(
        total_rows, route_count, model_width
    )
    mixed_grad = product_transposed_right(logit_grad, router_w) + jnp.sum(
        returned_rows.astype(jnp.float32), axis=1
    )
    _, second_back = jax.vjp(normalize, hidden_state, gain_second)
    state_part, gain_two_grad = second_back(mixed_grad)
    state_grad = upstream + state_part
    branch_gradient = state_grad.astype(jnp.bfloat16)
    out_grad_w = product_tn(attended, branch_gradient)
    attended_gradient = (
        product_transposed_right(branch_gradient, output_matrix)
        .astype(jnp.bfloat16)
        .reshape(total_rows, KEY_VALUE_HEADS, query_group_width, HEAD_DIM)
    )
    probability = jnp.exp(score_table() - log_total)
    prob_grad = jnp.einsum(
        "vuol,mul->uovm", attended_gradient, value_matrix_rows, preferred_element_type=jnp.float32
    )
    score_gradient = (
        probability * (prob_grad - jnp.sum(probability * prob_grad, axis=-1, keepdims=True))
    ).astype(jnp.bfloat16)
    query_grad = (
        jnp.einsum(
            "yjvu,uyw->vyjw", score_gradient, key_matrix_rows, preferred_element_type=jnp.float32
        )
        * score_scale
    )
    key_gradient = (
        jnp.einsum("cuyf,ycul->fcl", score_gradient, query_rows, preferred_element_type=jnp.float32)
        * score_scale
    )
    value_gradient = jnp.einsum(
        "cuyf,ycul->fcl", lower_probabilities, attended_gradient, preferred_element_type=jnp.float32
    )
    query_back = (
        apply_rotary(
            query_grad.reshape(total_rows, QUERY_HEADS, HEAD_DIM), cosine_table, -sine_lookup
        )
        .astype(jnp.bfloat16)
        .reshape(total_rows, QUERY_HEADS * HEAD_DIM)
    )
    key_back = (
        apply_rotary(key_gradient, cosine_table, -sine_lookup)
        .astype(jnp.bfloat16)
        .reshape(total_rows, KEY_VALUE_HEADS * HEAD_DIM)
    )
    value_backward = value_gradient.astype(jnp.bfloat16).reshape(
        total_rows, KEY_VALUE_HEADS * HEAD_DIM
    )
    query_grad_w = product_tn(normalized_input, query_back)
    key_grad_w = product_tn(normalized_input, key_back)
    value_grad_w = product_tn(normalized_input, value_backward)
    normed_grad = (
        product_transposed_right(query_back, query_w)
        + product_transposed_right(key_back, key_matrix)
        + product_transposed_right(value_backward, value_matrix)
    )
    _, first_back = jax.vjp(normalize, inputs, gain_first)
    input_part, gain_one_grad = first_back(normed_grad)
    input_grad = state_grad + input_part
    part_one, part_query, part_key, part_value, part_out, part_two, part_router = (
        lax.psum_scatter(
            gain_one_grad.astype(jnp.bfloat16), "shard", scatter_dimension=0, tiled=True
        ).astype(jnp.float32),
        lax.psum_scatter(
            query_grad_w.astype(jnp.bfloat16), "shard", scatter_dimension=0, tiled=True
        ).astype(jnp.float32),
        lax.psum_scatter(
            key_grad_w.astype(jnp.bfloat16), "shard", scatter_dimension=0, tiled=True
        ).astype(jnp.float32),
        lax.psum_scatter(
            value_grad_w.astype(jnp.bfloat16), "shard", scatter_dimension=0, tiled=True
        ).astype(jnp.float32),
        lax.psum_scatter(
            out_grad_w.astype(jnp.bfloat16), "shard", scatter_dimension=0, tiled=True
        ).astype(jnp.float32),
        lax.psum_scatter(
            gain_two_grad.astype(jnp.bfloat16), "shard", scatter_dimension=0, tiled=True
        ).astype(jnp.float32),
        lax.psum_scatter(
            router_grad.astype(jnp.bfloat16), "shard", scatter_dimension=0, tiled=True
        ).astype(jnp.float32),
    )
    sum_one, sum_query, sum_key, sum_value, sum_out, sum_two, sum_router = (
        lax.psum(part_one.astype(jnp.bfloat16), "expert").astype(jnp.float32),
        lax.psum(part_query.astype(jnp.bfloat16), "expert").astype(jnp.float32),
        lax.psum(part_key.astype(jnp.bfloat16), "expert").astype(jnp.float32),
        lax.psum(part_value.astype(jnp.bfloat16), "expert").astype(jnp.float32),
        lax.psum(part_out.astype(jnp.bfloat16), "expert").astype(jnp.float32),
        lax.psum(part_two.astype(jnp.bfloat16), "expert").astype(jnp.float32),
        lax.psum(part_router.astype(jnp.bfloat16), "expert").astype(jnp.float32),
    )
    return (
        output.astype(jnp.bfloat16),
        input_grad.astype(jnp.bfloat16),
        sum_one,
        sum_query,
        sum_key,
        sum_value,
        sum_out,
        sum_two,
        sum_router,
        expert_gate_sum,
        expert_up_sum,
        expert_down_sum,
    )


def solution(mesh):
    in_specs = (
        P(("expert", "shard"), None),
        P("shard"),
        P("shard", None),
        P("shard", None),
        P("shard", None),
        P("shard", None),
        P("shard"),
        P("shard", None),
        P("expert", "shard", None),
        P("expert", "shard", None),
        P("expert", "shard", None),
        P(("expert", "shard"), None),
        P(("expert", "shard"), None),
        P(("expert", "shard"), None),
    )
    out_specs = (
        P(("expert", "shard"), None),
        P(("expert", "shard"), None),
        P("shard"),
        P("shard", None),
        P("shard", None),
        P("shard", None),
        P("shard", None),
        P("shard"),
        P("shard", None),
        P("expert", "shard", None),
        P("expert", "shard", None),
        P("expert", "shard", None),
    )
    return jax.shard_map(
        per_device, mesh=mesh, in_specs=in_specs, out_specs=out_specs, check_vma=False
    )
```

profile of v0, /device:TPU:0, one launch (start us, length us, event | category | flops | bytes accessed | tf_op | source)
XLA Modules:
  0.0 1632.2 jit_solution(1266696090533430635)
XLA Ops:
  41.6 26.2 %all-gather.10.cloned.1.call-done = bf16[1024,512]{1,0:T(8,128)(2,1)} async-done(((bf16[256,512]{1,0:T(8,128)(2,1)}), bf16[1024,512]{1,0:T(8,128)(2,1)}) %all-gather.10.cloned.1.call-update) | async-done | bytes 1048592 | tf_op jit(solution)/shard_map/all_gather | solution.py:84
  69.9 35.1 %all-gather.14.cloned.1.call-done = bf16[1024,1024]{1,0:T(8,128)(2,1)} async-done(((bf16[256,1024]{1,0:T(8,128)(2,1)}), bf16[1024,1024]{1,0:T(8,128)(2,1)}) %all-gather.14.cloned.1.call-update) | async-done | bytes 2097168 | tf_op jit(solution)/shard_map/all_gather | solution.py:82
  146.6 25.7 %scatter_custom_fusion = bf16[6144,1024]{1,0:T(8,128)(2,1)} fusion(s32[4096]{0:T(1024)S(1)} %bitcast.243, bf16[]{:T(256)} %constant.58.clone.1, bf16[512,1024]{1,0:T(8,128)(2,1)S(1)} %multiply_convert_fusion), kind=kCustom, calls=%fused_computation.49 | custom fusion | bytes 13631490 | tf_op jit(solution)/shard_map/scatter | solution.py:160
  189.2 33.0 %gather_fusion.2 = f32[4096]{0:T(1024)S(1)} fusion(f32[512,16]{0,1:T(8,128)S(1)} %fusion.90, s32[4096]{0:T(1024)S(1)} %reshape.427), kind=kCustom, calls=%fused_computation.2 | custom fusion | bytes 65536 | tf_op jit(solution)/shard_map/jit(take_along_axis)/gather | solution.py:152
  223.0 27.3 %scatter_custom_fusion.1 = bf16[6144,1024]{1,0:T(8,128)(2,1)} fusion(s32[4096]{0:T(1024)S(1)} %bitcast.244, f32[4096]{0:T(1024)S(1)} %mul.407, f32[512,1024]{1,0:T(8,128)S(1)} %convert_element_type.220, bf16[]{:T(256)} %constant.58.clone.1), kind=kCustom, calls=%fused_computation.48 | custom fusion | flops 8388608 | bytes 14696450 | tf_op jit(solution)/shard_map/scatter | solution.py:184
  250.3 201.3 %all-to-all-done = bf16[8,2,384,1024]{3,2,1,0:T(8,128)(2,1)} async-done(((bf16[8,2,384,1024]{3,2,1,0:T(8,128)(2,1)}), bf16[8,2,384,1024]{3,2,1,0:T(8,128)(2,1)}, u32[]{:S(2)}, u32[]{:S(2)}) %all-to-all-start) | async-done | bytes 12582944 | tf_op jit(solution)/shard_map/all_to_all | solution.py:163
  458.9 36.2 %all-gather.20.cloned.1.call-done = bf16[2,1024,512]{2,1,0:T(8,128)(2,1)} async-done(((bf16[2,256,512]{2,1,0:T(8,128)(2,1)}), bf16[2,1024,512]{2,1,0:T(8,128)(2,1)}) %all-gather.20.cloned.1.call-update) | async-done | bytes 2097168 | tf_op jit(solution)/shard_map/all_gather | solution.py:91
  495.1 14.5 fusion.21
  509.5 22.6 %all-gather.18.cloned.1.call-done = bf16[2,1024,512]{2,1,0:T(8,128)(2,1)} async-done(((bf16[2,256,512]{2,1,0:T(8,128)(2,1)}), bf16[2,1024,512]{2,1,0:T(8,128)(2,1)}) %all-gather.18.cloned.1.call-update) | async-done | bytes 2097168 | tf_op jit(solution)/shard_map/all_gather | solution.py:90
  532.1 14.5 fusion.23
  546.7 22.6 %all-gather.22.cloned.1.call-done = bf16[2,512,1024]{2,1,0:T(8,128)(2,1)} async-done(((bf16[2,128,1024]{2,1,0:T(8,128)(2,1)}), bf16[2,512,1024]{2,1,0:T(8,128)(2,1)}) %all-gather.22.cloned.1.call-update) | async-done | bytes 2097168 | tf_op jit(solution)/shard_map/all_gather | solution.py:92
  569.3 161.4 %all-to-all-done.2 = bf16[8,2,384,1024]{3,2,1,0:T(8,128)(2,1)} async-done(((bf16[8,2,384,1024]{3,2,1,0:T(8,128)(2,1)}), bf16[8,2,384,1024]{3,2,1,0:T(8,128)(2,1)}, u32[]{:S(2)}, u32[]{:S(2)}) %all-to-all-start.2) | async-done | bytes 12582944 | tf_op jit(solution)/shard_map/all_to_all | solution.py:187
  730.7 25.1 %fusion.11 = (bf16[8,2,384,512]{3,2,0,1:T(8,128)(2,1)}, bf16[8,2,384,512]{3,2,0,1:T(8,128)(2,1)}, bf16[8,2,384,512]{3,2,0,1:T(8,128)(2,1)}) fusion(f32[2,8,384,512]{3,2,1,0:T(8,128)} %fusion.23, f32[2,8,384,512]{3,2,1,0:T(8,128)} %fusion.21, bf16[2,512,1024]{2,1,0:T(8,128)(2,1)} %all-gather.22.cloned.1.call-done, bf16[8,2,384,1024]{3,2,1,0:T(8,128)(2,1)} %all-to-all-done.2), kind=kOutput, calls=%fused_computation.29 | convolution fusion | flops 6489636864 | bytes 58720256 | tf_op jit(solution)/shard_map/sjcd,jfd->sjcf/dot_general | solution.py:193
  776.6 14.5 fusion.55
  791.1 17.0 %fusion.7 = bf16[8,2,384,1024]{3,2,0,1:T(8,128)(2,1)} fusion(f32[2,8,384,1024]{3,2,1,0:T(8,128)} %fusion.55, bf16[8,2,384,512]{3,2,0,1:T(8,128)(2,1)} %get-tuple-element.29, bf16[2,1024,512]{2,1,0:T(8,128)(2,1)S(1)} %copy-done.64), kind=kOutput, calls=%fused_computation.23 | convolution fusion | flops 6455033856 | bytes 46137344 | tf_op jit(solution)/shard_map/sjcf,jdf->sjcd/dot_general | solution.py:209
  818.6 231.8 %all-to-all-done.1 = bf16[8,2,384,1024]{3,2,1,0:T(8,128)(2,1)} async-done(((bf16[8,2,384,1024]{3,2,1,0:T(8,128)(2,1)}), bf16[8,2,384,1024]{3,2,1,0:T(8,128)(2,1)}, u32[]{:S(2)}, u32[]{:S(2)}) %all-to-all-start.1) | async-done | bytes 12582944 | tf_op jit(solution)/shard_map/all_to_all | solution.py:170
  1055.7 13.8 bitcast_convert_fusion
  1096.0 27.4 %gather_fusion = bf16[4096,1024]{1,0:T(8,128)(2,1)} fusion(bf16[6144,1024]{1,0:T(8,128)(2,1)} %bitcast.32, s32[4096]{0:T(1024)S(1)} %broadcast_clamp_fusion), kind=kCustom, calls=%fused_computation | custom fusion | bytes 16793600 | tf_op jit(solution)/shard_map/gather | solution.py:172
  1133.6 195.8 %all-to-all-done.3 = bf16[8,2,384,1024]{3,2,1,0:T(8,128)(2,1)} async-done(((bf16[8,2,384,1024]{3,2,1,0:T(8,128)(2,1)}), bf16[8,2,384,1024]{3,2,1,0:T(8,128)(2,1)}, u32[]{:S(2)}, u32[]{:S(2)}) %all-to-all-start.3) | async-done | bytes 12582944 | tf_op jit(solution)/shard_map/all_to_all | solution.py:211
  1329.5 27.0 %gather_fusion.1 = bf16[4096,1024]{1,0:T(8,128)(2,1)} fusion(bf16[6144,1024]{1,0:T(8,128)(2,1)} %bitcast.42, s32[4096]{0:T(1024)S(1)} %broadcast_clamp_fusion), kind=kCustom, calls=%fused_computation.1 | custom fusion | bytes 16793600 | tf_op jit(solution)/shard_map/gather | solution.py:229
  1452.0 38.5 %reduce-scatter.15.cloned.1.call-done = bf16[256,1024]{1,0:T(8,128)(2,1)} async-done(((bf16[1024,1024]{1,0:T(8,128)(2,1)}), bf16[256,1024]{1,0:T(8,128)(2,1)}) %reduce-scatter.15.cloned.1.call-update) | async-done | bytes 524304 | tf_op jit(solution)/shard_map/reduce_scatter | solution.py:304
  1490.5 38.0 %reduce-scatter.9.cloned.1.call-done = bf16[256,1024]{1,0:T(8,128)(2,1)} async-done(((bf16[1024,1024]{1,0:T(8,128)(2,1)}), bf16[256,1024]{1,0:T(8,128)(2,1)}) %reduce-scatter.9.cloned.1.call-update) | async-done | bytes 524304 | tf_op jit(solution)/shard_map/reduce_scatter | solution.py:295
  1554.4 16.7 %all-reduce.2 = (bf16[256]{0:T(256)(128)(2,1)S(1)}, bf16[256]{0:T(256)(128)(2,1)S(1)}, bf16[256,16]{0,1:T(8,128)(2,1)S(1)}) all-reduce(bf16[256]{0:T(256)(128)(2,1)S(1)} %dynamic-slice.1, bf16[256]{0:T(256)(128)(2,1)S(1)} %dynamic-slice.3, ...), channel_id=1, replica_groups=mesh['expert'=8,'shard'=4] {'expert'}, use_global_device_ids=true, to_apply=%region_24.25 | all-reduce | flops 4608 | bytes 18432 | tf_op jit(solution)/shard_map/psum | solution.py:315
  1572.8 46.4 %all-reduce.7.cloned.1.call-done = (bf16[256,1024]{1,0:T(8,128)(2,1)}, bf16[256,512]{1,0:T(8,128)(2,1)}, bf16[256,512]{1,0:T(8,128)(2,1)}, bf16[256,1024]{1,0:T(8,128)(2,1)}) async-done(((bf16[256,1024]{1,0:T(8,128)(2,1)}, bf16[256,512]{1,0:T(8,128)(2,1)}, bf16[256,512]{1,0:T(8,128)(2,1)}, bf16[256,1024]{1,0:T(8,128)(2,1)}), (bf16[256,1024]{1,0:T(8,128)(2,1)}, bf16[256,512]{1,0:T(8,128)(2,1)}, ...) | async-done | bytes 1572880 | tf_op jit(solution)/shard_map/psum | solution.py:316
  (285 shorter events, 303.3 us)
Async XLA Ops:
  7.2 32.0 %all-gather.12.cloned.1.call-start = ((), (), s32[]{:S(2)}) async-start(), calls=%async_computation.13 | async-start | bytes 1310720 | tf_op jit(solution)/shard_map/all_gather | solution.py:83
  8.0 59.8 %all-gather.10.cloned.1.call-start = ((), (), s32[]{:S(2)}) async-start(), calls=%async_computation.12 | async-start | bytes 1310720 | tf_op jit(solution)/shard_map/all_gather | solution.py:84
  8.7 96.3 %all-gather.14.cloned.1.call-start = ((), (), s32[]{:S(2)}) async-start(), calls=%async_computation.14 | async-start | bytes 2621440 | tf_op jit(solution)/shard_map/all_gather | solution.py:82
  9.4 132.6 %all-gather.16.cloned.1.call-start = ((), (), s32[]{:S(2)}) async-start(), calls=%async_computation.15 | async-start | bytes 2621440 | tf_op jit(solution)/shard_map/all_gather | solution.py:85
  37.6 70.4 %copy-start.24 = (f32[512,32]{0,1:T(8,128)}, f32[512,32]{0,1:T(8,128)S(1)}, u32[]{:S(2)}) copy-start(f32[512,32]{0,1:T(8,128)S(1)} %get-tuple-element.44) | copy-start | bytes 196612
  37.9 185.1 %copy-start.46 = (s32[4096,1]{0,1:T(1,128)}, s32[4096,1]{0,1:T(1,128)S(1)}, u32[]{:S(2)}) copy-start(s32[4096,1]{0,1:T(1,128)S(1)} %compare_select_fusion) | copy-start | bytes 49156
  172.3 279.3 %all-to-all-start = ((bf16[8,2,384,1024]{3,2,1,0:T(8,128)(2,1)}), bf16[8,2,384,1024]{3,2,1,0:T(8,128)(2,1)}, u32[]{:S(2)}, u32[]{:S(2)}) async-start(bf16[8,2,384,1024]{3,2,1,0:T(8,128)(2,1)} %bitcast.217), calls=%async_computation | async-start | bytes 25165824 | tf_op jit(solution)/shard_map/all_to_all | solution.py:163
  451.6 279.1 %all-to-all-start.2 = ((bf16[8,2,384,1024]{3,2,1,0:T(8,128)(2,1)}), bf16[8,2,384,1024]{3,2,1,0:T(8,128)(2,1)}, u32[]{:S(2)}, u32[]{:S(2)}) async-start(bf16[8,2,384,1024]{3,2,1,0:T(8,128)(2,1)} %bitcast.216), calls=%async_computation.2 | async-start | bytes 25165824 | tf_op jit(solution)/shard_map/all_to_all | solution.py:187
  457.0 38.1 %all-gather.20.cloned.1.call-start = ((), (), s32[]{:S(2)}) async-start(), calls=%async_computation.17 | async-start | bytes 2621440 | tf_op jit(solution)/shard_map/all_gather | solution.py:91
  457.6 74.6 %all-gather.18.cloned.1.call-start = ((), (), s32[]{:S(2)}) async-start(), calls=%async_computation.16 | async-start | bytes 2621440 | tf_op jit(solution)/shard_map/all_gather | solution.py:90
  458.1 111.2 %all-gather.22.cloned.1.call-start = ((), (), s32[]{:S(2)}) async-start(), calls=%async_computation.18 | async-start | bytes 2621440 | tf_op jit(solution)/shard_map/all_gather | solution.py:92
  569.3 186.6 %copy-start.65 = (bf16[2,512,1024]{2,1,0:T(8,128)(2,1)S(1)}, bf16[2,512,1024]{2,1,0:T(8,128)(2,1)}, u32[]{:S(2)}) copy-start(bf16[2,512,1024]{2,1,0:T(8,128)(2,1)} %all-gather.22.cloned.1.call-done) | copy-start | bytes 6291460
  771.2 279.1 %all-to-all-start.1 = ((bf16[8,2,384,1024]{3,2,1,0:T(8,128)(2,1)}), bf16[8,2,384,1024]{3,2,1,0:T(8,128)(2,1)}, u32[]{:S(2)}, u32[]{:S(2)}) async-start(bf16[8,2,384,1024]{3,2,1,0:T(8,128)(2,1)} %copy.151), calls=%async_computation.1 | async-start | bytes 25165824 | tf_op jit(solution)/shard_map/all_to_all | solution.py:170
  1050.3 279.1 %all-to-all-start.3 = ((bf16[8,2,384,1024]{3,2,1,0:T(8,128)(2,1)}), bf16[8,2,384,1024]{3,2,1,0:T(8,128)(2,1)}, u32[]{:S(2)}, u32[]{:S(2)}) async-start(bf16[8,2,384,1024]{3,2,1,0:T(8,128)(2,1)} %copy.156), calls=%async_computation.3 | async-start | bytes 25165824 | tf_op jit(solution)/shard_map/all_to_all | solution.py:211
  1055.7 374.3 %reduce-scatter.23.cloned.1.call-start = ((), (), s32[]{:S(2)}) async-start(), calls=%async_computation.26 | async-start | bytes 2621440 | tf_op jit(solution)/shard_map/reduce_scatter | solution.py:219
  1069.6 362.7 %reduce-scatter.21.cloned.1.call-start = ((), (), s32[]{:S(2)}) async-start(), calls=%async_computation.25 | async-start | bytes 2621440 | tf_op jit(solution)/shard_map/reduce_scatter | solution.py:216
  1082.2 352.2 %reduce-scatter.19.cloned.1.call-start = ((), (), s32[]{:S(2)}) async-start(), calls=%async_computation.24 | async-start | bytes 2621440 | tf_op jit(solution)/shard_map/reduce_scatter | solution.py:213
  1095.9 348.7 %reduce-scatter.13.cloned.1.call-start = ((), (), s32[]{:S(2)}) async-start(), calls=%async_computation.21 | async-start | bytes 1310720 | tf_op jit(solution)/shard_map/reduce_scatter | solution.py:301
  1395.2 56.9 %reduce-scatter.11.cloned.1.call-start = ((), (), s32[]{:S(2)}) async-start(), calls=%async_computation.20 | async-start | bytes 1310720 | tf_op jit(solution)/shard_map/reduce_scatter | solution.py:298
  1413.5 77.0 %reduce-scatter.15.cloned.1.call-start = ((), (), s32[]{:S(2)}) async-start(), calls=%async_computation.22 | async-start | bytes 2621440 | tf_op jit(solution)/shard_map/reduce_scatter | solution.py:304
  1417.8 110.7 %reduce-scatter.9.cloned.1.call-start = ((), (), s32[]{:S(2)}) async-start(), calls=%async_computation.19 | async-start | bytes 2621440 | tf_op jit(solution)/shard_map/reduce_scatter | solution.py:295
  1428.1 126.3 %reduce-scatter.17.cloned.1.call-start = ((), (), s32[]{:S(2)}) async-start(), calls=%async_computation.23 | async-start | bytes 40960 | tf_op jit(solution)/shard_map/reduce_scatter | solution.py:310
  1437.5 181.7 %all-reduce.7.cloned.1.call-start = ((), (), s32[]{:S(2)}) async-start(), calls=%async_computation.27 | async-start | bytes 3145728 | tf_op jit(solution)/shard_map/psum | solution.py:316
  1444.5 84.0 %copy-start.32 = (bf16[1024,512]{1,0:T(8,128)(2,1)S(1)}, bf16[1024,512]{1,0:T(8,128)(2,1)}, u32[]{:S(2)}) copy-start(bf16[1024,512]{1,0:T(8,128)(2,1)} %all-gather.10.cloned.1.call-done) | copy-start | bytes 3145732
  (65 other events, 934.6 us)
Sparse Core Ops, SparseCore 0:
  9.9 29.3 all-gather.11
  41.1 26.6 all-gather.9
  69.7 35.2 all-gather.13
  106.7 35.2 all-gather.15
  459.3 35.6 all-gather.19
  496.8 35.2 all-gather.17
  534.0 35.2 all-gather.21
  1069.7 35.5 reduce-scatter.22
  1108.5 35.1 reduce-scatter.20
  1146.6 35.1 reduce-scatter.18
  1395.3 25.6 reduce-scatter.12
  1424.3 27.7 reduce-scatter.10
  1455.3 35.1 reduce-scatter.14
  1493.3 35.1 reduce-scatter.8
  1531.9 22.4 reduce-scatter.16
  1557.0 62.1 all-reduce.6
where the time goes:
time: 1640 us; the launch traced here: 1630 us
  waiting for transfers between devices  1080 us (66%)
  matrix products  206 us (13%)
  local copies, waits for them, and re-layouts  144 us (9%)
  other arithmetic  109 us (7%)
  blocking collectives  51.7 us (3%)
  starting transfers between devices  22.6 us (1%)
    all_to_all x1, waiting for transfers between devices, per_device(): lax.all_to_all(result, 'expert', split_axis=0, concat_axis=0, tiled=True)  232 us
    all_to_all x1, waiting for transfers between devices, per_device(): lax.all_to_all(outgoing, 'expert', split_axis=0, concat_axis=0, tiled=True)  201 us
    all_to_all x1, waiting for transfers between devices, per_device(): lax.all_to_all(row_grad, 'expert', split_axis=0, concat_axis=0, tiled=True)  196 us
    all_to_all x1, waiting for transfers between devices, per_device(): lax.all_to_all(grad_slots, 'expert', split_axis=0, concat_axis=0, tiled=T...  161 us
    psum x1, waiting for transfers between devices, per_device(): lax.psum(part_query.astype(jnp.bfloat16), 'expert').astype(jnp.float32)  46.4 us
    reduce_scatter x1, waiting for transfers between devices, per_device(): lax.psum_scatter(out_grad_w.astype(jnp.bfloat16), 'shard', scatter_dimens...  38.5 us
    reduce_scatter x1, waiting for transfers between devices, per_device(): lax.psum_scatter(query_grad_w.astype(jnp.bfloat16), 'shard', scatter_dime...  38 us
    all_gather x1, waiting for transfers between devices, per_device(): lax.all_gather(w_up, 'shard', axis=1, tiled=True)  36.2 us
  transfers between devices with their start and end apart: 20, of which 16 were waited for; matrix products, arithmetic and copies ran while one was open for 23% of the time, Pallas kernels for 0%

commit v1 on v0

v1 whole, which is shorter than its diff:
```python
import functools
import math

import jax
import jax.numpy as jnp
from jax import lax
from jax.experimental import pallas as pl
from jax.experimental.pallas import tpu as pltpu
from jax.sharding import PartitionSpec as P

QUERY_HEADS = 16
KEY_VALUE_HEADS = 8
HEAD_DIM = 64
LANES = 128
F32 = jnp.float32
BF16 = jnp.bfloat16


def normalize(values, gain_vector):
    return (
        values * lax.rsqrt(jnp.mean(values * values, axis=-1, keepdims=True) + 1e-06) * gain_vector
    )


def apply_rotary(values, cosine_table, sine_lookup):
    half_width = values.shape[-1] // 2
    first_half = values[..., :half_width]
    second_half = values[..., half_width:]
    return jnp.concatenate(
        [
            first_half * cosine_table - second_half * sine_lookup,
            second_half * cosine_table + first_half * sine_lookup,
        ],
        axis=-1,
    )


def place_tables(lengths_row, total_rows, head_width):
    doc_ends = jnp.cumsum(lengths_row)
    token_index = jnp.arange(total_rows, dtype=jnp.int32)
    past_end = token_index[:, None] >= doc_ends[None, :]
    document = jnp.sum(past_end.astype(jnp.int32), axis=1)
    doc_start = jnp.sum(jnp.where(past_end, lengths_row[None, :], 0), axis=1)
    position = (token_index - doc_start).astype(jnp.float32)
    half_width = head_width // 2
    inverse = 10000.0 ** (-(jnp.arange(half_width, dtype=jnp.float32) * 2.0 / head_width))
    angles = position[:, None] * inverse[None, :]
    allowed = (document[:, None] == document[None, :]) & (
        token_index[None, :] <= token_index[:, None]
    )
    return (jnp.cos(angles)[:, None, :], jnp.sin(angles)[:, None, :], allowed)


def matrix_product(left_side, right_side):
    return jnp.dot(left_side, right_side, preferred_element_type=jnp.float32)


def product_tn(left_side, right_side):
    return lax.dot_general(
        left_side, right_side, (((0,), (0,)), ((), ())), preferred_element_type=jnp.float32
    )


def product_transposed_right(left_side, right_side):
    return lax.dot_general(
        left_side, right_side, (((1,), (1,)), ((), ())), preferred_element_type=jnp.float32
    )


def pick(blocks, index):
    return lax.dynamic_index_in_dim(blocks, index, 0, keepdims=False)


def gather_pieces(piece):
    count = lax.axis_size("shard")
    if count == 4:
        me = lax.axis_index("shard")
        pieces = [(piece, me)]
        for flip in (1, 2, 3):
            got = lax.ppermute(piece, "shard", [(i, i ^ flip) for i in range(4)])
            pieces.append((got, me ^ flip))
        return pieces
    every = lax.all_gather(piece, "shard", axis=0)
    return [(every[i], jnp.int32(i)) for i in range(count)]


def swap_cores(value):
    size = lax.axis_size("expert")
    return lax.ppermute(value, "expert", [(i, i ^ 1) for i in range(size)])


def gather_rows(rows):
    core = lax.axis_index("expert") % 2
    half = rows.shape[0] // 2
    mine = lax.dynamic_slice_in_dim(rows, core * half, half, 0)
    pieces = gather_pieces(mine)
    count = len(pieces)
    kept = jnp.stack([piece for piece, _ in pieces])
    other = swap_cores(kept)
    low = jnp.where(core == 0, kept, other)
    high = jnp.where(core == 0, other, kept)
    both = jnp.stack([low, high], axis=1).reshape(count, rows.shape[0], rows.shape[1])
    me = lax.axis_index("shard")
    if count == 4:
        both = jnp.concatenate([pick(both, me ^ i) for i in range(4)], axis=0)
    return both.reshape(count * rows.shape[0], rows.shape[1])


def scatter_sum(blocks):
    count = lax.axis_size("shard")
    if count != 4:
        return lax.psum_scatter(blocks.astype(BF16), "shard", scatter_dimension=0).astype(F32)
    me = lax.axis_index("shard")
    total = pick(blocks, me).astype(F32)
    for flip in (1, 2, 3):
        sent = pick(blocks, me ^ flip).astype(BF16)
        got = lax.ppermute(sent, "shard", [(i, i ^ flip) for i in range(4)])
        total = total + got.astype(F32)
    return total


def sum_everywhere(grad):
    count = lax.axis_size("shard")
    size = lax.axis_size("expert")
    layers = size // 2
    place = lax.axis_index("expert")
    core, layer = place % 2, place // 2
    width = grad.shape[1]
    half = grad.shape[0] // count // 2
    blocks = grad.reshape(count, 2, half, width)
    mine = lax.dynamic_index_in_dim(blocks, core, 1, keepdims=False)
    away = lax.dynamic_index_in_dim(blocks, 1 - core, 1, keepdims=False)
    paired = mine + swap_cores(away.astype(BF16)).astype(F32)
    local = scatter_sum(paired).reshape(layers, half // layers, width)
    total = pick(local, layer)
    for step in range(1, layers):
        perm = [(i, (i + 2 * step) % size) for i in range(size)]
        sent = pick(local, (layer + step) % layers).astype(BF16)
        total = total + lax.ppermute(sent, "expert", perm).astype(F32)
    total = total.astype(BF16)
    parts = jnp.zeros((layers, half // layers, width), BF16)
    parts = lax.dynamic_update_index_in_dim(parts, total, layer, 0)
    for step in range(1, layers):
        perm = [(i, (i + 2 * step) % size) for i in range(size)]
        got = lax.ppermute(total, "expert", perm)
        parts = lax.dynamic_update_index_in_dim(parts, got, (layer - step) % layers, 0)
    mine = parts.reshape(half, width)
    other = swap_cores(mine)
    low = jnp.where(core == 0, mine, other)
    high = jnp.where(core == 0, other, mine)
    return jnp.concatenate([low, high], axis=0).astype(F32)


def expert_kernel(count, experts, place_ref, x_ref, dy_ref, mask_ref, router_ref, *refs):
    pieces = refs[:count]
    out_ref, row_ref, act_ref, gate_ref, up_ref, score_ref, gu, down, sem = refs[count:]
    local, rows, width = pieces[0].shape
    third = rows // 3
    hidden = width // 2

    @pl.when(pl.program_id(0) == 0)
    def _():
        copies = []
        for i in range(count):
            at = place_ref[i]
            copies.append(
                pltpu.make_async_copy(
                    pieces[i].at[:, pl.ds(0, 2 * third), :],
                    gu.at[:, pl.ds(pl.multiple_of(at * (2 * third), 16), 2 * third), :],
                    sem.at[2 * i],
                )
            )
            copies.append(
                pltpu.make_async_copy(
                    pieces[i].at[:, pl.ds(2 * third, third), :],
                    down.at[:, pl.ds(pl.multiple_of(at * third, 16), third), :],
                    sem.at[2 * i + 1],
                )
            )
        for copy in copies:
            copy.start()
        for copy in copies:
            copy.wait()

    x = x_ref[...]
    dy = dy_ref[...]
    lane = lax.broadcasted_iota(jnp.int32, (x.shape[0], LANES), 1)
    logits = jnp.where(
        mask_ref[...] > 0, jnp.dot(x, router_ref[...], preferred_element_type=F32), -1e30
    )
    powers = jnp.exp(logits - jnp.max(logits, axis=1, keepdims=True))
    chances = powers / jnp.sum(powers, axis=1, keepdims=True)
    out = None
    row = None
    scores = jnp.zeros((x.shape[0], LANES), F32)
    for j in range(local):
        own = place_ref[count] * local + j
        gate = jnp.sum(jnp.where(lane == own, chances, 0.0), axis=1, keepdims=True)
        left = gu[j, :, :hidden]
        right = gu[j, :, hidden:]
        back = down[j]
        gate_val = jnp.dot(x, left, preferred_element_type=F32)
        up_val = jnp.dot(x, right, preferred_element_type=F32)
        inner_grad = product_transposed_right(dy, back)
        sigmoid = 1.0 / (1.0 + jnp.exp(-gate_val))
        swish = gate_val * sigmoid
        inner = (swish * up_val).astype(BF16).astype(F32)
        score = jnp.sum(inner * inner_grad, axis=1, keepdims=True)
        scores = jnp.where(lane == j, score, scores)
        act = (gate * inner).astype(BF16)
        scaled = gate * inner_grad
        gate_back = (scaled * up_val * sigmoid * (1.0 + gate_val * (1.0 - sigmoid))).astype(BF16)
        up_back = (scaled * swish).astype(BF16)
        act_ref[:, j * hidden : (j + 1) * hidden] = act
        gate_ref[:, j * hidden : (j + 1) * hidden] = gate_back
        up_ref[:, j * hidden : (j + 1) * hidden] = up_back
        part = jnp.dot(act, back, preferred_element_type=F32)
        out = part if out is None else out + part
        part = product_transposed_right(gate_back, left) + product_transposed_right(up_back, right)
        row = part if row is None else row + part
    out_ref[...] = out.astype(BF16)
    row_ref[...] = row.astype(BF16)
    score_ref[...] = scores


def run_experts(every_x, every_dy, mask, router, pieces, tile):
    count = len(pieces)
    total, width = every_x.shape
    local, rows, _ = pieces[0][0].shape
    third = rows // 3
    hidden = width // 2
    place = jnp.stack([index for _, index in pieces] + [lax.axis_index("expert")]).astype(jnp.int32)
    block = pl.BlockSpec((tile, width), lambda i, p: (i, 0))
    thin = pl.BlockSpec((tile, LANES), lambda i, p: (i, 0))
    steps = every_dy.shape[1] // tile
    return pl.pallas_call(
        functools.partial(expert_kernel, count, router.shape[1]),
        grid_spec=pltpu.PrefetchScalarGridSpec(
            num_scalar_prefetch=1,
            grid=(total // tile,),
            in_specs=[
                block,
                pl.BlockSpec((None, tile, width), lambda i, p: (i // steps, i % steps, 0)),
                thin,
                pl.BlockSpec((width, LANES), lambda i, p: (0, 0)),
            ]
            + [pl.BlockSpec(memory_space=pl.ANY)] * count,
            out_specs=[block, block, block, block, block, thin],
            scratch_shapes=[
                pltpu.VMEM((local, 2 * third * count, width), BF16),
                pltpu.VMEM((local, third * count, width), BF16),
                pltpu.SemaphoreType.DMA((2 * count,)),
            ],
        ),
        out_shape=[jax.ShapeDtypeStruct((total, width), BF16)] * 5
        + [jax.ShapeDtypeStruct((total, LANES), F32)],
        compiler_params=pltpu.CompilerParams(vmem_limit_bytes=58 * 1024 * 1024),
        cost_estimate=pl.CostEstimate(
            flops=2 * total * width * width * 6, bytes_accessed=total * width * 14, transcendentals=0
        ),
        name="experts",
    )(place, every_x, every_dy, mask, router, *[piece for piece, _ in pieces])


def per_device(
    tokens,
    gain_attn,
    w_query,
    key_weight,
    value_weight,
    w_out,
    gain_mix,
    router,
    w_gate,
    w_up,
    w_down,
    routes,
    lengths,
    cotangent,
):
    total_rows, model_width = tokens.shape
    query_group_width = QUERY_HEADS // KEY_VALUE_HEADS
    experts = router.shape[1]
    local_experts, _, hidden = w_gate.shape
    peers = lax.axis_size("expert")
    count = lax.axis_size("shard")
    part_rows = w_query.shape[0]
    kv_width = key_weight.shape[1]
    score_scale = 1.0 / math.sqrt(HEAD_DIM)

    small = jnp.concatenate(
        [
            router,
            gain_attn[:, None],
            gain_mix[:, None],
            jnp.zeros((part_rows, LANES - experts - 2), BF16),
        ],
        axis=1,
    )
    first_weights = gather_rows(
        jnp.concatenate([w_query, key_weight, value_weight, small], axis=1)
    )
    q_end = w_query.shape[1]
    query_w = first_weights[:, :q_end]
    key_matrix = first_weights[:, q_end : q_end + kv_width]
    value_matrix = first_weights[:, q_end + kv_width : q_end + 2 * kv_width]
    small_all = first_weights[:, q_end + 2 * kv_width :]
    gain_first = small_all[:, experts].astype(F32)
    gain_second = small_all[:, experts + 1].astype(F32)
    router_lanes = jnp.where(jnp.arange(LANES)[None, :] < experts, small_all, jnp.zeros((), BF16))
    router_w = small_all[:, :experts]
    output_matrix = gather_rows(w_out)
    packed = jnp.concatenate([jnp.concatenate([w_gate, w_up], axis=2), w_down], axis=1)
    pieces = gather_pieces(packed)

    expert_ids = jnp.arange(experts, dtype=jnp.int32)
    chosen = jnp.any(routes[:, :, None] == expert_ids[None, None, :], axis=1)
    mask_rows = total_rows * experts // model_width
    mask_space = -(-mask_rows // 16) * 16
    every_dy = lax.all_gather(
        jnp.concatenate(
            [
                cotangent,
                jnp.pad(
                    chosen.astype(BF16).reshape(mask_rows, model_width),
                    ((0, mask_space - mask_rows), (0, 0)),
                ),
            ],
            axis=0,
        ),
        "expert",
        axis=0,
    )
    every_mask = jnp.pad(
        every_dy[:, total_rows : total_rows + mask_rows].reshape(peers * total_rows, experts),
        ((0, 0), (0, LANES - experts)),
    )

    inputs = tokens.astype(jnp.float32)
    normalized_input = normalize(inputs, gain_first).astype(jnp.bfloat16)
    cosine_table, sine_lookup, allowed = place_tables(lengths[0], total_rows, HEAD_DIM)
    query_raw = matrix_product(normalized_input, query_w).reshape(total_rows, QUERY_HEADS, HEAD_DIM)
    unrotated_keys = matrix_product(normalized_input, key_matrix).reshape(
        total_rows, KEY_VALUE_HEADS, HEAD_DIM
    )
    query_rows = (
        apply_rotary(query_raw, cosine_table, sine_lookup)
        .astype(jnp.bfloat16)
        .reshape(total_rows, KEY_VALUE_HEADS, query_group_width, HEAD_DIM)
    )
    key_matrix_rows = apply_rotary(unrotated_keys, cosine_table, sine_lookup).astype(jnp.bfloat16)
    value_matrix_rows = (
        matrix_product(normalized_input, value_matrix)
        .astype(jnp.bfloat16)
        .reshape(total_rows, KEY_VALUE_HEADS, HEAD_DIM)
    )

    def score_table():
        raw_scores = (
            jnp.einsum(
                "vuol,mul->uovm", query_rows, key_matrix_rows, preferred_element_type=jnp.float32
            )
            * score_scale
        )
        return jnp.where(allowed[None, None], raw_scores, -1e30)

    scores = score_table()
    top_score = jnp.max(scores, axis=-1, keepdims=True)
    weights = jnp.exp(scores - top_score)
    sum_weights = jnp.sum(weights, axis=-1, keepdims=True)
    probability = weights / sum_weights
    log_total = top_score + jnp.log(sum_weights)
    lower_probabilities = probability.astype(jnp.bfloat16)
    attended = (
        jnp.einsum(
            "yjvu,uyw->vyjw",
            lower_probabilities,
            value_matrix_rows,
            preferred_element_type=jnp.float32,
        )
        .astype(jnp.bfloat16)
        .reshape(total_rows, QUERY_HEADS * HEAD_DIM)
    )
    hidden_state = inputs + matrix_product(attended, output_matrix)
    mixed_in = normalize(hidden_state, gain_second).astype(jnp.bfloat16)
    logits = matrix_product(mixed_in, router_w)
    gates = jax.nn.softmax(jnp.where(chosen, logits, -1e30), axis=-1)

    every_x = lax.all_gather(mixed_in, "expert", axis=0, tiled=True)
    out_part, row_part, act, gate_back, up_back, scores_part = run_experts(
        every_x, every_dy, every_mask, router_lanes, pieces, 512 if total_rows % 512 == 0 else 128
    )
    out_sum = lax.psum_scatter(out_part, "expert", scatter_dimension=0, tiled=True)
    row_sum = lax.psum_scatter(row_part, "expert", scatter_dimension=0, tiled=True)
    sent_scores = scores_part[:, :local_experts].reshape(peers, -1, LANES)
    gate_grad = lax.all_to_all(sent_scores, "expert", split_axis=0, concat_axis=0, tiled=True)
    gate_grad = (
        gate_grad.reshape(peers, total_rows, local_experts)
        .transpose(1, 0, 2)
        .reshape(total_rows, experts)
    )
    output = hidden_state + out_sum.astype(F32)
    upstream = cotangent.astype(jnp.float32)

    flat_dy = every_dy[:, :total_rows].reshape(peers * total_rows, model_width)
    down_grad = product_tn(act, flat_dy).astype(BF16)
    gate_grad_w = product_tn(every_x, gate_back).astype(BF16)
    up_grad_w = product_tn(every_x, up_back).astype(BF16)
    gu_grad = jnp.stack(
        [gate_grad_w.reshape(model_width, local_experts, hidden),
         up_grad_w.reshape(model_width, local_experts, hidden)], axis=2
    )
    gu_blocks = gu_grad.reshape(count, part_rows, local_experts, 2 * hidden).transpose(0, 2, 1, 3)
    down_blocks = down_grad.reshape(
        local_experts, count, hidden // count, model_width
    ).transpose(1, 0, 2, 3)
    expert_sum = scatter_sum(jnp.concatenate([gu_blocks, down_blocks], axis=2))
    expert_gate_sum = expert_sum[:, :part_rows, :hidden]
    expert_up_sum = expert_sum[:, :part_rows, hidden:]
    expert_down_sum = expert_sum[:, part_rows:, :]

    logit_grad = (
        gates * (gate_grad - jnp.sum(gates * gate_grad, axis=1, keepdims=True))
    ).astype(jnp.bfloat16)
    router_grad = product_tn(mixed_in, logit_grad)
    mixed_grad = product_transposed_right(logit_grad, router_w) + row_sum.astype(F32)
    _, second_back = jax.vjp(normalize, hidden_state, gain_second)
    state_part, gain_two_grad = second_back(mixed_grad)
    state_grad = upstream + state_part
    branch_gradient = state_grad.astype(jnp.bfloat16)
    out_grad_w = product_tn(attended, branch_gradient)
    early = sum_everywhere(
        jnp.concatenate(
            [
                out_grad_w,
                router_grad,
                gain_two_grad[:, None],
                jnp.zeros((model_width, LANES - experts - 1), F32),
            ],
            axis=1,
        )
    )
    attended_gradient = (
        product_transposed_right(branch_gradient, output_matrix)
        .astype(jnp.bfloat16)
        .reshape(total_rows, KEY_VALUE_HEADS, query_group_width, HEAD_DIM)
    )
    probability = jnp.exp(score_table() - log_total)
    prob_grad = jnp.einsum(
        "vuol,mul->uovm", attended_gradient, value_matrix_rows, preferred_element_type=jnp.float32
    )
    score_gradient = (
        probability * (prob_grad - jnp.sum(probability * prob_grad, axis=-1, keepdims=True))
    ).astype(jnp.bfloat16)
    query_grad = (
        jnp.einsum(
            "yjvu,uyw->vyjw", score_gradient, key_matrix_rows, preferred_element_type=jnp.float32
        )
        * score_scale
    )
    key_gradient = (
        jnp.einsum("cuyf,ycul->fcl", score_gradient, query_rows, preferred_element_type=jnp.float32)
        * score_scale
    )
    value_gradient = jnp.einsum(
        "cuyf,ycul->fcl", lower_probabilities, attended_gradient, preferred_element_type=jnp.float32
    )
    query_back = (
        apply_rotary(
            query_grad.reshape(total_rows, QUERY_HEADS, HEAD_DIM), cosine_table, -sine_lookup
        )
        .astype(jnp.bfloat16)
        .reshape(total_rows, QUERY_HEADS * HEAD_DIM)
    )
    key_back = (
        apply_rotary(key_gradient, cosine_table, -sine_lookup)
        .astype(jnp.bfloat16)
        .reshape(total_rows, KEY_VALUE_HEADS * HEAD_DIM)
    )
    value_backward = value_gradient.astype(jnp.bfloat16).reshape(
        total_rows, KEY_VALUE_HEADS * HEAD_DIM
    )
    all_back = jnp.concatenate([query_back, key_back, value_backward], axis=1)
    first_grad_w = product_tn(normalized_input, all_back)
    normed_grad = product_transposed_right(all_back, first_weights[:, : q_end + 2 * kv_width])
    _, first_back = jax.vjp(normalize, inputs, gain_first)
    input_part, gain_one_grad = first_back(normed_grad)
    input_grad = state_grad + input_part
    late = sum_everywhere(
        jnp.concatenate(
            [first_grad_w, gain_one_grad[:, None], jnp.zeros((model_width, LANES - 1), F32)], axis=1
        )
    )
    return (
        output.astype(jnp.bfloat16),
        input_grad.astype(jnp.bfloat16),
        late[:, q_end + 2 * kv_width],
        late[:, :q_end],
        late[:, q_end : q_end + kv_width],
        late[:, q_end + kv_width : q_end + 2 * kv_width],
        early[:, :model_width],
        early[:, model_width + experts],
        early[:, model_width : model_width + experts],
        expert_gate_sum,
        expert_up_sum,
        expert_down_sum,
    )


def solution(mesh):
    in_specs = (
        P(("expert", "shard"), None),
        P("shard"),
        P("shard", None),
        P("shard", None),
        P("shard", None),
        P("shard", None),
        P("shard"),
        P("shard", None),
        P("expert", "shard", None),
        P("expert", "shard", None),
        P("expert", "shard", None),
        P(("expert", "shard"), None),
        P(("expert", "shard"), None),
        P(("expert", "shard"), None),
    )
    out_specs = (
        P(("expert", "shard"), None),
        P(("expert", "shard"), None),
        P("shard"),
        P("shard", None),
        P("shard", None),
        P("shard", None),
        P("shard", None),
        P("shard"),
        P("shard", None),
        P("expert", "shard", None),
        P("expert", "shard", None),
        P("expert", "shard", None),
    )
    return jax.shard_map(
        per_device, mesh=mesh, in_specs=in_specs, out_specs=out_specs, check_vma=False
    )
```

time: 1640 us -> 661 us (0.40)
  waiting for transfers between devices: 1080 us -> 217 us
  matrix products: 206 us -> 113 us
  Pallas kernels: 0 us -> 83.4 us
  blocking collectives: 51.7 us -> 0 us
  local copies, waits for them, and re-layouts: 144 us -> 94.3 us
  other arithmetic: 109 us -> 82.8 us
  starting transfers between devices: 22.6 us -> 43.8 us
    all_to_all x4 -> x1, waiting for transfers between devices: 790 us -> 6.12 us  [per_device(): lax.all_to_all(sent_scores, 'expert', split_axis=0, concat_axis=0, tiled=...]
    ppermute x0 -> x36, waiting for transfers between devices: none -> 200 us  [the longest x9 96.3 us: gather_pieces(): got = lax.ppermute(piece, 'shard', [(i, i ^ flip) for i in range(4)])]
    all_gather x7 -> x2, waiting for transfers between devices: 149 us -> 8.9 us  [the longest x1 8.89 us: per_device(): every_x = lax.all_gather(mixed_in, 'expert', axis=0, tiled=True)]
    dot_general x9 -> x0, matrix products: 135 us -> none  [the longest x1 25.1 us: per_device(): jnp.einsum('sjcd,jfd->sjcf', arrived_grad, down_w, preferred_element_type...]
    reduce_scatter x8 -> x2, waiting for transfers between devices: 92.2 us -> 0.71 us  [the longest x1 0.71 us: per_device(): lax.psum_scatter(out_part, 'expert', scatter_dimension=0, tiled=True)]
    gather x7 -> x0, local copies, waits for them, and re-layouts: 88 us -> none  [the longest x5 33.6 us: per_device(): jnp.take_along_axis(logits, routes, axis=1)]
    pallas_call x0 -> x1, Pallas kernels: none -> 83.4 us  [run_experts(): pl.pallas_call(functools.partial(expert_kernel, count, router.shape[1]),...]
    psum x1 -> x0, waiting for transfers between devices: 46.4 us -> none  [per_device(): lax.psum(part_query.astype(jnp.bfloat16), 'expert').astype(jnp.float32)]
  transfers between devices with their start and end apart: 20 -> 41, of which waited for: 16 -> 25; matrix products, arithmetic and copies ran while one was open for 23% -> 32% of each run, Pallas kernels for 0% -> 0%
where the time goes in v1:
time: 661 us; the launch traced here: 650 us
  waiting for transfers between devices  217 us (33%)
  matrix products  113 us (17%)
  local copies, waits for them, and re-layouts  94.3 us (14%)
  Pallas kernels  83.4 us (13%)
  other arithmetic  82.8 us (13%)
  starting transfers between devices  43.8 us (7%)
  between operations  15.3 us (2%)
    ppermute x9, waiting for transfers between devices, gather_pieces(): got = lax.ppermute(piece, 'shard', [(i, i ^ flip) for i in range(4)])  96.3 us
    ppermute x9, waiting for transfers between devices, scatter_sum(): got = lax.ppermute(sent, 'shard', [(i, i ^ flip) for i in range(4)])  83.5 us
    pallas_call x1, Pallas kernels, run_experts(): pl.pallas_call(functools.partial(expert_kernel, count, router.shape[1]),...  83.4 us
    dot_general x6, matrix products, product_tn(): lax.dot_general(left_side, right_side, (((0,), (0,)), ((), ())), preferre...  55.4 us
    another operation x2, local copies, waits for them, and re-layouts, per_device(): jnp.stack([gate_grad_w.reshape(model_width, local_experts, hidden), up_gr...  21.6 us
    dot_general x1, matrix products, per_device(): jnp.einsum('vuol,mul->uovm', attended_gradient, value_matrix_rows, prefer...  15.3 us
    unnamed x156, local copies, waits for them, and re-layouts  13.9 us
  transfers between devices with their start and end apart: 41, of which 25 were waited for; matrix products, arithmetic and copies ran while one was open for 32% of the time, Pallas kernels for 0%

profile of v1, /device:TPU:0, one launch (start us, length us, event | category | flops | bytes accessed | tf_op | source)
XLA Modules:
  0.0 649.8 jit_solution(7039447781113165612)
XLA Ops:
  17.4 11.9 %collective-permute-done = bf16[128,2176]{1,0:T(8,128)(2,1)S(1)} collective-permute-done((bf16[128,2176]{1,0:T(8,128)(2,1)S(1)}, bf16[128,2176]{1,0:T(8,128)(2,1)S(1)}, u32[]{:S(2)}, u32[]{:S(2)}) %collective-permute-start) | collective-permute-done | bytes 557088 | tf_op jit(solution)/shard_map/ppermute | solution.py:80
  29.3 12.6 %collective-permute-done.1 = bf16[128,2176]{1,0:T(8,128)(2,1)S(1)} collective-permute-done((bf16[128,2176]{1,0:T(8,128)(2,1)S(1)}, bf16[128,2176]{1,0:T(8,128)(2,1)S(1)}, u32[]{:S(2)}, u32[]{:S(2)}) %collective-permute-start.1) | collective-permute-done | bytes 557088 | tf_op jit(solution)/shard_map/ppermute | solution.py:80
  80.7 7.7 %fusion.83 = (f32[8,2,512]{2,1,0:T(2,128)S(1)}, f32[8,2,512,512]{2,3,1,0:T(8,128)}) fusion(bf16[512,8,2,32]{0,3,2,1:T(8,128)(2,1)S(1)} %bitcast.288, bf16[512,8,2,32]{0,3,2,1:T(8,128)(2,1)S(1)} %bitcast.286, bf16[512,8,32]{0,2,1:T(8,128)(2,1)S(1)} %get-tuple-element.116, bf16[512,8,32]{0,2,1:T(8,128)(2,1)S(1)} %get-tuple-element.115, ...), kind=kOutput, calls=%fused_computation.213 | convolution fusion | flops 552591360 | bytes 18644992 | tf_op jit(solution)/shard_map/vuol,mul->uovm/dot_general | solution.py:360
  88.4 8.3 %fusion.3 = f32[8,2,512]{2,1,0:T(2,128)S(1)} fusion(f32[8,2,512,512]{2,3,1,0:T(8,128)} %get-tuple-element.133, f32[8,2,512]{2,1,0:T(2,128)S(1)} %get-tuple-element.132), kind=kLoop, calls=%fused_computation.9 | loop fusion | flops 8380416 | bytes 16842752 | tf_op jit(solution)/shard_map/reduce_sum | solution.py:370
  125.0 27.6 %collective-permute-done.10.refs_3_ = bf16[2,384,1024]{2,1,0:T(8,128)(2,1)} collective-permute-done((bf16[2,384,1024]{2,1,0:T(8,128)(2,1)}, bf16[2,384,1024]{2,1,0:T(8,128)(2,1)}, u32[]{:S(2)}, u32[]{:S(2)}) %collective-permute-start.10) | collective-permute-done | bytes 1572896 | tf_op jit(solution)/shard_map/ppermute | solution.py:80
  152.6 32.3 %collective-permute-done.8.refs_1_ = bf16[2,384,1024]{2,1,0:T(8,128)(2,1)} collective-permute-done((bf16[2,384,1024]{2,1,0:T(8,128)(2,1)}, bf16[2,384,1024]{2,1,0:T(8,128)(2,1)}, u32[]{:S(2)}, u32[]{:S(2)}) %collective-permute-start.8) | collective-permute-done | bytes 1572896 | tf_op jit(solution)/shard_map/ppermute | solution.py:80
  185.4 8.9 %all-gather.4.cloned.1.call-done.x_ref = bf16[4096,1024]{1,0:T(8,128)(2,1)} async-done(((bf16[512,1024]{1,0:T(8,128)(2,1)}), bf16[4096,1024]{1,0:T(8,128)(2,1)}) %all-gather.4.cloned.1.call-update) | async-done | bytes 8388624 | tf_op jit(solution)/shard_map/all_gather | solution.py:389
  194.3 83.4 %experts.1 = (bf16[4096,1024]{1,0:T(8,128)(2,1)}, bf16[4096,1024]{1,0:T(8,128)(2,1)}, bf16[4096,1024]{1,0:T(8,128)(2,1)}, bf16[4096,1024]{1,0:T(8,128)(2,1)}, bf...) custom-call(s32[5]{0:T(128)} %stack.90.place_ref, bf16[4096,1024]{1,0:T(8,128)(2,1)} %all-gather.4.cloned.1.call-done.x_ref, ...), custom_call_target="tpu_custom_call" | custom-call | flops 51539607552 | bytes 58720256 | tf_op jit(solution)/shard_map/experts/pallas_call | solution.py:236
  278.3 7.7 %slice.134 = bf16[8,512,1024]{2,1,0:T(8,128)(2,1)} slice(bf16[8,528,1024]{2,1,0:T(8,128)(2,1)} %bitcast.264), slice={[0:8], [0:512], [0:1024]} | slice | bytes 16777216 | tf_op jit(solution)/shard_map/slice | solution.py:405
  286.0 15.0 %convolution_convert_fusion.2 = bf16[1024,1024]{0,1:T(8,128)(2,1)} fusion(bf16[4096,1024]{1,0:T(8,128)(2,1)} %all-gather.4.cloned.1.call-done.x_ref, bf16[4096,1024]{1,0:T(8,128)(2,1)} %get-tuple-element.21), kind=kOutput, calls=%fused_computation.63 | convolution fusion | flops 8590983168 | bytes 18874368 | tf_op jit(solution)/shard_map/dot_general | solution.py:59
  300.9 10.8 %copy.110 = bf16[1024,2,1,512]{3,2,0,1:T(2,128)(2,1)} copy(bf16[1024,2,1,512]{0,3,1,2:T(8,128)(2,1)} %bitcast.285) | data formatting | bytes 4194304 | tf_op jit(solution)/shard_map/stack;reshape | solution.py:409
  311.7 14.8 %convolution_convert_fusion.1 = bf16[1024,1024]{0,1:T(8,128)(2,1)} fusion(bf16[4096,1024]{1,0:T(8,128)(2,1)} %all-gather.4.cloned.1.call-done.x_ref, bf16[4096,1024]{1,0:T(8,128)(2,1)} %get-tuple-element.22), kind=kOutput, calls=%fused_computation.62 | convolution fusion | flops 8590983168 | bytes 18874368 | tf_op jit(solution)/shard_map/dot_general | solution.py:59
  326.6 10.8 %copy.111 = bf16[1024,2,1,512]{3,2,0,1:T(2,128)(2,1)} copy(bf16[1024,2,1,512]{0,3,1,2:T(8,128)(2,1)} %bitcast.284) | data formatting | bytes 4194304 | tf_op jit(solution)/shard_map/stack;reshape | solution.py:409
  337.4 11.0 %pad_maximum_fusion.2 = bf16[1024,2,2,512]{3,2,0,1:T(2,128)(2,1)} fusion(bf16[1024,2,1,512]{3,2,0,1:T(2,128)(2,1)} %copy.111, bf16[1024,2,1,512]{3,2,0,1:T(2,128)(2,1)} %copy.110), kind=kLoop, calls=%fused_computation.24 | loop fusion | flops 8388608 | bytes 8388608 | tf_op jit(solution)/shard_map/stack | solution.py:409
  348.3 7.7 %reshape.368 = bf16[4,256,2,1024]{3,1,0,2:T(8,128)(2,1)} reshape(bf16[1024,2,2,512]{3,2,0,1:T(2,128)(2,1)} %pad_maximum_fusion.2) | data formatting | bytes 8388608 | tf_op jit(solution)/shard_map/reshape | solution.py:413
  356.1 14.2 %convolution_convert_fusion = bf16[1024,1024]{1,0:T(8,128)(2,1)S(1)} fusion(bf16[4096,1024]{1,0:T(8,128)(2,1)} %get-tuple-element.23, bf16[4096,1024]{1,0:T(8,128)(2,1)} %bitcast.265), kind=kOutput, calls=%fused_computation.61 | convolution fusion | flops 8590983168 | bytes 18874368 | tf_op jit(solution)/shard_map/dot_general | solution.py:59
  392.6 18.3 %collective-permute-done.33 = bf16[2,384,1024]{2,1,0:T(8,128)(2,1)} collective-permute-done((bf16[2,384,1024]{2,1,0:T(8,128)(2,1)}, bf16[2,384,1024]{2,1,0:T(8,128)(2,1)}, u32[]{:S(2)}, u32[]{:S(2)}) %collective-permute-start.33) | collective-permute-done | bytes 1572896 | tf_op jit(solution)/shard_map/ppermute | solution.py:117
  410.8 34.0 %collective-permute-done.34 = bf16[2,384,1024]{2,1,0:T(8,128)(2,1)} collective-permute-done((bf16[2,384,1024]{2,1,0:T(8,128)(2,1)}, bf16[2,384,1024]{2,1,0:T(8,128)(2,1)}, u32[]{:S(2)}, u32[]{:S(2)}) %collective-permute-start.34) | collective-permute-done | bytes 1572896 | tf_op jit(solution)/shard_map/ppermute | solution.py:117
  466.3 15.3 %fusion = (f32[8,2,512]{2,1,0:T(2,128)S(1)}, f32[8,512,512,2]{2,1,3,0:T(8,128)}) fusion(f32[8,2,512,512]{2,3,1,0:T(8,128)} %get-tuple-element.133, f32[8,2,512]{2,1,0:T(2,128)S(1)} %bitcast.312, bf16[512,8,64,1]{0,2,3,1:T(8,128)(2,1)S(1)} %bitcast.283, bf16[512,8,2,64]{0,3,2,1:T(8,128)(2,1)S(1)} %bitcast.260), kind=kOutput, calls=%fused_computation.2 | convolution fusion | flops 549445632 | bytes 35192832 | tf_op jit(solution)/shard_map/vuol,mul->uovm/dot_general | solution.py:449
  483.1 11.3 %fusion.2 = bf16[8,2,512,512]{2,3,1,0:T(8,128)(2,1)} fusion(f32[8,512,512,2]{2,1,3,0:T(8,128)} %get-tuple-element.140, f32[8,2,512,512]{2,3,1,0:T(8,128)S(1)} %bitcast.254, f32[8,2,512]{2,1,0:T(2,128)S(1)} %get-tuple-element.139, f32[8,2,512]{2,1,0:T(2,128)S(1)} %bitcast.313), kind=kLoop, calls=%fused_computation.4 | loop fusion | flops 16777216 | bytes 42008576 | tf_op jit(solution)/shard_map/convert_element_type | solution.py:454
  534.3 7.6 %fusion.40 = f32[1024,2048]{1,0:T(8,128)} fusion(bf16[512,512]{0,1:T(8,128)(2,1)S(1)} %bitcast.295, bf16[512,512]{0,1:T(8,128)(2,1)} %bitcast.309, bf16[512,1024]{0,1:T(8,128)(2,1)} %bitcast.300, bf16[512,1024]{1,0:T(8,128)(2,1)} %param.14, f32[1024]{0:T(1024)S(1)} %copy-done.64, f32[512]{0:T(512)S(1)} %copy-done.66), kind=kOutput, calls=%fused_computation.112 | convolution fusion | flops 2155872256 | bytes 11540480 | tf_op jit(solution)/shard_map/dot_general | solution.py:59
  542.0 10.3 %concatenate.82 = f32[4,2,128,2176]{3,2,1,0:T(8,128)} concatenate(f32[4,2,128,2048]{3,2,1,0:T(8,128)} %bitcast.266, f32[4,2,128,1]{3,2,1,0:T(8,128)S(1)} %copy.107, f32[4,2,128,127]{3,2,1,0:T(8,128)S(1)} %broadcast_in_dim.144), dimensions={3} | concatenate | bytes 17825792 | tf_op jit(solution)/shard_map/concatenate | solution.py:490
  592.7 8.1 %collective-permute-done.12 = bf16[128,2176]{1,0:T(8,128)(2,1)S(1)} collective-permute-done((bf16[128,2176]{1,0:T(8,128)(2,1)S(1)}, bf16[128,2176]{1,0:T(8,128)(2,1)S(1)}, u32[]{:S(2)}, u32[]{:S(2)}) %collective-permute-start.12) | collective-permute-done | bytes 557088 | tf_op jit(solution)/shard_map/ppermute | solution.py:117
  600.8 11.2 %collective-permute-done.13 = bf16[128,2176]{1,0:T(8,128)(2,1)S(1)} collective-permute-done((bf16[128,2176]{1,0:T(8,128)(2,1)S(1)}, bf16[128,2176]{1,0:T(8,128)(2,1)S(1)}, u32[]{:S(2)}, u32[]{:S(2)}) %collective-permute-start.13) | collective-permute-done | bytes 557088 | tf_op jit(solution)/shard_map/ppermute | solution.py:117
  (349 shorter events, 234.0 us)
Async XLA Ops:
  7.3 112.6 %all-gather.6.cloned.1.call-start = ((), (), s32[]{:S(2)}) async-start(), calls=%async_computation.6 | async-start | bytes 9732096 | tf_op jit(solution)/shard_map/all_gather | solution.py:320
  10.9 183.5 %all-gather.4.cloned.1.call-start = ((), (), s32[]{:S(2)}) async-start(), calls=%async_computation.3 | async-start | bytes 9437184 | tf_op jit(solution)/shard_map/all_gather | solution.py:389
  12.8 16.5 %collective-permute-start = (bf16[128,2176]{1,0:T(8,128)(2,1)S(1)}, bf16[128,2176]{1,0:T(8,128)(2,1)S(1)}, u32[]{:S(2)}, u32[]{:S(2)}) collective-permute-start(bf16[128,2176]{1,0:T(8,128)(2,1)S(1)} %constant_dynamic-slice_fusion.1), channel_id=1, source_target_pairs={{0,1},{1,0},{2,3},{3,2},{4,5},{5,4},{6,7},{7,6},{8,9},{9,8},{10,11... | collective-permute-start | bytes 1671176 | tf_op jit(solution)/shard_map/ppermute | solution.py:80
  15.8 26.0 %collective-permute-start.1 = (bf16[128,2176]{1,0:T(8,128)(2,1)S(1)}, bf16[128,2176]{1,0:T(8,128)(2,1)S(1)}, u32[]{:S(2)}, u32[]{:S(2)}) collective-permute-start(bf16[128,2176]{1,0:T(8,128)(2,1)S(1)} %constant_dynamic-slice_fusion.1), channel_id=1, source_target_pairs={{0,2},{1,3},{2,0},{3,1},{4,6},{5,7},{6,4},{7,5},{8,10},{9,11},{10,... | collective-permute-start | bytes 1671176 | tf_op jit(solution)/shard_map/ppermute | solution.py:80
  17.4 24.5 %collective-permute-start.2 = (bf16[128,2176]{1,0:T(8,128)(2,1)S(1)}, bf16[128,2176]{1,0:T(8,128)(2,1)S(1)}, u32[]{:S(2)}, u32[]{:S(2)}) collective-permute-start(bf16[128,2176]{1,0:T(8,128)(2,1)S(1)} %constant_dynamic-slice_fusion.1), channel_id=1, source_target_pairs={{0,3},{1,2},{2,1},{3,0},{4,7},{5,6},{6,5},{7,4},{8,11},{9,10},{10,... | collective-permute-start | bytes 1671176 | tf_op jit(solution)/shard_map/ppermute | solution.py:80
  43.5 22.5 %collective-permute-start.3 = (bf16[4,128,2176]{2,1,0:T(8,128)(2,1)}, bf16[4,128,2176]{2,1,0:T(8,128)(2,1)}, u32[]{:S(2)}, u32[]{:S(2)}) collective-permute-start(bf16[4,128,2176]{2,1,0:T(8,128)(2,1)} %pad_maximum_fusion.3), channel_id=1, source_target_pairs={{0,4},{4,0},{8,12},{12,8},{16,20},{20,16},{24,28},{28,24},{1,5},{5... | collective-permute-start | bytes 6684680 | tf_op jit(solution)/shard_map/ppermute | solution.py:89
  45.7 13.2 %collective-permute-start.6 = (bf16[128,1024]{1,0:T(8,128)(2,1)S(1)}, bf16[128,1024]{1,0:T(8,128)(2,1)S(1)}, u32[]{:S(2)}, u32[]{:S(2)}) collective-permute-start(bf16[128,1024]{1,0:T(8,128)(2,1)S(1)} %constant_dynamic-slice_fusion), channel_id=1, source_target_pairs={{0,3},{1,2},{2,1},{3,0},{4,7},{5,6},{6,5},{7,4},{8,11},{9,10},{10,... | collective-permute-start | bytes 786440 | tf_op jit(solution)/shard_map/ppermute | solution.py:80
  111.6 340.1 %reduce-scatter.5.cloned.1.call-start = ((), (), s32[]{:S(2)}) async-start(), calls=%async_computation.5 | async-start | bytes 9437184 | tf_op jit(solution)/shard_map/reduce_scatter | solution.py:394
  114.1 38.5 %collective-permute-start.10 = (bf16[2,384,1024]{2,1,0:T(8,128)(2,1)}, bf16[2,384,1024]{2,1,0:T(8,128)(2,1)}, u32[]{:S(2)}, u32[]{:S(2)}) collective-permute-start(bf16[2,384,1024]{2,1,0:T(8,128)(2,1)} %pad_maximum_fusion.7.refs_0_), channel_id=1, source_target_pairs={{0,3},{1,2},{2,1},{3,0},{4,7},{5,6},{6,5},{7,4},{8,11},{9,10},{10,... | collective-permute-start | bytes 4718600 | tf_op jit(solution)/shard_map/ppermute | solution.py:80
  115.9 69.0 %collective-permute-start.8 = (bf16[2,384,1024]{2,1,0:T(8,128)(2,1)}, bf16[2,384,1024]{2,1,0:T(8,128)(2,1)}, u32[]{:S(2)}, u32[]{:S(2)}) collective-permute-start(bf16[2,384,1024]{2,1,0:T(8,128)(2,1)} %pad_maximum_fusion.7.refs_0_), channel_id=1, source_target_pairs={{0,1},{1,0},{2,3},{3,2},{4,5},{5,4},{6,7},{7,6},{8,9},{9,8},{10,11... | collective-permute-start | bytes 4718600 | tf_op jit(solution)/shard_map/ppermute | solution.py:80
  116.4 69.0 %collective-permute-start.9 = (bf16[2,384,1024]{2,1,0:T(8,128)(2,1)}, bf16[2,384,1024]{2,1,0:T(8,128)(2,1)}, u32[]{:S(2)}, u32[]{:S(2)}) collective-permute-start(bf16[2,384,1024]{2,1,0:T(8,128)(2,1)} %pad_maximum_fusion.7.refs_0_), channel_id=1, source_target_pairs={{0,2},{1,3},{2,0},{3,1},{4,6},{5,7},{6,4},{7,5},{8,10},{9,11},{10,... | collective-permute-start | bytes 4718600 | tf_op jit(solution)/shard_map/ppermute | solution.py:80
  277.7 178.9 %reduce-scatter.3.cloned.1.call-start = ((), (), s32[]{:S(2)}) async-start(), calls=%async_computation.4 | async-start | bytes 9437184 | tf_op jit(solution)/shard_map/reduce_scatter | solution.py:393
  373.3 37.6 %collective-permute-start.33 = (bf16[2,384,1024]{2,1,0:T(8,128)(2,1)}, bf16[2,384,1024]{2,1,0:T(8,128)(2,1)}, u32[]{:S(2)}, u32[]{:S(2)}) collective-permute-start(bf16[2,384,1024]{2,1,0:T(8,128)(2,1)} %get-tuple-element.84), channel_id=1, source_target_pairs={{0,1},{1,0},{2,3},{3,2},{4,5},{5,4},{6,7},{7,6},{8,9},{9,8},{10,11... | collective-permute-start | bytes 4718600 | tf_op jit(solution)/shard_map/ppermute | solution.py:117
  374.7 70.1 %collective-permute-start.34 = (bf16[2,384,1024]{2,1,0:T(8,128)(2,1)}, bf16[2,384,1024]{2,1,0:T(8,128)(2,1)}, u32[]{:S(2)}, u32[]{:S(2)}) collective-permute-start(bf16[2,384,1024]{2,1,0:T(8,128)(2,1)} %get-tuple-element.85), channel_id=1, source_target_pairs={{0,2},{1,3},{2,0},{3,1},{4,6},{5,7},{6,4},{7,5},{8,10},{9,11},{10,... | collective-permute-start | bytes 4718600 | tf_op jit(solution)/shard_map/ppermute | solution.py:117
  376.2 68.7 %collective-permute-start.35 = (bf16[2,384,1024]{2,1,0:T(8,128)(2,1)}, bf16[2,384,1024]{2,1,0:T(8,128)(2,1)}, u32[]{:S(2)}, u32[]{:S(2)}) collective-permute-start(bf16[2,384,1024]{2,1,0:T(8,128)(2,1)} %get-tuple-element.86), channel_id=1, source_target_pairs={{0,3},{1,2},{2,1},{3,0},{4,7},{5,6},{6,5},{7,4},{8,11},{9,10},{10,... | collective-permute-start | bytes 4718600 | tf_op jit(solution)/shard_map/ppermute | solution.py:117
  524.9 29.9 %collective-permute-start.22 = (bf16[4,128,1152]{2,1,0:T(8,128)(2,1)}, bf16[4,128,1152]{2,1,0:T(8,128)(2,1)}, u32[]{:S(2)}, u32[]{:S(2)}) collective-permute-start(bf16[4,128,1152]{2,1,0:T(8,128)(2,1)} %fusion.31), channel_id=1, source_target_pairs={{0,4},{4,0},{8,12},{12,8},{16,20},{20,16},{24,28},{28,24},{1,5},{5... | collective-permute-start | bytes 3538952 | tf_op jit(solution)/shard_map/ppermute | solution.py:89
  554.7 29.9 %collective-permute-start.11 = (bf16[4,128,2176]{2,1,0:T(8,128)(2,1)S(1)}, bf16[4,128,2176]{2,1,0:T(8,128)(2,1)S(1)}, u32[]{:S(2)}, u32[]{:S(2)}) collective-permute-start(bf16[4,128,2176]{2,1,0:T(8,128)(2,1)S(1)} %fusion.10), channel_id=1, source_target_pairs={{0,4},{4,0},{8,12},{12,8},{16,20},{20,16},{24,28},{28,24},{1,5},{5... | collective-permute-start | bytes 6684680 | tf_op jit(solution)/shard_map/ppermute | solution.py:89
  558.9 15.4 %collective-permute-start.24 = (bf16[128,1152]{1,0:T(8,128)(2,1)S(1)}, bf16[128,1152]{1,0:T(8,128)(2,1)S(1)}, u32[]{:S(2)}, u32[]{:S(2)}) collective-permute-start(bf16[128,1152]{1,0:T(8,128)(2,1)S(1)} %get-tuple-element.100), channel_id=1, source_target_pairs={{0,2},{1,3},{2,0},{3,1},{4,6},{5,7},{6,4},{7,5},{8,10},{9,11},{10,... | collective-permute-start | bytes 884744 | tf_op jit(solution)/shard_map/ppermute | solution.py:117
  560.4 13.9 %collective-permute-start.25 = (bf16[128,1152]{1,0:T(8,128)(2,1)S(1)}, bf16[128,1152]{1,0:T(8,128)(2,1)S(1)}, u32[]{:S(2)}, u32[]{:S(2)}) collective-permute-start(bf16[128,1152]{1,0:T(8,128)(2,1)S(1)} %get-tuple-element.99), channel_id=1, source_target_pairs={{0,3},{1,2},{2,1},{3,0},{4,7},{5,6},{6,5},{7,4},{8,11},{9,10},{10,... | collective-permute-start | bytes 884744 | tf_op jit(solution)/shard_map/ppermute | solution.py:117
  585.2 15.6 %collective-permute-start.12 = (bf16[128,2176]{1,0:T(8,128)(2,1)S(1)}, bf16[128,2176]{1,0:T(8,128)(2,1)S(1)}, u32[]{:S(2)}, u32[]{:S(2)}) collective-permute-start(bf16[128,2176]{1,0:T(8,128)(2,1)S(1)} %get-tuple-element.87), channel_id=1, source_target_pairs={{0,1},{1,0},{2,3},{3,2},{4,5},{5,4},{6,7},{7,6},{8,9},{9,8},{10,11... | collective-permute-start | bytes 1671176 | tf_op jit(solution)/shard_map/ppermute | solution.py:117
  586.7 25.3 %collective-permute-start.13 = (bf16[128,2176]{1,0:T(8,128)(2,1)S(1)}, bf16[128,2176]{1,0:T(8,128)(2,1)S(1)}, u32[]{:S(2)}, u32[]{:S(2)}) collective-permute-start(bf16[128,2176]{1,0:T(8,128)(2,1)S(1)} %get-tuple-element.89), channel_id=1, source_target_pairs={{0,2},{1,3},{2,0},{3,1},{4,6},{5,7},{6,4},{7,5},{8,10},{9,11},{10,... | collective-permute-start | bytes 1671176 | tf_op jit(solution)/shard_map/ppermute | solution.py:117
  587.3 24.7 %collective-permute-start.14 = (bf16[128,2176]{1,0:T(8,128)(2,1)S(1)}, bf16[128,2176]{1,0:T(8,128)(2,1)S(1)}, u32[]{:S(2)}, u32[]{:S(2)}) collective-permute-start(bf16[128,2176]{1,0:T(8,128)(2,1)S(1)} %get-tuple-element.88), channel_id=1, source_target_pairs={{0,3},{1,2},{2,1},{3,0},{4,7},{5,6},{6,5},{7,4},{8,11},{9,10},{10,... | collective-permute-start | bytes 1671176 | tf_op jit(solution)/shard_map/ppermute | solution.py:117
  590.3 26.6 %collective-permute-start.30 = (bf16[32,1152]{1,0:T(8,128)(2,1)S(1)}, bf16[32,1152]{1,0:T(8,128)(2,1)S(1)}, u32[]{:S(2)}, u32[]{:S(2)}) collective-permute-start(bf16[32,1152]{1,0:T(8,128)(2,1)S(1)} %get-tuple-element.81), channel_id=1, source_target_pairs={{0,16},{4,20},{8,24},{12,28},{16,0},{20,4},{24,8},{28,12},{1,17},{... | collective-permute-start | bytes 221192 | tf_op jit(solution)/shard_map/ppermute | solution.py:145
  591.4 35.4 %collective-permute-start.31 = (bf16[32,1152]{1,0:T(8,128)(2,1)S(1)}, bf16[32,1152]{1,0:T(8,128)(2,1)S(1)}, u32[]{:S(2)}, u32[]{:S(2)}) collective-permute-start(bf16[32,1152]{1,0:T(8,128)(2,1)S(1)} %get-tuple-element.81), channel_id=1, source_target_pairs={{0,24},{4,28},{8,0},{12,4},{16,8},{20,12},{24,16},{28,20},{1,25},{... | collective-permute-start | bytes 221192 | tf_op jit(solution)/shard_map/ppermute | solution.py:145
  (94 other events, 690.1 us)
Sparse Core Ops, SparseCore 0:
  11.0 86.9 all-gather.5
  111.7 82.5 all-gather.3
  277.8 88.1 reduce-scatter.4
  368.2 88.4 reduce-scatter.2

commit v2 on v1

--- a/solution.py
+++ b/solution.py
@@ -12,6 +12,8 @@
 KEY_VALUE_HEADS = 8
 HEAD_DIM = 64
 LANES = 128
+VMEM_LIMIT = 58 * 1024 * 1024
+CHUNKS = 2
 F32 = jnp.float32
 BF16 = jnp.bfloat16
 
@@ -106,14 +108,17 @@
     return both.reshape(count * rows.shape[0], rows.shape[1])
 
 
-def scatter_sum(blocks):
+def scatter_sum(values, axis):
     count = lax.axis_size("shard")
     if count != 4:
-        return lax.psum_scatter(blocks.astype(BF16), "shard", scatter_dimension=0).astype(F32)
+        return lax.psum_scatter(
+            values.astype(BF16), "shard", scatter_dimension=axis, tiled=True
+        ).astype(F32)
     me = lax.axis_index("shard")
-    total = pick(blocks, me).astype(F32)
+    size = values.shape[axis] // count
+    total = lax.dynamic_slice_in_dim(values, me * size, size, axis).astype(F32)
     for flip in (1, 2, 3):
-        sent = pick(blocks, me ^ flip).astype(BF16)
+        sent = lax.dynamic_slice_in_dim(values, (me ^ flip) * size, size, axis).astype(BF16)
         got = lax.ppermute(sent, "shard", [(i, i ^ flip) for i in range(4)])
         total = total + got.astype(F32)
     return total
@@ -131,7 +136,7 @@
     mine = lax.dynamic_index_in_dim(blocks, core, 1, keepdims=False)
     away = lax.dynamic_index_in_dim(blocks, 1 - core, 1, keepdims=False)
     paired = mine + swap_cores(away.astype(BF16)).astype(F32)
-    local = scatter_sum(paired).reshape(layers, half // layers, width)
+    local = scatter_sum(paired, 0).reshape(layers, half // layers, width)
     total = pick(local, layer)
     for step in range(1, layers):
         perm = [(i, (i + 2 * step) % size) for i in range(size)]
@@ -151,7 +156,7 @@
     return jnp.concatenate([low, high], axis=0).astype(F32)
 
 
-def expert_kernel(count, experts, place_ref, x_ref, dy_ref, mask_ref, router_ref, *refs):
+def expert_kernel(count, place_ref, x_ref, dy_ref, mask_ref, router_ref, *refs):
     pieces = refs[:count]
     out_ref, row_ref, act_ref, gate_ref, up_ref, score_ref, gu, down, sem = refs[count:]
     local, rows, width = pieces[0].shape
@@ -183,16 +188,16 @@
             copy.wait()
 
     x = x_ref[...]
-    dy = dy_ref[...]
-    lane = lax.broadcasted_iota(jnp.int32, (x.shape[0], LANES), 1)
-    logits = jnp.where(
-        mask_ref[...] > 0, jnp.dot(x, router_ref[...], preferred_element_type=F32), -1e30
-    )
+    tile = x.shape[0]
+    dy = dy_ref[...].reshape(tile, width)
+    mask = mask_ref[...].reshape(tile, LANES)
+    lane = lax.broadcasted_iota(jnp.int32, (tile, LANES), 1)
+    logits = jnp.where(mask > 0, jnp.dot(x, router_ref[...], preferred_element_type=F32), -1e30)
     powers = jnp.exp(logits - jnp.max(logits, axis=1, keepdims=True))
     chances = powers / jnp.sum(powers, axis=1, keepdims=True)
     out = None
     row = None
-    scores = jnp.zeros((x.shape[0], LANES), F32)
+    scores = jnp.zeros((tile, LANES), F32)
     for j in range(local):
         own = place_ref[count] * local + j
         gate = jnp.sum(jnp.where(lane == own, chances, 0.0), axis=1, keepdims=True)
@@ -202,14 +207,14 @@
         gate_val = jnp.dot(x, left, preferred_element_type=F32)
         up_val = jnp.dot(x, right, preferred_element_type=F32)
         inner_grad = product_transposed_right(dy, back)
-        sigmoid = 1.0 / (1.0 + jnp.exp(-gate_val))
+        sigmoid = 0.5 + 0.5 * jnp.tanh(0.5 * gate_val)
         swish = gate_val * sigmoid
         inner = (swish * up_val).astype(BF16).astype(F32)
         score = jnp.sum(inner * inner_grad, axis=1, keepdims=True)
         scores = jnp.where(lane == j, score, scores)
         act = (gate * inner).astype(BF16)
         scaled = gate * inner_grad
-        gate_back = (scaled * up_val * sigmoid * (1.0 + gate_val * (1.0 - sigmoid))).astype(BF16)
+        gate_back = (scaled * up_val * (sigmoid + swish * (1.0 - sigmoid))).astype(BF16)
         up_back = (scaled * swish).astype(BF16)
         act_ref[:, j * hidden : (j + 1) * hidden] = act
         gate_ref[:, j * hidden : (j + 1) * hidden] = gate_back
@@ -223,25 +228,27 @@
     score_ref[...] = scores
 
 
-def run_experts(every_x, every_dy, mask, router, pieces, tile):
+def run_experts(every_x, every_dy, mask, router, pieces, chunk):
     count = len(pieces)
     total, width = every_x.shape
     local, rows, _ = pieces[0][0].shape
     third = rows // 3
-    hidden = width // 2
+    peers = every_dy.shape[0]
+    rows_each = total // peers
+    group = 2
+    tile = group * rows_each
     place = jnp.stack([index for _, index in pieces] + [lax.axis_index("expert")]).astype(jnp.int32)
     block = pl.BlockSpec((tile, width), lambda i, p: (i, 0))
     thin = pl.BlockSpec((tile, LANES), lambda i, p: (i, 0))
-    steps = every_dy.shape[1] // tile
     return pl.pallas_call(
-        functools.partial(expert_kernel, count, router.shape[1]),
+        functools.partial(expert_kernel, count),
         grid_spec=pltpu.PrefetchScalarGridSpec(
             num_scalar_prefetch=1,
-            grid=(total // tile,),
+            grid=(peers // group,),
             in_specs=[
                 block,
-                pl.BlockSpec((None, tile, width), lambda i, p: (i // steps, i % steps, 0)),
-                thin,
+                pl.BlockSpec((group, rows_each, width), lambda i, p: (i, chunk, 0)),
+                pl.BlockSpec((group, rows_each, LANES), lambda i, p: (i, chunk, 0)),
                 pl.BlockSpec((width, LANES), lambda i, p: (0, 0)),
             ]
             + [pl.BlockSpec(memory_space=pl.ANY)] * count,
@@ -254,12 +261,81 @@
         ),
         out_shape=[jax.ShapeDtypeStruct((total, width), BF16)] * 5
         + [jax.ShapeDtypeStruct((total, LANES), F32)],
-        compiler_params=pltpu.CompilerParams(vmem_limit_bytes=58 * 1024 * 1024),
+        compiler_params=pltpu.CompilerParams(vmem_limit_bytes=VMEM_LIMIT),
         cost_estimate=pl.CostEstimate(
             flops=2 * total * width * width * 6, bytes_accessed=total * width * 14, transcendentals=0
         ),
         name="experts",
     )(place, every_x, every_dy, mask, router, *[piece for piece, _ in pieces])
+
+
+def columns_kernel(chunks, local, *refs):
+    xs, gates, ups = refs[:chunks], refs[chunks : 2 * chunks], refs[2 * chunks : 3 * chunks]
+    out_ref = refs[3 * chunks]
+    hidden = out_ref.shape[2] // 2
+    for j in range(local):
+        for side, values in ((0, gates), (1, ups)):
+            total = None
+            for x_ref, value_ref in zip(xs, values):
+                part = product_tn(x_ref[...], value_ref[:, j * hidden : (j + 1) * hidden])
+                total = part if total is None else total + part
+            out_ref[j, :, side * hidden : (side + 1) * hidden] = total.astype(BF16)
+
+
+def gate_up_gradient(xs, gates, ups, local):
+    rows, width = xs[0].shape
+    chunks = len(xs)
+    piece = width // 4
+    whole = pl.BlockSpec((rows, width), lambda i: (0, 0), pipeline_mode=pl.Buffered(1))
+    return pl.pallas_call(
+        functools.partial(columns_kernel, chunks, local),
+        grid=(4,),
+        in_specs=[pl.BlockSpec((rows, piece), lambda i: (0, i))] * chunks + [whole] * (2 * chunks),
+        out_specs=pl.BlockSpec((local, piece, width), lambda i: (0, i, 0)),
+        out_shape=jax.ShapeDtypeStruct((local, width, width), BF16),
+        compiler_params=pltpu.CompilerParams(vmem_limit_bytes=VMEM_LIMIT),
+        cost_estimate=pl.CostEstimate(
+            flops=4 * chunks * rows * width * width, bytes_accessed=chunks * rows * width * 6, transcendentals=0
+        ),
+        name="gate_up_gradient",
+    )(*xs, *gates, *ups)
+
+
+def down_kernel(chunks, *refs):
+    total = None
+    for act_ref, dy_ref in zip(refs[:chunks], refs[chunks : 2 * chunks]):
+        dy = dy_ref[...].reshape(act_ref.shape[0], dy_ref.shape[2])
+        part = product_tn(act_ref[...], dy)
+        total = part if total is None else total + part
+    refs[2 * chunks][...] = total.astype(BF16)
+
+
+def down_gradient(acts, every_dy, local):
+    rows, width = acts[0].shape
+    chunks = len(acts)
+    peers = every_dy.shape[0]
+    piece = width // 4
+
+    def spec(chunk):
+        return pl.BlockSpec(
+            (peers, rows // peers, width),
+            lambda i: (0, chunk, 0),
+            pipeline_mode=pl.Buffered(1),
+        )
+
+    return pl.pallas_call(
+        functools.partial(down_kernel, chunks),
+        grid=(4,),
+        in_specs=[pl.BlockSpec((rows, piece), lambda i: (0, i))] * chunks
+        + [spec(chunk) for chunk in range(chunks)],
+        out_specs=pl.BlockSpec((piece, width), lambda i: (i, 0)),
+        out_shape=jax.ShapeDtypeStruct((width, width), BF16),
+        compiler_params=pltpu.CompilerParams(vmem_limit_bytes=VMEM_LIMIT),
+        cost_estimate=pl.CostEstimate(
+            flops=2 * chunks * rows * width * width, bytes_accessed=chunks * rows * width * 4, transcendentals=0
+        ),
+        name="down_gradient",
+    )(*acts, *([every_dy] * chunks)).reshape(local, width // local, width)
 
 
 def per_device(
@@ -332,8 +408,8 @@
         axis=0,
     )
     every_mask = jnp.pad(
-        every_dy[:, total_rows : total_rows + mask_rows].reshape(peers * total_rows, experts),
-        ((0, 0), (0, LANES - experts)),
+        every_dy[:, total_rows : total_rows + mask_rows].reshape(peers, total_rows, experts),
+        ((0, 0), (0, 0), (0, LANES - experts)),
     )
 
     inputs = tokens.astype(jnp.float32)
@@ -386,38 +462,45 @@
     logits = matrix_product(mixed_in, router_w)
     gates = jax.nn.softmax(jnp.where(chosen, logits, -1e30), axis=-1)
 
-    every_x = lax.all_gather(mixed_in, "expert", axis=0, tiled=True)
-    out_part, row_part, act, gate_back, up_back, scores_part = run_experts(
-        every_x, every_dy, every_mask, router_lanes, pieces, 512 if total_rows % 512 == 0 else 128
-    )
-    out_sum = lax.psum_scatter(out_part, "expert", scatter_dimension=0, tiled=True)
-    row_sum = lax.psum_scatter(row_part, "expert", scatter_dimension=0, tiled=True)
-    sent_scores = scores_part[:, :local_experts].reshape(peers, -1, LANES)
+    part = total_rows // CHUNKS
+    every_x, out_part, row_part, act, gate_back, up_back, scores_part = [], [], [], [], [], [], []
+    for chunk in range(CHUNKS):
+        gathered = lax.all_gather(
+            mixed_in[chunk * part : (chunk + 1) * part], "expert", axis=0, tiled=True
+        )
+        results = run_experts(gathered, every_dy, every_mask, router_lanes, pieces, chunk)
+        every_x.append(gathered)
+        for kept, result in zip((out_part, row_part, act, gate_back, up_back, scores_part), results):
+            kept.append(result)
+    row_sum = [
+        lax.psum_scatter(rows, "expert", scatter_dimension=0, tiled=True) for rows in row_part
+    ]
+    sent_scores = jnp.concatenate(
+        [
+            values[:, :local_experts].reshape(peers, -1, LANES)
+            for values in scores_part
+        ],
+        axis=1,
+    )
     gate_grad = lax.all_to_all(sent_scores, "expert", split_axis=0, concat_axis=0, tiled=True)
     gate_grad = (
         gate_grad.reshape(peers, total_rows, local_experts)
         .transpose(1, 0, 2)
         .reshape(total_rows, experts)
     )
+    *out_part, row_last = lax.optimization_barrier((*out_part, row_sum[-1]))
+    row_sum = jnp.concatenate([*row_sum[:-1], row_last], axis=0)
+    out_sum = jnp.concatenate(
+        [lax.psum_scatter(rows, "expert", scatter_dimension=0, tiled=True) for rows in out_part],
+        axis=0,
+    )
     output = hidden_state + out_sum.astype(F32)
     upstream = cotangent.astype(jnp.float32)
 
-    flat_dy = every_dy[:, :total_rows].reshape(peers * total_rows, model_width)
-    down_grad = product_tn(act, flat_dy).astype(BF16)
-    gate_grad_w = product_tn(every_x, gate_back).astype(BF16)
-    up_grad_w = product_tn(every_x, up_back).astype(BF16)
-    gu_grad = jnp.stack(
-        [gate_grad_w.reshape(model_width, local_experts, hidden),
-         up_grad_w.reshape(model_width, local_experts, hidden)], axis=2
-    )
-    gu_blocks = gu_grad.reshape(count, part_rows, local_experts, 2 * hidden).transpose(0, 2, 1, 3)
-    down_blocks = down_grad.reshape(
-        local_experts, count, hidden // count, model_width
-    ).transpose(1, 0, 2, 3)
-    expert_sum = scatter_sum(jnp.concatenate([gu_blocks, down_blocks], axis=2))
-    expert_gate_sum = expert_sum[:, :part_rows, :hidden]
-    expert_up_sum = expert_sum[:, :part_rows, hidden:]
-    expert_down_sum = expert_sum[:, part_rows:, :]
+    expert_down_sum = scatter_sum(down_gradient(act, every_dy, local_experts), 1)
+    gu_sum = scatter_sum(gate_up_gradient(every_x, gate_back, up_back, local_experts), 1)
+    expert_gate_sum = gu_sum[:, :, :hidden]
+    expert_up_sum = gu_sum[:, :, hidden:]
 
     logit_grad = (
         gates * (gate_grad - jnp.sum(gates * gate_grad, axis=1, keepdims=True))

time: 661 us -> 636 us (0.962)
  Pallas kernels: 83.4 us -> 130 us
  matrix products: 113 us -> 70.3 us
  local copies, waits for them, and re-layouts: 94.3 us -> 57.2 us
  waiting for transfers between devices: 217 us -> 232 us
  other arithmetic: 82.8 us -> 73.4 us
    pallas_call x1 -> x4, Pallas kernels: 83.4 us -> 130 us  [the longest x2 88.8 us: run_experts(): pl.pallas_call(functools.partial(expert_kernel, count), grid_spec=pltpu.P...]
    dot_general x6 -> x3, matrix products: 55.4 us -> 12.3 us  [product_tn(): lax.dot_general(left_side, right_side, (((0,), (0,)), ((), ())), preferre...]
    reduce_scatter x2 -> x4, waiting for transfers between devices: 0.71 us -> 23.9 us  [per_device(): lax.psum_scatter(rows, 'expert', scatter_dimension=0, tiled=True)]
    another operation x2 -> x0, local copies, waits for them, and re-layouts: 21.6 us -> none  [per_device(): jnp.stack([gate_grad_w.reshape(model_width, local_experts, hidden), up_gr...]
    reshape x2, local copies, waits for them, and re-layouts: 11.1 us -> 1.05 us  [per_device(): values[:, :local_experts].reshape(peers, -1, LANES)]
    another operation x6 -> x5, other arithmetic: 12.2 us -> 2.43 us  [the longest x1 11 us: per_device(): jnp.stack([gate_grad_w.reshape(model_width, local_experts, hidden), up_gr...]
    all_gather x1 -> x2, waiting for transfers between devices: 8.89 us -> 0.02 us  [per_device(): lax.all_gather(mixed_in[chunk * part:(chunk + 1) * part], 'expert', axis=...]
    slice x3 -> x2, local copies, waits for them, and re-layouts: 10.3 us -> 2.52 us  [the longest x1 1.49 us: per_device(): expert_up_sum = gu_sum[:, :, hidden:]]
  transfers between devices with their start and end apart: 41 -> 47, of which waited for: 25 -> 29; matrix products, arithmetic and copies ran while one was open for 32% -> 19% of each run, Pallas kernels for 0% -> 21%
where the time goes in v2:
time: 636 us; the launch traced here: 626 us
  waiting for transfers between devices  232 us (36%)
  Pallas kernels  130 us (20%)
  other arithmetic  73.4 us (12%)
  matrix products  70.3 us (11%)
  local copies, waits for them, and re-layouts  57.2 us (9%)
  starting transfers between devices  47.7 us (8%)
  between operations  15.8 us (2%)
    ppermute x9, waiting for transfers between devices, gather_pieces(): got = lax.ppermute(piece, 'shard', [(i, i ^ flip) for i in range(4)])  96.6 us
    pallas_call x2, Pallas kernels, run_experts(): pl.pallas_call(functools.partial(expert_kernel, count), grid_spec=pltpu.P...  88.8 us
    ppermute x12, waiting for transfers between devices, scatter_sum(): got = lax.ppermute(sent, 'shard', [(i, i ^ flip) for i in range(4)])  81.8 us
    pallas_call x1, Pallas kernels, gate_up_gradient(): pl.pallas_call(functools.partial(columns_kernel, chunks, local), grid=(4,...  26 us
    reduce_scatter x4, waiting for transfers between devices, per_device(): lax.psum_scatter(rows, 'expert', scatter_dimension=0, tiled=True)  23.9 us
    dot_general x1, matrix products, per_device(): jnp.einsum('vuol,mul->uovm', attended_gradient, value_matrix_rows, prefer...  15.4 us
    ppermute x12, starting transfers between devices, scatter_sum(): got = lax.ppermute(sent, 'shard', [(i, i ^ flip) for i in range(4)])  15.1 us
    pallas_call x1, Pallas kernels, down_gradient(): pl.pallas_call(functools.partial(down_kernel, chunks), grid=(4,), in_spec...  15 us
  transfers between devices with their start and end apart: 47, of which 29 were waited for; matrix products, arithmetic and copies ran while one was open for 19% of the time, Pallas kernels for 21%

profile of v2, /device:TPU:0, one launch (start us, length us, event | category | flops | bytes accessed | tf_op | source)
XLA Modules:
  0.0 626.0 jit_solution(12191637910129155593)
XLA Ops:
  17.4 11.0 %collective-permute-done.1 = bf16[128,2176]{1,0:T(8,128)(2,1)S(1)} collective-permute-done((bf16[128,2176]{1,0:T(8,128)(2,1)S(1)}, bf16[128,2176]{1,0:T(8,128)(2,1)S(1)}, u32[]{:S(2)}, u32[]{:S(2)}) %collective-permute-start.1) | collective-permute-done | bytes 557088 | tf_op jit(solution)/shard_map/ppermute | solution.py:82
  31.4 10.3 %collective-permute-done.2 = bf16[128,2176]{1,0:T(8,128)(2,1)S(1)} collective-permute-done((bf16[128,2176]{1,0:T(8,128)(2,1)S(1)}, bf16[128,2176]{1,0:T(8,128)(2,1)S(1)}, u32[]{:S(2)}, u32[]{:S(2)}) %collective-permute-start.2) | collective-permute-done | bytes 557088 | tf_op jit(solution)/shard_map/ppermute | solution.py:82
  70.2 6.7 %pad_maximum_fusion.1 = bf16[1024,2176]{1,0:T(8,128)(2,1)S(1)} fusion(bf16[256,2176]{1,0:T(8,128)(2,1)S(1)} %get-tuple-element.106, bf16[256,2176]{1,0:T(8,128)(2,1)S(1)} %get-tuple-element.107, bf16[256,2176]{1,0:T(8,128)(2,1)S(1)} %get-tuple-element.108, bf16[256,2176]{1,0:T(8,128)(2,1)S(1)} %get-tuple-element.105), kind=kLoop, calls=%fused_computation.11 | loop fusion | flops 17825792 | bytes 8912896 | tf_op jit(solution)/shard_map/concatenate | solution.py:107
  80.8 7.7 %fusion.64 = (f32[8,2,512]{2,1,0:T(2,128)S(1)}, f32[8,2,512,512]{2,3,1,0:T(8,128)}) fusion(bf16[512,8,2,32]{0,3,2,1:T(8,128)(2,1)S(1)} %bitcast.228, bf16[512,8,2,32]{0,3,2,1:T(8,128)(2,1)S(1)} %bitcast.226, bf16[512,8,32]{0,2,1:T(8,128)(2,1)S(1)} %get-tuple-element.137, bf16[512,8,32]{0,2,1:T(8,128)(2,1)S(1)} %get-tuple-element.136, ...), kind=kOutput, calls=%fused_computation.190 | convolution fusion | flops 552591360 | bytes 18644992 | tf_op jit(solution)/shard_map/vuol,mul->uovm/dot_general | solution.py:436
  88.5 8.3 %fusion.3 = f32[8,2,512]{2,1,0:T(2,128)S(1)} fusion(f32[8,2,512,512]{2,3,1,0:T(8,128)} %get-tuple-element.156, f32[8,2,512]{2,1,0:T(2,128)S(1)} %get-tuple-element.155), kind=kLoop, calls=%fused_computation.9 | loop fusion | flops 8380416 | bytes 16842752 | tf_op jit(solution)/shard_map/reduce_sum | solution.py:446
  96.8 7.3 %divide_convert_fusion = bf16[8,2,512,512]{2,3,1,0:T(8,128)(2,1)S(1)} fusion(f32[8,2,512,512]{2,3,1,0:T(8,128)} %get-tuple-element.156, f32[8,2,512]{2,1,0:T(2,128)S(1)} %fusion.3, f32[8,2,512]{2,1,0:T(2,128)S(1)} %get-tuple-element.155), kind=kLoop, calls=%fused_computation.7 | loop fusion | flops 12582912 | bytes 25231360 | tf_op jit(solution)/shard_map/convert_element_type | solution.py:449
  125.9 27.6 %collective-permute-done.10.refs_3_ = bf16[2,384,1024]{2,1,0:T(8,128)(2,1)} collective-permute-done((bf16[2,384,1024]{2,1,0:T(8,128)(2,1)}, bf16[2,384,1024]{2,1,0:T(8,128)(2,1)}, u32[]{:S(2)}, u32[]{:S(2)}) %collective-permute-start.10) | collective-permute-done | bytes 1572896 | tf_op jit(solution)/shard_map/ppermute | solution.py:82
  153.5 32.8 %collective-permute-done.9.refs_2_ = bf16[2,384,1024]{2,1,0:T(8,128)(2,1)} collective-permute-done((bf16[2,384,1024]{2,1,0:T(8,128)(2,1)}, bf16[2,384,1024]{2,1,0:T(8,128)(2,1)}, u32[]{:S(2)}, u32[]{:S(2)}) %collective-permute-start.9) | collective-permute-done | bytes 1572896 | tf_op jit(solution)/shard_map/ppermute | solution.py:82
  186.5 44.5 %experts.3 = (bf16[2048,1024]{1,0:T(8,128)(2,1)}, bf16[2048,1024]{1,0:T(8,128)(2,1)}, bf16[2048,1024]{1,0:T(8,128)(2,1)}, bf16[2048,1024]{1,0:T(8,128)(2,1)}, bf...) custom-call(s32[5]{0:T(128)} %stack.93.place_ref, bf16[2048,1024]{1,0:T(8,128)(2,1)} %all-gather.7.cloned.1.call-done.x_ref.refs_1_, ...), custom_call_target="tpu_custom_call" | custom-call | flops 25769803776 | bytes 29360128 | tf_op jit(solution)/shard_map/experts/pallas_call | solution.py:243
  231.2 44.2 %experts.2 = (bf16[2048,1024]{1,0:T(8,128)(2,1)}, bf16[2048,1024]{1,0:T(8,128)(2,1)}, bf16[2048,1024]{1,0:T(8,128)(2,1)}, bf16[2048,1024]{1,0:T(8,128)(2,1)}, bf...) custom-call(s32[5]{0:T(128)} %stack.93.place_ref, bf16[2048,1024]{1,0:T(8,128)(2,1)} %all-gather.5.cloned.1.call-done.x_ref.refs_0_, ...), custom_call_target="tpu_custom_call" | custom-call | flops 25769803776 | bytes 29360128 | tf_op jit(solution)/shard_map/experts/pallas_call | solution.py:243
  284.2 15.0 %down_gradient.1 = bf16[1024,1024]{1,0:T(8,128)(2,1)} custom-call(bf16[2048,1024]{1,0:T(8,128)(2,1)} %get-tuple-element.40.refs_0_, bf16[2048,1024]{1,0:T(8,128)(2,1)} %get-tuple-element.41.refs_1_, bf16[8,528,1024]{2,1,0:T(8,128)(2,1)} %bitcast.262, bf16[8,528,1024]{2,1,0:T(8,128)(2,1)} %bitcast.263), custom_call_target="tpu_custom_call" | custom-call | flops 8589934592 | bytes 16777216 | tf_op jit(solution)/shard_map/down_gradient/pallas_call | solution.py:326
  303.1 26.0 %gate_up_gradient.1 = bf16[2,1024,1024]{2,1,0:T(8,128)(2,1)} custom-call(bf16[2048,1024]{1,0:T(8,128)(2,1)} %all-gather.5.cloned.1.call-done.x_ref.refs_0_, bf16[2048,1024]{1,0:T(8,128)(2,1)} %all-gather.7.cloned.1.call-done.x_ref.refs_1_, bf16[2048,1024]{1,0:T(8,128)(2,1)} %get-tuple-element.36.refs_2_, bf16[2048,1024]{1,0:T(8,128)(2,1)} %get-tuple-element.37.refs_3_, ...), custom_call_target="tpu_custom_call" | custom-call | flops 17179869184 | bytes 25165824 | tf_op jit(solution)/shard_map/gate_up_gradient/pallas_call | solution.py:290
  351.3 39.9 %collective-permute-done.38 = bf16[2,128,1024]{2,1,0:T(8,128)(2,1)} collective-permute-done((bf16[2,128,1024]{2,1,0:T(8,128)(2,1)}, bf16[2,128,1024]{2,1,0:T(8,128)(2,1)}, u32[]{:S(2)}, u32[]{:S(2)}) %collective-permute-start.38) | collective-permute-done | bytes 524320 | tf_op jit(solution)/shard_map/ppermute | solution.py:122
  391.2 12.5 %collective-permute-done.37 = bf16[2,128,1024]{2,1,0:T(8,128)(2,1)S(1)} collective-permute-done((bf16[2,128,1024]{2,1,0:T(8,128)(2,1)S(1)}, bf16[2,128,1024]{2,1,0:T(8,128)(2,1)S(1)}, u32[]{:S(2)}, u32[]{:S(2)}) %collective-permute-start.37) | collective-permute-done | bytes 524320 | tf_op jit(solution)/shard_map/ppermute | solution.py:122
  415.3 17.9 %reduce-scatter.9.cloned.1.call-done = bf16[256,1024]{1,0:T(8,128)(2,1)} async-done(((bf16[2048,1024]{1,0:T(8,128)(2,1)}), bf16[256,1024]{1,0:T(8,128)(2,1)}) %reduce-scatter.9.cloned.1.call-update) | async-done | bytes 524304 | tf_op jit(solution)/shard_map/reduce_scatter | solution.py:494
  442.7 6.8 %fusion.20 = bf16[8,64,512]{2,1,0:T(8,128)(2,1)} fusion(bf16[512,8,2,64]{0,3,2,1:T(8,128)(2,1)S(1)} %bitcast.208, bf16[8,2,512,512]{2,3,1,0:T(8,128)(2,1)} %copy-done.2), kind=kOutput, calls=%fused_computation.58 | convolution fusion | flops 537133056 | bytes 9961472 | tf_op jit(solution)/shard_map/cuyf,ycul->fcl/dot_general | solution.py:548
  449.5 15.4 %fusion = (f32[8,2,512]{2,1,0:T(2,128)S(1)}, f32[8,512,512,2]{2,1,3,0:T(8,128)}) fusion(f32[8,2,512,512]{2,3,1,0:T(8,128)} %get-tuple-element.156, f32[8,2,512]{2,1,0:T(2,128)S(1)} %bitcast.255, bf16[512,8,64,1]{0,2,3,1:T(8,128)(2,1)S(1)} %bitcast.225, bf16[512,8,2,64]{0,3,2,1:T(8,128)(2,1)S(1)} %bitcast.209), kind=kOutput, calls=%fused_computation.2 | convolution fusion | flops 549445632 | bytes 35192832 | tf_op jit(solution)/shard_map/vuol,mul->uovm/dot_general | solution.py:532
  465.5 11.1 %fusion.2 = bf16[8,2,512,512]{2,3,1,0:T(8,128)(2,1)} fusion(f32[8,512,512,2]{2,1,3,0:T(8,128)} %get-tuple-element.163, f32[8,2,512,512]{2,3,1,0:T(8,128)S(1)} %bitcast.206, f32[8,2,512]{2,1,0:T(2,128)S(1)} %get-tuple-element.162, f32[8,2,512]{2,1,0:T(2,128)S(1)} %bitcast.256), kind=kLoop, calls=%fused_computation.4 | loop fusion | flops 16777216 | bytes 42008576 | tf_op jit(solution)/shard_map/convert_element_type | solution.py:537
  476.7 7.1 %fusion.19 = f32[512,8,64]{0,2,1:T(8,128)} fusion(bf16[8,2,512,512]{2,3,1,0:T(8,128)(2,1)} %fusion.2, bf16[512,8,2,32]{0,3,2,1:T(8,128)(2,1)S(1)} %bitcast.229, bf16[512,8,2,32]{0,3,2,1:T(8,128)(2,1)S(1)} %bitcast.227), kind=kOutput, calls=%fused_computation.57 | convolution fusion | flops 539230208 | bytes 10485760 | tf_op jit(solution)/shard_map/cuyf,ycul->fcl/dot_general | solution.py:545
  510.1 7.7 %fusion.28 = f32[1024,2048]{1,0:T(8,128)} fusion(bf16[512,512]{0,1:T(8,128)(2,1)S(1)} %bitcast.236, bf16[512,512]{0,1:T(8,128)(2,1)} %bitcast.252, bf16[512,1024]{0,1:T(8,128)(2,1)} %bitcast.243, bf16[512,1024]{1,0:T(8,128)(2,1)} %param.14, f32[1024]{0:T(1024)S(1)} %copy-done.60, f32[512]{0:T(512)S(1)} %copy-done.62), kind=kOutput, calls=%fused_computation.89 | convolution fusion | flops 2155872256 | bytes 11540480 | tf_op jit(solution)/shard_map/dot_general | solution.py:61
  517.8 10.1 %concatenate.91 = f32[4,2,128,2176]{3,2,1,0:T(8,128)} concatenate(f32[4,2,128,2048]{3,2,1,0:T(8,128)} %bitcast.210, f32[4,2,128,1]{3,2,1,0:T(8,128)S(1)} %copy.102, f32[4,2,128,127]{3,2,1,0:T(8,128)S(1)} %broadcast_in_dim.144), dimensions={3} | concatenate | bytes 17825792 | tf_op jit(solution)/shard_map/concatenate | solution.py:573
  543.5 6.4 %collective-permute-done.25 = bf16[1,128,1152]{2,1,0:T(8,128)(2,1)S(1)} collective-permute-done((bf16[1,128,1152]{2,1,0:T(8,128)(2,1)S(1)}, bf16[1,128,1152]{2,1,0:T(8,128)(2,1)S(1)}, u32[]{:S(2)}, u32[]{:S(2)}) %collective-permute-start.25) | collective-permute-done | bytes 294944 | tf_op jit(solution)/shard_map/ppermute | solution.py:122
  570.5 6.7 %collective-permute-done.12 = bf16[1,128,2176]{2,1,0:T(8,128)(2,1)S(1)} collective-permute-done((bf16[1,128,2176]{2,1,0:T(8,128)(2,1)S(1)}, bf16[1,128,2176]{2,1,0:T(8,128)(2,1)S(1)}, u32[]{:S(2)}, u32[]{:S(2)}) %collective-permute-start.12) | collective-permute-done | bytes 557088 | tf_op jit(solution)/shard_map/ppermute | solution.py:122
  577.2 8.6 %collective-permute-done.14 = bf16[1,128,2176]{2,1,0:T(8,128)(2,1)S(1)} collective-permute-done((bf16[1,128,2176]{2,1,0:T(8,128)(2,1)S(1)}, bf16[1,128,2176]{2,1,0:T(8,128)(2,1)S(1)}, u32[]{:S(2)}, u32[]{:S(2)}) %collective-permute-start.14) | collective-permute-done | bytes 557088 | tf_op jit(solution)/shard_map/ppermute | solution.py:122
  (350 shorter events, 218.4 us)
Async XLA Ops:
  7.3 113.5 %all-gather.9.cloned.1.call-start = ((), (), s32[]{:S(2)}) async-start(), calls=%async_computation.11 | async-start | bytes 9732096 | tf_op jit(solution)/shard_map/all_gather | solution.py:396
  10.9 175.7 %all-gather.7.cloned.1.call-start = ((), (), s32[]{:S(2)}) async-start(), calls=%async_computation.6 | async-start | bytes 4718592 | tf_op jit(solution)/shard_map/all_gather | solution.py:468
  17.3 24.3 %collective-permute-start.2 = (bf16[128,2176]{1,0:T(8,128)(2,1)S(1)}, bf16[128,2176]{1,0:T(8,128)(2,1)S(1)}, u32[]{:S(2)}, u32[]{:S(2)}) collective-permute-start(bf16[128,2176]{1,0:T(8,128)(2,1)S(1)} %constant_dynamic-slice_fusion.7), channel_id=1, source_target_pairs={{0,3},{1,2},{2,1},{3,0},{4,7},{5,6},{6,5},{7,4},{8,11},{9,10},{10,... | collective-permute-start | bytes 1671176 | tf_op jit(solution)/shard_map/ppermute | solution.py:82
  43.4 22.8 %collective-permute-start.3 = (bf16[4,128,2176]{2,1,0:T(8,128)(2,1)}, bf16[4,128,2176]{2,1,0:T(8,128)(2,1)}, u32[]{:S(2)}, u32[]{:S(2)}) collective-permute-start(bf16[4,128,2176]{2,1,0:T(8,128)(2,1)} %pad_maximum_fusion.2), channel_id=1, source_target_pairs={{0,4},{4,0},{8,12},{12,8},{16,20},{20,16},{24,28},{28,24},{1,5},{5... | collective-permute-start | bytes 6684680 | tf_op jit(solution)/shard_map/ppermute | solution.py:91
  111.6 119.6 %all-gather.5.cloned.1.call-start = ((), (), s32[]{:S(2)}) async-start(), calls=%async_computation.5 | async-start | bytes 4718592 | tf_op jit(solution)/shard_map/all_gather | solution.py:468
  112.3 169.2 %reduce-scatter.5.cloned.1.call-start = ((), (), s32[]{:S(2)}) async-start(), calls=%async_computation.7 | async-start | bytes 4718592 | tf_op jit(solution)/shard_map/reduce_scatter | solution.py:476
  115.0 38.5 %collective-permute-start.10 = (bf16[2,384,1024]{2,1,0:T(8,128)(2,1)}, bf16[2,384,1024]{2,1,0:T(8,128)(2,1)}, u32[]{:S(2)}, u32[]{:S(2)}) collective-permute-start(bf16[2,384,1024]{2,1,0:T(8,128)(2,1)} %pad_maximum_fusion.6.refs_0_), channel_id=1, source_target_pairs={{0,3},{1,2},{2,1},{3,0},{4,7},{5,6},{6,5},{7,4},{8,11},{9,10},{10,... | collective-permute-start | bytes 4718600 | tf_op jit(solution)/shard_map/ppermute | solution.py:82
  117.6 68.7 %collective-permute-start.9 = (bf16[2,384,1024]{2,1,0:T(8,128)(2,1)}, bf16[2,384,1024]{2,1,0:T(8,128)(2,1)}, u32[]{:S(2)}, u32[]{:S(2)}) collective-permute-start(bf16[2,384,1024]{2,1,0:T(8,128)(2,1)} %pad_maximum_fusion.6.refs_0_), channel_id=1, source_target_pairs={{0,2},{1,3},{2,0},{3,1},{4,6},{5,7},{6,4},{7,5},{8,10},{9,11},{10,... | collective-permute-start | bytes 4718600 | tf_op jit(solution)/shard_map/ppermute | solution.py:82
  118.1 68.4 %collective-permute-start.8 = (bf16[2,384,1024]{2,1,0:T(8,128)(2,1)}, bf16[2,384,1024]{2,1,0:T(8,128)(2,1)}, u32[]{:S(2)}, u32[]{:S(2)}) collective-permute-start(bf16[2,384,1024]{2,1,0:T(8,128)(2,1)} %pad_maximum_fusion.6.refs_0_), channel_id=1, source_target_pairs={{0,1},{1,0},{2,3},{3,2},{4,5},{5,4},{6,7},{7,6},{8,9},{9,8},{10,11... | collective-permute-start | bytes 4718600 | tf_op jit(solution)/shard_map/ppermute | solution.py:82
  231.1 179.9 %reduce-scatter.11.cloned.1.call-start = ((), (), s32[]{:S(2)}) async-start(), calls=%async_computation.10 | async-start | bytes 4718592 | tf_op jit(solution)/shard_map/reduce_scatter | solution.py:476
  275.4 139.9 %reduce-scatter.7.cloned.1.call-start = ((), (), s32[]{:S(2)}) async-start(), calls=%async_computation.8 | async-start | bytes 4718592 | tf_op jit(solution)/shard_map/reduce_scatter | solution.py:494
  281.5 151.7 %reduce-scatter.9.cloned.1.call-start = ((), (), s32[]{:S(2)}) async-start(), calls=%async_computation.9 | async-start | bytes 4718592 | tf_op jit(solution)/shard_map/reduce_scatter | solution.py:494
  301.8 46.5 %collective-permute-start.36 = (bf16[2,128,1024]{2,1,0:T(8,128)(2,1)}, bf16[2,128,1024]{2,1,0:T(8,128)(2,1)}, u32[]{:S(2)}, u32[]{:S(2)}) collective-permute-start(bf16[2,128,1024]{2,1,0:T(8,128)(2,1)} %get-tuple-element.121), channel_id=1, source_target_pairs={{0,1},{1,0},{2,3},{3,2},{4,5},{5,4},{6,7},{7,6},{8,9},{9,8},{10,11... | collective-permute-start | bytes 1572872 | tf_op jit(solution)/shard_map/ppermute | solution.py:122
  333.9 72.4 %collective-permute-start.33 = (bf16[2,256,1024]{2,1,0:T(8,128)(2,1)}, bf16[2,256,1024]{2,1,0:T(8,128)(2,1)}, u32[]{:S(2)}, u32[]{:S(2)}) collective-permute-start(bf16[2,256,1024]{2,1,0:T(8,128)(2,1)} %get-tuple-element.111), channel_id=1, source_target_pairs={{0,1},{1,0},{2,3},{3,2},{4,5},{5,4},{6,7},{7,6},{8,9},{9,8},{10,11... | collective-permute-start | bytes 3145736 | tf_op jit(solution)/shard_map/ppermute | solution.py:122
  334.6 71.7 %collective-permute-start.35 = (bf16[2,256,1024]{2,1,0:T(8,128)(2,1)}, bf16[2,256,1024]{2,1,0:T(8,128)(2,1)}, u32[]{:S(2)}, u32[]{:S(2)}) collective-permute-start(bf16[2,256,1024]{2,1,0:T(8,128)(2,1)} %get-tuple-element.112), channel_id=1, source_target_pairs={{0,3},{1,2},{2,1},{3,0},{4,7},{5,6},{6,5},{7,4},{8,11},{9,10},{10,... | collective-permute-start | bytes 3145736 | tf_op jit(solution)/shard_map/ppermute | solution.py:122
  336.9 69.5 %collective-permute-start.34 = (bf16[2,256,1024]{2,1,0:T(8,128)(2,1)}, bf16[2,256,1024]{2,1,0:T(8,128)(2,1)}, u32[]{:S(2)}, u32[]{:S(2)}) collective-permute-start(bf16[2,256,1024]{2,1,0:T(8,128)(2,1)} %get-tuple-element.113), channel_id=1, source_target_pairs={{0,2},{1,3},{2,0},{3,1},{4,6},{5,7},{6,4},{7,5},{8,10},{9,11},{10,... | collective-permute-start | bytes 3145736 | tf_op jit(solution)/shard_map/ppermute | solution.py:122
  341.8 49.4 %collective-permute-start.38 = (bf16[2,128,1024]{2,1,0:T(8,128)(2,1)}, bf16[2,128,1024]{2,1,0:T(8,128)(2,1)}, u32[]{:S(2)}, u32[]{:S(2)}) collective-permute-start(bf16[2,128,1024]{2,1,0:T(8,128)(2,1)} %get-tuple-element.122), channel_id=1, source_target_pairs={{0,3},{1,2},{2,1},{3,0},{4,7},{5,6},{6,5},{7,4},{8,11},{9,10},{10,... | collective-permute-start | bytes 1572872 | tf_op jit(solution)/shard_map/ppermute | solution.py:122
  348.3 55.4 %collective-permute-start.37 = (bf16[2,128,1024]{2,1,0:T(8,128)(2,1)S(1)}, bf16[2,128,1024]{2,1,0:T(8,128)(2,1)S(1)}, u32[]{:S(2)}, u32[]{:S(2)}) collective-permute-start(bf16[2,128,1024]{2,1,0:T(8,128)(2,1)S(1)} %copy-done.44), channel_id=1, source_target_pairs={{0,2},{1,3},{2,0},{3,1},{4,6},{5,7},{6,4},{7,5},{8,10},{9,11},{10,... | collective-permute-start | bytes 1572872 | tf_op jit(solution)/shard_map/ppermute | solution.py:122
  500.0 31.1 %collective-permute-start.22 = (bf16[4,128,1152]{2,1,0:T(8,128)(2,1)}, bf16[4,128,1152]{2,1,0:T(8,128)(2,1)}, u32[]{:S(2)}, u32[]{:S(2)}) collective-permute-start(bf16[4,128,1152]{2,1,0:T(8,128)(2,1)} %fusion.21), channel_id=1, source_target_pairs={{0,4},{4,0},{8,12},{12,8},{16,20},{20,16},{24,28},{28,24},{1,5},{5... | collective-permute-start | bytes 3538952 | tf_op jit(solution)/shard_map/ppermute | solution.py:91
  530.5 30.5 %collective-permute-start.11 = (bf16[4,128,2176]{2,1,0:T(8,128)(2,1)S(1)}, bf16[4,128,2176]{2,1,0:T(8,128)(2,1)S(1)}, u32[]{:S(2)}, u32[]{:S(2)}) collective-permute-start(bf16[4,128,2176]{2,1,0:T(8,128)(2,1)S(1)} %fusion.8), channel_id=1, source_target_pairs={{0,4},{4,0},{8,12},{12,8},{16,20},{20,16},{24,28},{28,24},{1,5},{5... | collective-permute-start | bytes 6684680 | tf_op jit(solution)/shard_map/ppermute | solution.py:91
  563.1 22.8 %collective-permute-start.14 = (bf16[1,128,2176]{2,1,0:T(8,128)(2,1)S(1)}, bf16[1,128,2176]{2,1,0:T(8,128)(2,1)S(1)}, u32[]{:S(2)}, u32[]{:S(2)}) collective-permute-start(bf16[1,128,2176]{2,1,0:T(8,128)(2,1)S(1)} %get-tuple-element.103), channel_id=1, source_target_pairs={{0,3},{1,2},{2,1},{3,0},{4,7},{5,6},{6,5},{7,4},{8,11},{9,10},{10,... | collective-permute-start | bytes 1671176 | tf_op jit(solution)/shard_map/ppermute | solution.py:122
  563.6 23.6 %collective-permute-start.13 = (bf16[1,128,2176]{2,1,0:T(8,128)(2,1)S(1)}, bf16[1,128,2176]{2,1,0:T(8,128)(2,1)S(1)}, u32[]{:S(2)}, u32[]{:S(2)}) collective-permute-start(bf16[1,128,2176]{2,1,0:T(8,128)(2,1)S(1)} %get-tuple-element.104), channel_id=1, source_target_pairs={{0,2},{1,3},{2,0},{3,1},{4,6},{5,7},{6,4},{7,5},{8,10},{9,11},{10,... | collective-permute-start | bytes 1671176 | tf_op jit(solution)/shard_map/ppermute | solution.py:122
  566.7 24.9 %collective-permute-start.30 = (bf16[32,1152]{1,0:T(8,128)(2,1)S(1)}, bf16[32,1152]{1,0:T(8,128)(2,1)S(1)}, u32[]{:S(2)}, u32[]{:S(2)}) collective-permute-start(bf16[32,1152]{1,0:T(8,128)(2,1)S(1)} %get-tuple-element.99), channel_id=1, source_target_pairs={{0,16},{4,20},{8,24},{12,28},{16,0},{20,4},{24,8},{28,12},{1,17},{... | collective-permute-start | bytes 221192 | tf_op jit(solution)/shard_map/ppermute | solution.py:150
  568.1 31.9 %collective-permute-start.31 = (bf16[32,1152]{1,0:T(8,128)(2,1)S(1)}, bf16[32,1152]{1,0:T(8,128)(2,1)S(1)}, u32[]{:S(2)}, u32[]{:S(2)}) collective-permute-start(bf16[32,1152]{1,0:T(8,128)(2,1)S(1)} %get-tuple-element.99), channel_id=1, source_target_pairs={{0,24},{4,28},{8,0},{12,4},{16,8},{20,12},{24,16},{28,20},{1,25},{... | collective-permute-start | bytes 221192 | tf_op jit(solution)/shard_map/ppermute | solution.py:150
  (94 other events, 758.8 us)
Sparse Core Ops, SparseCore 0:
  11.0 86.9 all-gather.8
  111.7 48.6 all-gather.6
  162.6 45.6 all-gather.4
  231.2 50.2 reduce-scatter.4
  283.6 48.1 reduce-scatter.10
  334.0 48.6 reduce-scatter.6
  385.0 48.1 reduce-scatter.8

commit v3 on v2

--- a/solution.py
+++ b/solution.py
@@ -14,43 +14,9 @@
 LANES = 128
 VMEM_LIMIT = 58 * 1024 * 1024
 CHUNKS = 2
+SMALL_COST = pl.CostEstimate(flops=0, bytes_accessed=0, transcendentals=0)
 F32 = jnp.float32
 BF16 = jnp.bfloat16
-
-
-def normalize(values, gain_vector):
-    return (
-        values * lax.rsqrt(jnp.mean(values * values, axis=-1, keepdims=True) + 1e-06) * gain_vector
-    )
-
-
-def apply_rotary(values, cosine_table, sine_lookup):
-    half_width = values.shape[-1] // 2
-    first_half = values[..., :half_width]
-    second_half = values[..., half_width:]
-    return jnp.concatenate(
-        [
-            first_half * cosine_table - second_half * sine_lookup,
-            second_half * cosine_table + first_half * sine_lookup,
-        ],
-        axis=-1,
-    )
-
-
-def place_tables(lengths_row, total_rows, head_width):
-    doc_ends = jnp.cumsum(lengths_row)
-    token_index = jnp.arange(total_rows, dtype=jnp.int32)
-    past_end = token_index[:, None] >= doc_ends[None, :]
-    document = jnp.sum(past_end.astype(jnp.int32), axis=1)
-    doc_start = jnp.sum(jnp.where(past_end, lengths_row[None, :], 0), axis=1)
-    position = (token_index - doc_start).astype(jnp.float32)
-    half_width = head_width // 2
-    inverse = 10000.0 ** (-(jnp.arange(half_width, dtype=jnp.float32) * 2.0 / head_width))
-    angles = position[:, None] * inverse[None, :]
-    allowed = (document[:, None] == document[None, :]) & (
-        token_index[None, :] <= token_index[:, None]
-    )
-    return (jnp.cos(angles)[:, None, :], jnp.sin(angles)[:, None, :], allowed)
 
 
 def matrix_product(left_side, right_side):
@@ -91,24 +57,25 @@
     return lax.ppermute(value, "expert", [(i, i ^ 1) for i in range(size)])
 
 
-def gather_rows(rows):
+def fetch_rows(rows):
+    count = lax.axis_size("shard")
+    size = rows.shape[0]
+    if count != 4:
+        return [lax.all_gather(rows, "shard", axis=0, tiled=True)], jnp.zeros((1,), jnp.int32)
+    me = lax.axis_index("shard")
     core = lax.axis_index("expert") % 2
-    half = rows.shape[0] // 2
+    half = size // 2
     mine = lax.dynamic_slice_in_dim(rows, core * half, half, 0)
-    pieces = gather_pieces(mine)
-    count = len(pieces)
-    kept = jnp.stack([piece for piece, _ in pieces])
-    other = swap_cores(kept)
-    low = jnp.where(core == 0, kept, other)
-    high = jnp.where(core == 0, other, kept)
-    both = jnp.stack([low, high], axis=1).reshape(count, rows.shape[0], rows.shape[1])
-    me = lax.axis_index("shard")
-    if count == 4:
-        both = jnp.concatenate([pick(both, me ^ i) for i in range(4)], axis=0)
-    return both.reshape(count * rows.shape[0], rows.shape[1])
-
-
-def scatter_sum(values, axis):
+    pieces, places = [rows], [me * size]
+    for flip in (1, 2, 3):
+        got = lax.ppermute(mine, "shard", [(i, i ^ flip) for i in range(4)])
+        first = (me ^ flip) * size
+        pieces += [got, swap_cores(got)]
+        places += [first + core * half, first + (1 - core) * half]
+    return pieces, jnp.stack(places).astype(jnp.int32)
+
+
+def scatter_sum(values, axis, after=None):
     count = lax.axis_size("shard")
     if count != 4:
         return lax.psum_scatter(
@@ -116,7 +83,10 @@
         ).astype(F32)
     me = lax.axis_index("shard")
     size = values.shape[axis] // count
-    total = lax.dynamic_slice_in_dim(values, me * size, size, axis).astype(F32)
+    own = lax.dynamic_slice_in_dim(values, me * size, size, axis)
+    if after is not None:
+        own, _ = lax.optimization_barrier((own, after))
+    total = own.astype(F32)
     for flip in (1, 2, 3):
         sent = lax.dynamic_slice_in_dim(values, (me ^ flip) * size, size, axis).astype(BF16)
         got = lax.ppermute(sent, "shard", [(i, i ^ flip) for i in range(4)])
@@ -135,7 +105,7 @@
     blocks = grad.reshape(count, 2, half, width)
     mine = lax.dynamic_index_in_dim(blocks, core, 1, keepdims=False)
     away = lax.dynamic_index_in_dim(blocks, 1 - core, 1, keepdims=False)
-    paired = mine + swap_cores(away.astype(BF16)).astype(F32)
+    paired = mine.astype(F32) + swap_cores(away).astype(F32)
     local = scatter_sum(paired, 0).reshape(layers, half // layers, width)
     total = pick(local, layer)
     for step in range(1, layers):
@@ -338,6 +308,349 @@
     )(*acts, *([every_dy] * chunks)).reshape(local, width // local, width)
 
 
+def row_copies(place_ref, pieces, target, sem):
+    copies = []
+    for i, piece in enumerate(pieces):
+        rows = piece.shape[0]
+        first = pl.multiple_of(place_ref[i], 16)
+        copies.append(
+            pltpu.make_async_copy(piece, target.at[pl.ds(first, rows), :], sem.at[i])
+        )
+    for copy in copies:
+        copy.start()
+    return copies
+
+
+def scale_of(values):
+    return lax.rsqrt(jnp.mean(values * values, axis=-1, keepdims=True) + 1e-06)
+
+
+def rotate(values, cosine, sine):
+    lane = lax.broadcasted_iota(jnp.int32, values.shape, 1) % HEAD_DIM
+    half = HEAD_DIM // 2
+    turned = jnp.where(
+        lane < half, pltpu.roll(values, LANES - half, 1), pltpu.roll(values, half, 1)
+    )
+    return values * cosine + turned * sine
+
+
+def project_kernel(count, experts, place_ref, x_ref, cos_ref, sin_ref, *refs):
+    pieces = refs[:count]
+    normed_ref, q_ref, k_ref, v_ref, gains_ref, router_ref, weight, sem = refs[count:]
+    copies = row_copies(place_ref, pieces, weight, sem)
+    x = x_ref[...].astype(F32)
+    scaled = x * scale_of(x)
+    cosine, sine = cos_ref[...], sin_ref[...]
+    for copy in copies:
+        copy.wait()
+    q_width, kv_width = q_ref.shape[1], k_ref.shape[1]
+    small = weight[:, q_width + 2 * kv_width :]
+    lane = lax.broadcasted_iota(jnp.int32, small.shape, 1)
+    router_ref[...] = jnp.where(lane < experts, small.astype(F32), 0.0).astype(BF16)
+    turned = small.astype(F32).T
+    gains_ref[...] = jnp.concatenate(
+        [turned[experts : experts + 2], jnp.zeros((6, turned.shape[1]), F32)], axis=0
+    )
+    normed = (scaled * turned[experts : experts + 1]).astype(BF16)
+    normed_ref[...] = normed
+    for first in range(0, q_width, 256):
+        values = jnp.dot(normed, weight[:, first : first + 256], preferred_element_type=F32)
+        for part in (0, LANES):
+            q_ref[:, first + part : first + part + LANES] = rotate(
+                values[:, part : part + LANES], cosine, sine
+            ).astype(BF16)
+    for first in range(0, kv_width, 256):
+        at = q_width + first
+        values = jnp.dot(normed, weight[:, at : at + 256], preferred_element_type=F32)
+        for part in (0, LANES):
+            k_ref[:, first + part : first + part + LANES] = rotate(
+                values[:, part : part + LANES], cosine, sine
+            ).astype(BF16)
+    at = q_width + kv_width
+    v_ref[...] = jnp.dot(
+        normed, weight[:, at : at + kv_width], preferred_element_type=F32
+    ).astype(BF16)
+
+
+def simple_call(kernel, name, prefetch, inputs, pieces, outputs, scratch, cost=None):
+    def whole(shape):
+        return pl.BlockSpec(shape, lambda i, p: (0,) * len(shape))
+
+    return pl.pallas_call(
+        kernel,
+        grid_spec=pltpu.PrefetchScalarGridSpec(
+            num_scalar_prefetch=1,
+            grid=(1,),
+            in_specs=[whole(value.shape) for value in inputs]
+            + [pl.BlockSpec(memory_space=pl.ANY)] * len(pieces),
+            out_specs=[whole(shape) for shape, _ in outputs],
+            scratch_shapes=scratch,
+        ),
+        out_shape=[jax.ShapeDtypeStruct(shape, kind) for shape, kind in outputs],
+        compiler_params=pltpu.CompilerParams(vmem_limit_bytes=VMEM_LIMIT),
+        cost_estimate=cost,
+        name=name,
+    )(prefetch, *inputs, *pieces)
+
+
+def key_window(tile, size, rows):
+    low = max(0, tile * size - (rows // 2 - 1)) // size * size
+    return low, (tile + 1) * size
+
+
+def tile_mask(start_ref, low, high, first, size):
+    shape = (high - low, size)
+    key = lax.broadcasted_iota(jnp.int32, shape, 0) + low
+    query = lax.broadcasted_iota(jnp.int32, shape, 1) + first
+    seen = (key >= start_ref[:, first : first + size]) & (key <= query)
+    return jnp.concatenate([seen, seen], axis=1)
+
+
+def two_heads(values):
+    return jnp.concatenate([values[:, :HEAD_DIM], values[:, HEAD_DIM:]], axis=0)
+
+
+def untwo(values):
+    size = values.shape[1] // 2
+    return jnp.concatenate([values[:, :size], values[:, size:]], axis=0).T
+
+
+def attend_kernel(start_ref, q_ref, k_ref, v_ref, out_ref, log_ref):
+    rows = q_ref.shape[0]
+    size = LANES
+    scale = 1.0 / math.sqrt(HEAD_DIM)
+    logs = [[], []]
+    for tile in range(rows // size):
+        low, high = key_window(tile, size, rows)
+        first = tile * size
+        seen = tile_mask(start_ref, low, high, first, size)
+        for pair in range(2):
+            q = two_heads(q_ref[first : first + size, pair * LANES : (pair + 1) * LANES])
+            q = (q.astype(F32) * scale).astype(BF16)
+            at = pair * HEAD_DIM
+            scores = product_transposed_right(k_ref[low:high, at : at + HEAD_DIM], q)
+            scores = jnp.where(seen, scores, -1e30)
+            top = jnp.max(scores, axis=0, keepdims=True)
+            powers = jnp.exp(scores - top)
+            total = jnp.sum(powers, axis=0, keepdims=True)
+            low_chances = (powers * (1.0 / total)).astype(BF16)
+            mixed = product_tn(v_ref[low:high, at : at + HEAD_DIM], low_chances)
+            out_ref[first : first + size, pair * LANES : (pair + 1) * LANES] = untwo(mixed).astype(
+                BF16
+            )
+            logs[pair].append(top + jnp.log(total))
+    lines = []
+    for pair in range(2):
+        for head in range(2):
+            lines.append(
+                jnp.concatenate([v[:, head * size : (head + 1) * size] for v in logs[pair]], axis=1)
+            )
+    log_ref[...] = jnp.concatenate(lines + [jnp.zeros((4, rows), F32)], axis=0)
+
+
+def attend_back_kernel(
+    start_ref, q_ref, k_ref, v_ref, grad_ref, log_ref, cos_ref, sin_ref, qb_ref, kb_ref, vb_ref
+):
+    rows = q_ref.shape[0]
+    size = LANES
+    tiles = rows // size
+    scale = 1.0 / math.sqrt(HEAD_DIM)
+    key_sums = [[None] * tiles, [None] * tiles]
+    value_sums = [[None] * tiles, [None] * tiles]
+
+    def add(sums, low, part):
+        for i in range(part.shape[0] // size):
+            piece = part[i * size : (i + 1) * size]
+            at = low // size + i
+            sums[at] = piece if sums[at] is None else sums[at] + piece
+
+    for tile in range(tiles):
+        low, high = key_window(tile, size, rows)
+        first = tile * size
+        seen = tile_mask(start_ref, low, high, first, size)
+        cosine, sine = cos_ref[first : first + size], sin_ref[first : first + size]
+        for pair in range(2):
+            lanes = slice(pair * LANES, (pair + 1) * LANES)
+            q = two_heads(q_ref[first : first + size, lanes])
+            q = (q.astype(F32) * scale).astype(BF16)
+            grad = two_heads(grad_ref[first : first + size, lanes])
+            at = pair * HEAD_DIM
+            keys = k_ref[low:high, at : at + HEAD_DIM]
+            scores = jnp.where(seen, product_transposed_right(keys, q), -1e30)
+            log_total = jnp.concatenate(
+                [
+                    log_ref[2 * pair : 2 * pair + 1, first : first + size],
+                    log_ref[2 * pair + 1 : 2 * pair + 2, first : first + size],
+                ],
+                axis=1,
+            )
+            chances = jnp.exp(scores - log_total)
+            chance_grad = product_transposed_right(v_ref[low:high, at : at + HEAD_DIM], grad)
+            mean = jnp.sum(chances * chance_grad, axis=0, keepdims=True)
+            score_grad = (chances * (chance_grad - mean)).astype(BF16)
+            add(value_sums[pair], low, jnp.dot(chances.astype(BF16), grad, preferred_element_type=F32))
+            add(key_sums[pair], low, jnp.dot(score_grad, q, preferred_element_type=F32))
+            query_grad = untwo(product_tn(keys, score_grad)) * scale
+            qb_ref[first : first + size, lanes] = rotate(query_grad, cosine, -sine).astype(BF16)
+    for tile in range(tiles):
+        here = slice(tile * size, (tile + 1) * size)
+        both = jnp.concatenate([key_sums[0][tile], key_sums[1][tile]], axis=1)
+        kb_ref[here, :] = rotate(both, cos_ref[here], -sin_ref[here]).astype(BF16)
+        both = jnp.concatenate([value_sums[0][tile], value_sums[1][tile]], axis=1)
+        vb_ref[here, :] = both.astype(BF16)
+
+
+def attention_specs(rows):
+    return (
+        pl.BlockSpec((1, rows), lambda i: (0, 0)),
+        pl.BlockSpec((rows, 2 * LANES), lambda i: (0, i)),
+        pl.BlockSpec((rows, LANES), lambda i: (0, i)),
+        pl.BlockSpec((8, rows), lambda i: (i, 0)),
+        pl.BlockSpec((rows, LANES), lambda i: (0, 0)),
+    )
+
+
+def attend(start, q, k, v):
+    rows = q.shape[0]
+    one, wide, thin, line, _ = attention_specs(rows)
+    steps = k.shape[1] // LANES
+    return pl.pallas_call(
+        attend_kernel,
+        grid=(steps,),
+        in_specs=[one, wide, thin, thin],
+        out_specs=[wide, line],
+        out_shape=[
+            jax.ShapeDtypeStruct(q.shape, BF16),
+            jax.ShapeDtypeStruct((8 * steps, rows), F32),
+        ],
+        compiler_params=pltpu.CompilerParams(vmem_limit_bytes=VMEM_LIMIT),
+        cost_estimate=SMALL_COST,
+        name="attend",
+    )(start, q, k, v)
+
+
+def attend_back(start, q, k, v, grad, logs, cosine, sine):
+    rows = q.shape[0]
+    one, wide, thin, line, table = attention_specs(rows)
+    return pl.pallas_call(
+        attend_back_kernel,
+        grid=(k.shape[1] // LANES,),
+        in_specs=[one, wide, thin, thin, wide, line, table, table],
+        out_specs=[wide, thin, thin],
+        out_shape=[
+            jax.ShapeDtypeStruct(q.shape, BF16),
+            jax.ShapeDtypeStruct(k.shape, BF16),
+            jax.ShapeDtypeStruct(v.shape, BF16),
+        ],
+        compiler_params=pltpu.CompilerParams(vmem_limit_bytes=VMEM_LIMIT),
+        name="attend_back",
+    )(start, q, k, v, grad, logs, cosine, sine)
+
+
+def mix_kernel(count, place_ref, attended_ref, x_ref, mask_ref, router_ref, gains_ref, *refs):
+    pieces = refs[:count]
+    state_ref, mixed_ref, gates_ref, weight, sem = refs[count:]
+    copies = row_copies(place_ref, pieces, weight, sem)
+    for copy in copies:
+        copy.wait()
+    state = x_ref[...].astype(F32) + jnp.dot(
+        attended_ref[...], weight[...], preferred_element_type=F32
+    )
+    state_ref[...] = state
+    mixed = (state * scale_of(state) * gains_ref[1:2, :]).astype(BF16)
+    mixed_ref[...] = mixed
+    logits = jnp.dot(mixed, router_ref[...], preferred_element_type=F32)
+    logits = jnp.where(mask_ref[...] > 0, logits, -1e30)
+    powers = jnp.exp(logits - jnp.max(logits, axis=1, keepdims=True))
+    gates_ref[...] = powers / jnp.sum(powers, axis=1, keepdims=True)
+
+
+def mix_back_kernel(
+    count,
+    chunks,
+    experts,
+    place_ref,
+    attended_ref,
+    state_ref,
+    mixed_ref,
+    dy_ref,
+    gates_ref,
+    gate_grad_ref,
+    router_ref,
+    gains_ref,
+    *refs,
+):
+    sums = refs[:chunks]
+    pieces = refs[chunks : chunks + count]
+    state_grad_ref, attended_grad_ref, pack_ref, weight, sem = refs[chunks + count :]
+    copies = row_copies(place_ref, pieces, weight, sem)
+    gates = gates_ref[...]
+    gate_grad = gate_grad_ref[...]
+    logit_grad = (
+        gates * (gate_grad - jnp.sum(gates * gate_grad, axis=1, keepdims=True))
+    ).astype(BF16)
+    rows = jnp.concatenate([part[...] for part in sums], axis=0).astype(F32)
+    mixed_grad = product_transposed_right(logit_grad, router_ref[...]) + rows
+    state = state_ref[...]
+    scale = scale_of(state)
+    gain_grad = jnp.sum(mixed_grad * (state * scale), axis=0, keepdims=True)
+    scaled = gains_ref[1:2, :] * mixed_grad
+    mean = jnp.mean(scaled * state, axis=1, keepdims=True)
+    state_grad = dy_ref[...].astype(F32) + scale * scaled - state * (scale * scale * scale * mean)
+    state_grad_ref[...] = state_grad
+    branch = state_grad.astype(BF16)
+    for copy in copies:
+        copy.wait()
+    attended_grad_ref[...] = product_transposed_right(branch, weight[...]).astype(BF16)
+    width = state.shape[1]
+    pack_ref[:, :width] = product_tn(attended_ref[...], branch).astype(BF16)
+    line = lax.broadcasted_iota(jnp.int32, (LANES, width), 0)
+    column = jnp.where(line == experts, gain_grad, 0.0).T
+    pack_ref[:, width:] = (product_tn(mixed_ref[...], logit_grad) + column).astype(BF16)
+
+
+def project_back_kernel(
+    count,
+    place_ref,
+    normed_ref,
+    x_ref,
+    state_grad_ref,
+    gains_ref,
+    qb_ref,
+    kb_ref,
+    vb_ref,
+    *refs,
+):
+    pieces = refs[:count]
+    out_ref, pack_ref, weight, sem = refs[count:]
+    copies = row_copies(place_ref, pieces, weight, sem)
+    normed = normed_ref[...]
+    at = 0
+    for back_ref in (qb_ref, kb_ref, vb_ref):
+        width = back_ref.shape[1]
+        pack_ref[:, at : at + width] = product_tn(normed, back_ref[...]).astype(BF16)
+        at += width
+    for copy in copies:
+        copy.wait()
+    grad = None
+    first = 0
+    for back_ref in (qb_ref, kb_ref, vb_ref):
+        width = back_ref.shape[1]
+        part = product_transposed_right(back_ref[...], weight[:, first : first + width])
+        grad = part if grad is None else grad + part
+        first += width
+    x = x_ref[...].astype(F32)
+    scale = scale_of(x)
+    gain_grad = jnp.sum(grad * (x * scale), axis=0, keepdims=True)
+    scaled = gains_ref[0:1, :] * grad
+    mean = jnp.mean(scaled * x, axis=1, keepdims=True)
+    out_ref[...] = (
+        state_grad_ref[...] + scale * scaled - x * (scale * scale * scale * mean)
+    ).astype(BF16)
+    line = lax.broadcasted_iota(jnp.int32, (LANES, x.shape[1]), 0)
+    pack_ref[:, at:] = jnp.where(line == 0, gain_grad, 0.0).T.astype(BF16)
+
+
 def per_device(
     tokens,
     gain_attn,
@@ -355,14 +668,12 @@
     cotangent,
 ):
     total_rows, model_width = tokens.shape
-    query_group_width = QUERY_HEADS // KEY_VALUE_HEADS
     experts = router.shape[1]
     local_experts, _, hidden = w_gate.shape
     peers = lax.axis_size("expert")
-    count = lax.axis_size("shard")
-    part_rows = w_query.shape[0]
+    part_rows, q_width = w_query.shape
     kv_width = key_weight.shape[1]
-    score_scale = 1.0 / math.sqrt(HEAD_DIM)
+    first_width = q_width + 2 * kv_width + LANES
 
     small = jnp.concatenate(
         [
@@ -373,19 +684,10 @@
         ],
         axis=1,
     )
-    first_weights = gather_rows(
+    first_pieces, first_places = fetch_rows(
         jnp.concatenate([w_query, key_weight, value_weight, small], axis=1)
     )
-    q_end = w_query.shape[1]
-    query_w = first_weights[:, :q_end]
-    key_matrix = first_weights[:, q_end : q_end + kv_width]
-    value_matrix = first_weights[:, q_end + kv_width : q_end + 2 * kv_width]
-    small_all = first_weights[:, q_end + 2 * kv_width :]
-    gain_first = small_all[:, experts].astype(F32)
-    gain_second = small_all[:, experts + 1].astype(F32)
-    router_lanes = jnp.where(jnp.arange(LANES)[None, :] < experts, small_all, jnp.zeros((), BF16))
-    router_w = small_all[:, :experts]
-    output_matrix = gather_rows(w_out)
+    out_pieces, out_places = fetch_rows(w_out)
     packed = jnp.concatenate([jnp.concatenate([w_gate, w_up], axis=2), w_down], axis=1)
     pieces = gather_pieces(packed)
 
@@ -412,55 +714,55 @@
         ((0, 0), (0, 0), (0, LANES - experts)),
     )
 
-    inputs = tokens.astype(jnp.float32)
-    normalized_input = normalize(inputs, gain_first).astype(jnp.bfloat16)
-    cosine_table, sine_lookup, allowed = place_tables(lengths[0], total_rows, HEAD_DIM)
-    query_raw = matrix_product(normalized_input, query_w).reshape(total_rows, QUERY_HEADS, HEAD_DIM)
-    unrotated_keys = matrix_product(normalized_input, key_matrix).reshape(
-        total_rows, KEY_VALUE_HEADS, HEAD_DIM
-    )
-    query_rows = (
-        apply_rotary(query_raw, cosine_table, sine_lookup)
-        .astype(jnp.bfloat16)
-        .reshape(total_rows, KEY_VALUE_HEADS, query_group_width, HEAD_DIM)
-    )
-    key_matrix_rows = apply_rotary(unrotated_keys, cosine_table, sine_lookup).astype(jnp.bfloat16)
-    value_matrix_rows = (
-        matrix_product(normalized_input, value_matrix)
-        .astype(jnp.bfloat16)
-        .reshape(total_rows, KEY_VALUE_HEADS, HEAD_DIM)
-    )
-
-    def score_table():
-        raw_scores = (
-            jnp.einsum(
-                "vuol,mul->uovm", query_rows, key_matrix_rows, preferred_element_type=jnp.float32
-            )
-            * score_scale
-        )
-        return jnp.where(allowed[None, None], raw_scores, -1e30)
-
-    scores = score_table()
-    top_score = jnp.max(scores, axis=-1, keepdims=True)
-    weights = jnp.exp(scores - top_score)
-    sum_weights = jnp.sum(weights, axis=-1, keepdims=True)
-    probability = weights / sum_weights
-    log_total = top_score + jnp.log(sum_weights)
-    lower_probabilities = probability.astype(jnp.bfloat16)
-    attended = (
-        jnp.einsum(
-            "yjvu,uyw->vyjw",
-            lower_probabilities,
-            value_matrix_rows,
-            preferred_element_type=jnp.float32,
-        )
-        .astype(jnp.bfloat16)
-        .reshape(total_rows, QUERY_HEADS * HEAD_DIM)
-    )
-    hidden_state = inputs + matrix_product(attended, output_matrix)
-    mixed_in = normalize(hidden_state, gain_second).astype(jnp.bfloat16)
-    logits = matrix_product(mixed_in, router_w)
-    gates = jax.nn.softmax(jnp.where(chosen, logits, -1e30), axis=-1)
+    own_mask = jnp.pad(chosen.astype(BF16), ((0, 0), (0, LANES - experts)))
+
+    doc_ends = jnp.cumsum(lengths[0])
+    token_index = jnp.arange(total_rows, dtype=jnp.int32)
+    past_end = token_index[:, None] >= doc_ends[None, :]
+    doc_start = jnp.sum(jnp.where(past_end, lengths[0][None, :], 0), axis=1)
+    position = (token_index - doc_start).astype(F32)
+    half_head = HEAD_DIM // 2
+    inverse = 10000.0 ** (-(jnp.arange(half_head, dtype=F32) * 2.0 / HEAD_DIM))
+    angles = position[:, None] * inverse[None, :]
+    cosine, sine = jnp.cos(angles), jnp.sin(angles)
+    cosine = jnp.concatenate([cosine] * (LANES // half_head), axis=1)
+    sine = jnp.concatenate([-sine, sine] * (LANES // HEAD_DIM), axis=1)
+    start = doc_start[None, :].astype(jnp.int32)
+
+    normed, q, k, v, gains, router_lanes = simple_call(
+        functools.partial(project_kernel, len(first_pieces), experts),
+        "project",
+        first_places,
+        [tokens, cosine, sine],
+        first_pieces,
+        [
+            (tokens.shape, BF16),
+            ((total_rows, q_width), BF16),
+            ((total_rows, kv_width), BF16),
+            ((total_rows, kv_width), BF16),
+            ((8, model_width), F32),
+            ((model_width, LANES), BF16),
+        ],
+        [
+            pltpu.VMEM((model_width, first_width), BF16),
+            pltpu.SemaphoreType.DMA((len(first_pieces),)),
+        ],
+        SMALL_COST,
+    )
+    attended, logs = attend(start, q, k, v)
+    state, mixed_in, gates = simple_call(
+        functools.partial(mix_kernel, len(out_pieces)),
+        "mix",
+        out_places,
+        [attended, tokens, own_mask, router_lanes, gains],
+        out_pieces,
+        [(tokens.shape, F32), (tokens.shape, BF16), ((total_rows, LANES), F32)],
+        [
+            pltpu.VMEM((q_width, model_width), BF16),
+            pltpu.SemaphoreType.DMA((len(out_pieces),)),
+        ],
+        SMALL_COST,
+    )
 
     part = total_rows // CHUNKS
     every_x, out_part, row_part, act, gate_back, up_back, scores_part = [], [], [], [], [], [], []
@@ -489,94 +791,65 @@
         .reshape(total_rows, experts)
     )
     *out_part, row_last = lax.optimization_barrier((*out_part, row_sum[-1]))
-    row_sum = jnp.concatenate([*row_sum[:-1], row_last], axis=0)
-    out_sum = jnp.concatenate(
-        [lax.psum_scatter(rows, "expert", scatter_dimension=0, tiled=True) for rows in out_part],
-        axis=0,
-    )
-    output = hidden_state + out_sum.astype(F32)
-    upstream = cotangent.astype(jnp.float32)
-
-    expert_down_sum = scatter_sum(down_gradient(act, every_dy, local_experts), 1)
-    gu_sum = scatter_sum(gate_up_gradient(every_x, gate_back, up_back, local_experts), 1)
+    row_sum[-1] = row_last
+    out_sum = [lax.psum_scatter(rows, "expert", scatter_dimension=0, tiled=True) for rows in out_part]
+
+    down_grad = down_gradient(act, every_dy, local_experts)
+    gu_grad = gate_up_gradient(every_x, gate_back, up_back, local_experts)
+
+    state_grad, attended_grad, pack = simple_call(
+        functools.partial(mix_back_kernel, len(out_pieces), CHUNKS, experts),
+        "mix_back",
+        out_places,
+        [
+            attended,
+            state,
+            mixed_in,
+            cotangent,
+            gates,
+            jnp.pad(gate_grad, ((0, 0), (0, LANES - experts))),
+            router_lanes,
+            gains,
+            *row_sum,
+        ],
+        out_pieces,
+        [
+            (tokens.shape, F32),
+            ((total_rows, q_width), BF16),
+            ((q_width, model_width + LANES), BF16),
+        ],
+        [
+            pltpu.VMEM((q_width, model_width), BF16),
+            pltpu.SemaphoreType.DMA((len(out_pieces),)),
+        ],
+    )
+    early = sum_everywhere(pack)
+    query_back, key_back, value_back = attend_back(
+        start, q, k, v, attended_grad, logs, cosine, sine
+    )
+    input_grad, late_pack = simple_call(
+        functools.partial(project_back_kernel, len(first_pieces)),
+        "project_back",
+        first_places,
+        [normed, tokens, state_grad, gains, query_back, key_back, value_back],
+        first_pieces,
+        [(tokens.shape, BF16), ((model_width, first_width), BF16)],
+        [
+            pltpu.VMEM((model_width, first_width), BF16),
+            pltpu.SemaphoreType.DMA((len(first_pieces),)),
+        ],
+    )
+    expert_down_sum = scatter_sum(down_grad, 1, value_back)
+    gu_sum = scatter_sum(gu_grad, 1, value_back)
     expert_gate_sum = gu_sum[:, :, :hidden]
     expert_up_sum = gu_sum[:, :, hidden:]
-
-    logit_grad = (
-        gates * (gate_grad - jnp.sum(gates * gate_grad, axis=1, keepdims=True))
-    ).astype(jnp.bfloat16)
-    router_grad = product_tn(mixed_in, logit_grad)
-    mixed_grad = product_transposed_right(logit_grad, router_w) + row_sum.astype(F32)
-    _, second_back = jax.vjp(normalize, hidden_state, gain_second)
-    state_part, gain_two_grad = second_back(mixed_grad)
-    state_grad = upstream + state_part
-    branch_gradient = state_grad.astype(jnp.bfloat16)
-    out_grad_w = product_tn(attended, branch_gradient)
-    early = sum_everywhere(
-        jnp.concatenate(
-            [
-                out_grad_w,
-                router_grad,
-                gain_two_grad[:, None],
-                jnp.zeros((model_width, LANES - experts - 1), F32),
-            ],
-            axis=1,
-        )
-    )
-    attended_gradient = (
-        product_transposed_right(branch_gradient, output_matrix)
-        .astype(jnp.bfloat16)
-        .reshape(total_rows, KEY_VALUE_HEADS, query_group_width, HEAD_DIM)
-    )
-    probability = jnp.exp(score_table() - log_total)
-    prob_grad = jnp.einsum(
-        "vuol,mul->uovm", attended_gradient, value_matrix_rows, preferred_element_type=jnp.float32
-    )
-    score_gradient = (
-        probability * (prob_grad - jnp.sum(probability * prob_grad, axis=-1, keepdims=True))
-    ).astype(jnp.bfloat16)
-    query_grad = (
-        jnp.einsum(
-            "yjvu,uyw->vyjw", score_gradient, key_matrix_rows, preferred_element_type=jnp.float32
-        )
-        * score_scale
-    )
-    key_gradient = (
-        jnp.einsum("cuyf,ycul->fcl", score_gradient, query_rows, preferred_element_type=jnp.float32)
-        * score_scale
-    )
-    value_gradient = jnp.einsum(
-        "cuyf,ycul->fcl", lower_probabilities, attended_gradient, preferred_element_type=jnp.float32
-    )
-    query_back = (
-        apply_rotary(
-            query_grad.reshape(total_rows, QUERY_HEADS, HEAD_DIM), cosine_table, -sine_lookup
-        )
-        .astype(jnp.bfloat16)
-        .reshape(total_rows, QUERY_HEADS * HEAD_DIM)
-    )
-    key_back = (
-        apply_rotary(key_gradient, cosine_table, -sine_lookup)
-        .astype(jnp.bfloat16)
-        .reshape(total_rows, KEY_VALUE_HEADS * HEAD_DIM)
-    )
-    value_backward = value_gradient.astype(jnp.bfloat16).reshape(
-        total_rows, KEY_VALUE_HEADS * HEAD_DIM
-    )
-    all_back = jnp.concatenate([query_back, key_back, value_backward], axis=1)
-    first_grad_w = product_tn(normalized_input, all_back)
-    normed_grad = product_transposed_right(all_back, first_weights[:, : q_end + 2 * kv_width])
-    _, first_back = jax.vjp(normalize, inputs, gain_first)
-    input_part, gain_one_grad = first_back(normed_grad)
-    input_grad = state_grad + input_part
-    late = sum_everywhere(
-        jnp.concatenate(
-            [first_grad_w, gain_one_grad[:, None], jnp.zeros((model_width, LANES - 1), F32)], axis=1
-        )
-    )
+    late = sum_everywhere(late_pack)
+    state, _ = lax.optimization_barrier((state, value_back))
+    output = state + jnp.concatenate(out_sum, axis=0).astype(F32)
+    q_end = q_width
     return (
-        output.astype(jnp.bfloat16),
-        input_grad.astype(jnp.bfloat16),
+        output.astype(BF16),
+        input_grad,
         late[:, q_end + 2 * kv_width],
         late[:, :q_end],
         late[:, q_end : q_end + kv_width],

time: 636 us -> 525 us (0.83)
  matrix products: 70.3 us -> 0 us
  Pallas kernels: 130 us -> 192 us
  other arithmetic: 73.4 us -> 25.1 us
  waiting for transfers between devices: 232 us -> 200 us
  local copies, waits for them, and re-layouts: 57.2 us -> 30.9 us
    dot_general x17 -> x0, matrix products: 70.3 us -> none  [the longest x1 15.4 us: per_device(): jnp.einsum('vuol,mul->uovm', attended_gradient, value_matrix_rows, prefer...]
    pallas_call x0 -> x6, Pallas kernels: none -> 63.6 us  [the longest x4 35.4 us: simple_call(): pl.pallas_call(kernel, grid_spec=pltpu.PrefetchScalarGridSpec(num_scalar_...]
    ppermute x12, waiting for transfers between devices: 81.8 us -> 46.2 us  [scatter_sum(): got = lax.ppermute(sent, 'shard', [(i, i ^ flip) for i in range(4)])]
    ppermute x9 -> x3, waiting for transfers between devices: 96.6 us -> 63.9 us  [gather_pieces(): got = lax.ppermute(piece, 'shard', [(i, i ^ flip) for i in range(4)])]
    ppermute x0 -> x6, waiting for transfers between devices: none -> 29.5 us  [fetch_rows(): got = lax.ppermute(mine, 'shard', [(i, i ^ flip) for i in range(4)])]
    convert_element_type x7 -> x2, other arithmetic: 20.7 us -> 2.53 us  [the longest x1 2.53 us: per_device(): output.astype(BF16)]
    concatenate x4 -> x0, local copies, waits for them, and re-layouts: 17.5 us -> none  [the longest x2 10.4 us: per_device(): jnp.concatenate([first_grad_w, gain_one_grad[:, None], jnp.zeros((model_w...]
    ppermute x0 -> x6, starting transfers between devices: none -> 11.1 us  [fetch_rows(): got = lax.ppermute(mine, 'shard', [(i, i ^ flip) for i in range(4)])]
  transfers between devices with their start and end apart: 47 -> 51, of which waited for: 29 -> 24; matrix products, arithmetic and copies ran while one was open for 19% -> 9% of each run, Pallas kernels for 21% -> 37%
where the time goes in v3:
time: 525 us; the launch traced here: 517 us
  waiting for transfers between devices  200 us (38%)
  Pallas kernels  192 us (37%)
  starting transfers between devices  52.9 us (10%)
  local copies, waits for them, and re-layouts  30.9 us (6%)
  other arithmetic  25.1 us (5%)
  between operations  15.5 us (3%)
    pallas_call x2, Pallas kernels, run_experts(): pl.pallas_call(functools.partial(expert_kernel, count), grid_spec=pltpu.P...  88.1 us
    ppermute x3, waiting for transfers between devices, gather_pieces(): got = lax.ppermute(piece, 'shard', [(i, i ^ flip) for i in range(4)])  63.9 us
    ppermute x12, waiting for transfers between devices, scatter_sum(): got = lax.ppermute(sent, 'shard', [(i, i ^ flip) for i in range(4)])  46.2 us
    pallas_call x4, Pallas kernels, simple_call(): pl.pallas_call(kernel, grid_spec=pltpu.PrefetchScalarGridSpec(num_scalar_...  35.4 us
    reduce_scatter x4, waiting for transfers between devices, per_device(): lax.psum_scatter(rows, 'expert', scatter_dimension=0, tiled=True)  29.8 us
    ppermute x6, waiting for transfers between devices, fetch_rows(): got = lax.ppermute(mine, 'shard', [(i, i ^ flip) for i in range(4)])  29.5 us
    pallas_call x1, Pallas kernels, gate_up_gradient(): pl.pallas_call(functools.partial(columns_kernel, chunks, local), grid=(4,...  25.9 us
    ppermute x6, waiting for transfers between devices, sum_everywhere(): total = total + lax.ppermute(sent, 'expert', perm).astype(F32)  20.8 us
  transfers between devices with their start and end apart: 51, of which 24 were waited for; matrix products, arithmetic and copies ran while one was open for 9% of the time, Pallas kernels for 37%

profile of v3, /device:TPU:0, one launch (start us, length us, event | category | flops | bytes accessed | tf_op | source)
XLA Modules:
  0.0 516.8 jit_solution(12332241726058585283)
XLA Ops:
  21.8 9.5 %collective-permute-done.4.refs_5_ = bf16[128,2176]{1,0:T(8,128)(2,1)S(1)} collective-permute-done((bf16[128,2176]{1,0:T(8,128)(2,1)}, bf16[128,2176]{1,0:T(8,128)(2,1)S(1)}, u32[]{:S(2)}, u32[]{:S(2)}) %collective-permute-start.4) | collective-permute-done | bytes 557088 | tf_op jit(solution)/shard_map/ppermute | solution.py:71
  33.6 14.5 %collective-permute-done.10.refs_5_.refs_7_ = bf16[128,1024]{1,0:T(8,128)(2,1)S(1)} collective-permute-done((bf16[128,1024]{1,0:T(8,128)(2,1)}, bf16[128,1024]{1,0:T(8,128)(2,1)S(1)}, u32[]{:S(2)}, u32[]{:S(2)}) %collective-permute-start.10) | collective-permute-done | bytes 262176 | tf_op jit(solution)/shard_map/ppermute | solution.py:71
  62.8 7.7 %project.1 = (bf16[512,1024]{1,0:T(8,128)(2,1)}, bf16[512,1024]{1,0:T(8,128)(2,1)}, bf16[512,512]{1,0:T(8,128)(2,1)}, bf16[512,512]{1,0:T(8,128)(2,1)}, f32[8,1024]{1,0:T(8,128)}, /*index=5*/bf16[1024,128]{1,0:T(8,128)(2,1)}) custom-call(s32[7]{0:T(128)} %stack.63.place_ref, bf16[512,1024]{1,0:T(8,128)(2,1)} %x_ref.5, ...), custom_call_target="tpu_custom_call" | custom-call | tf_op jit(solution)/shard_map/project/pallas_call | solution.py:379
  70.5 13.5 %attend.1 = (bf16[512,1024]{1,0:T(8,128)(2,1)}, f32[32,512]{1,0:T(8,128)}) custom-call(s32[1,512]{1,0:T(1,128)} %bitcast.105, bf16[512,1024]{1,0:T(8,128)(2,1)} %get-tuple-element.49.q_ref, bf16[512,512]{1,0:T(8,128)(2,1)} %get-tuple-element.50.k_ref, bf16[512,512]{1,0:T(8,128)(2,1)} %get-tuple-element.51.v_ref), custom_call_target="tpu_custom_call" | custom-call | tf_op jit(solution)/shard_map/attend/pallas_call | solution.py:517
  84.0 7.2 %mix.1 = (f32[512,1024]{1,0:T(8,128)}, bf16[512,1024]{1,0:T(8,128)(2,1)}, f32[512,128]{1,0:T(8,128)}) custom-call(s32[7]{0:T(128)} %stack.63.place_ref, bf16[512,1024]{1,0:T(8,128)(2,1)} %get-tuple-element.52.attended_ref, bf16[512,1024]{1,0:T(8,128)(2,1)} %x_ref.5, bf16[512,128]{1,0:T(8,128)(2,1)} %pad_convert_fusion.mask_ref, ...), custom_call_target="tpu_custom_call" | custom-call | tf_op jit(solution)/shard_map/mix/pallas_call | solution.py:379
  102.2 31.3 %collective-permute-done.14.refs_3_ = bf16[2,384,1024]{2,1,0:T(8,128)(2,1)} collective-permute-done((bf16[2,384,1024]{2,1,0:T(8,128)(2,1)S(1)}, bf16[2,384,1024]{2,1,0:T(8,128)(2,1)}, u32[]{:S(2)}, u32[]{:S(2)}) %collective-permute-start.14) | collective-permute-done | bytes 1572896 | tf_op jit(solution)/shard_map/ppermute | solution.py:48
  133.5 32.7 %collective-permute-done.13.refs_2_ = bf16[2,384,1024]{2,1,0:T(8,128)(2,1)} collective-permute-done((bf16[2,384,1024]{2,1,0:T(8,128)(2,1)S(1)}, bf16[2,384,1024]{2,1,0:T(8,128)(2,1)}, u32[]{:S(2)}, u32[]{:S(2)}) %collective-permute-start.13) | collective-permute-done | bytes 1572896 | tf_op jit(solution)/shard_map/ppermute | solution.py:48
  166.2 44.0 %experts.3 = (bf16[2048,1024]{1,0:T(8,128)(2,1)}, bf16[2048,1024]{1,0:T(8,128)(2,1)}, bf16[2048,1024]{1,0:T(8,128)(2,1)}, bf16[2048,1024]{1,0:T(8,128)(2,1)}, bf...) custom-call(s32[5]{0:T(128)} %stack.69.place_ref, bf16[2048,1024]{1,0:T(8,128)(2,1)} %all-gather.7.cloned.1.call-done.x_ref.refs_1_, ...), custom_call_target="tpu_custom_call" | custom-call | flops 25769803776 | bytes 29360128 | tf_op jit(solution)/shard_map/experts/pallas_call | solution.py:213
  210.5 44.0 %experts.2 = (bf16[2048,1024]{1,0:T(8,128)(2,1)}, bf16[2048,1024]{1,0:T(8,128)(2,1)}, bf16[2048,1024]{1,0:T(8,128)(2,1)}, bf16[2048,1024]{1,0:T(8,128)(2,1)}, bf...) custom-call(s32[5]{0:T(128)} %stack.69.place_ref, bf16[2048,1024]{1,0:T(8,128)(2,1)} %all-gather.5.cloned.1.call-done.x_ref.refs_0_, ...), custom_call_target="tpu_custom_call" | custom-call | flops 25769803776 | bytes 29360128 | tf_op jit(solution)/shard_map/experts/pallas_call | solution.py:213
  254.6 6.4 %reduce-scatter.7.cloned.1.call-done.refs_1_ = bf16[256,1024]{1,0:T(8,128)(2,1)} async-done(((bf16[2048,1024]{1,0:T(8,128)(2,1)}), bf16[256,1024]{1,0:T(8,128)(2,1)}) %reduce-scatter.7.cloned.1.call-update) | async-done | bytes 524304 | tf_op jit(solution)/shard_map/reduce_scatter | solution.py:778
  267.5 14.5 %down_gradient.1 = bf16[1024,1024]{1,0:T(8,128)(2,1)} custom-call(bf16[2048,1024]{1,0:T(8,128)(2,1)} %get-tuple-element.83.refs_0_, bf16[2048,1024]{1,0:T(8,128)(2,1)} %get-tuple-element.84.refs_1_, bf16[8,528,1024]{2,1,0:T(8,128)(2,1)} %bitcast.110, bf16[8,528,1024]{2,1,0:T(8,128)(2,1)} %bitcast.111), custom_call_target="tpu_custom_call" | custom-call | flops 8589934592 | bytes 16777216 | tf_op jit(solution)/shard_map/down_gradient/pallas_call | solution.py:296
  288.4 23.4 %reduce-scatter.5.cloned.1.call-done.refs_0_ = bf16[256,1024]{1,0:T(8,128)(2,1)} async-done(((bf16[2048,1024]{1,0:T(8,128)(2,1)}), bf16[256,1024]{1,0:T(8,128)(2,1)}) %reduce-scatter.5.cloned.1.call-update) | async-done | bytes 524304 | tf_op jit(solution)/shard_map/reduce_scatter | solution.py:778
  311.8 9.3 %mix_back.1 = (f32[512,1024]{1,0:T(8,128)}, bf16[512,1024]{1,0:T(8,128)(2,1)}, bf16[1024,1152]{1,0:T(8,128)(2,1)}) custom-call(s32[7]{0:T(128)} %stack.63.place_ref, bf16[512,1024]{1,0:T(8,128)(2,1)} %get-tuple-element.52.attended_ref, f32[512,1024]{1,0:T(8,128)} %get-tuple-element.68.state_ref, bf16[512,1024]{1,0:T(8,128)(2,1)} %get-tuple-element.56.mixed_ref, ...), custom_call_target="tpu_custom_call" | custom-call | tf_op jit(solution)/shard_map/mix_back/pallas_call | solution.py:379
  323.6 25.9 %gate_up_gradient.1 = bf16[2,1024,1024]{2,1,0:T(8,128)(2,1)} custom-call(bf16[2048,1024]{1,0:T(8,128)(2,1)} %all-gather.5.cloned.1.call-done.x_ref.refs_0_, bf16[2048,1024]{1,0:T(8,128)(2,1)} %all-gather.7.cloned.1.call-done.x_ref.refs_1_, bf16[2048,1024]{1,0:T(8,128)(2,1)} %get-tuple-element.78.refs_2_, bf16[2048,1024]{1,0:T(8,128)(2,1)} %get-tuple-element.79.refs_3_, ...), custom_call_target="tpu_custom_call" | custom-call | flops 17179869184 | bytes 25165824 | tf_op jit(solution)/shard_map/gate_up_gradient/pallas_call | solution.py:260
  357.2 14.7 %attend_back.1 = (bf16[512,1024]{1,0:T(8,128)(2,1)}, bf16[512,512]{1,0:T(8,128)(2,1)}, bf16[512,512]{1,0:T(8,128)(2,1)}) custom-call(s32[1,512]{1,0:T(1,128)} %bitcast.106, bf16[512,1024]{1,0:T(8,128)(2,1)} %get-tuple-element.49.q_ref, bf16[512,512]{1,0:T(8,128)(2,1)} %get-tuple-element.50.k_ref, bf16[512,512]{1,0:T(8,128)(2,1)} %get-tuple-element.51.v_ref, ...), custom_call_target="tpu_custom_call" | custom-call | tf_op jit(solution)/shard_map/attend_back/pallas_call | solution.py:535
  371.9 11.2 %project_back.1 = (bf16[512,1024]{1,0:T(8,128)(2,1)}, bf16[1024,2176]{1,0:T(8,128)(2,1)}) custom-call(s32[7]{0:T(128)} %stack.63.place_ref, bf16[512,1024]{1,0:T(8,128)(2,1)} %get-tuple-element.71.normed_ref, bf16[512,1024]{1,0:T(8,128)(2,1)} %x_ref.5, f32[512,1024]{1,0:T(8,128)} %get-tuple-element.72.state_grad_ref, f32[8,1024]{1,0:T(8,128)} %get-tuple-element.54.gains_ref, ...), custom_call_target="tpu_custom_call" | custom-call | tf_op jit(solution)/shard_map/project_back/pallas_call | solution.py:379
  387.4 15.6 %collective-permute-done.38 = bf16[2,256,1024]{2,1,0:T(8,128)(2,1)} collective-permute-done((bf16[2,256,1024]{2,1,0:T(8,128)(2,1)}, bf16[2,256,1024]{2,1,0:T(8,128)(2,1)}, u32[]{:S(2)}, u32[]{:S(2)}) %collective-permute-start.38) | collective-permute-done | bytes 1048608 | tf_op jit(solution)/shard_map/ppermute | solution.py:92
  409.6 6.0 %collective-permute-done.29 = bf16[1,128,1152]{2,1,0:T(8,128)(2,1)S(1)} collective-permute-done((bf16[1,128,1152]{2,1,0:T(8,128)(2,1)S(1)}, bf16[1,128,1152]{2,1,0:T(8,128)(2,1)S(1)}, u32[]{:S(2)}, u32[]{:S(2)}) %collective-permute-start.29) | collective-permute-done | bytes 294944 | tf_op jit(solution)/shard_map/ppermute | solution.py:92
  447.6 7.8 %collective-permute-done.16 = bf16[1,128,2176]{2,1,0:T(8,128)(2,1)S(1)} collective-permute-done((bf16[1,128,2176]{2,1,0:T(8,128)(2,1)S(1)}, bf16[1,128,2176]{2,1,0:T(8,128)(2,1)S(1)}, u32[]{:S(2)}, u32[]{:S(2)}) %collective-permute-start.16) | collective-permute-done | bytes 557088 | tf_op jit(solution)/shard_map/ppermute | solution.py:92
  455.4 7.8 %collective-permute-done.18 = bf16[1,128,2176]{2,1,0:T(8,128)(2,1)S(1)} collective-permute-done((bf16[1,128,2176]{2,1,0:T(8,128)(2,1)S(1)}, bf16[1,128,2176]{2,1,0:T(8,128)(2,1)S(1)}, u32[]{:S(2)}, u32[]{:S(2)}) %collective-permute-start.18) | collective-permute-done | bytes 557088 | tf_op jit(solution)/shard_map/ppermute | solution.py:92
  467.9 7.2 %collective-permute-done.19 = bf16[32,2176]{1,0:T(8,128)(2,1)S(1)} collective-permute-done((bf16[32,2176]{1,0:T(8,128)(2,1)S(1)}, bf16[32,2176]{1,0:T(8,128)(2,1)S(1)}, u32[]{:S(2)}, u32[]{:S(2)}) %collective-permute-start.19) | collective-permute-done | bytes 139296 | tf_op jit(solution)/shard_map/ppermute | solution.py:114
  477.0 10.3 %collective-permute-done.20 = bf16[32,2176]{1,0:T(8,128)(2,1)S(1)} collective-permute-done((bf16[32,2176]{1,0:T(8,128)(2,1)S(1)}, bf16[32,2176]{1,0:T(8,128)(2,1)S(1)}, u32[]{:S(2)}, u32[]{:S(2)}) %collective-permute-start.20) | collective-permute-done | bytes 139296 | tf_op jit(solution)/shard_map/ppermute | solution.py:114
  491.6 4.4 collective-permute-done.22
  496.0 4.4 collective-permute-done.23
  (212 shorter events, 128.0 us)
Async XLA Ops:
  7.2 92.0 %all-gather.9.cloned.1.call-start = ((), (), s32[]{:S(2)}) async-start(), calls=%async_computation.11 | async-start | bytes 9732096 | tf_op jit(solution)/shard_map/all_gather | solution.py:698
  10.8 155.3 %all-gather.7.cloned.1.call-start = ((), (), s32[]{:S(2)}) async-start(), calls=%async_computation.6 | async-start | bytes 4718592 | tf_op jit(solution)/shard_map/all_gather | solution.py:770
  17.6 32.2 %collective-permute-start.2 = (bf16[128,2176]{1,0:T(8,128)(2,1)}, bf16[128,2176]{1,0:T(8,128)(2,1)S(1)}, u32[]{:S(2)}, u32[]{:S(2)}) collective-permute-start(bf16[128,2176]{1,0:T(8,128)(2,1)} %constant_dynamic-slice_fusion.9), channel_id=1, source_target_pairs={{0,2},{1,3},{2,0},{3,1},{4,6},{5,7},{6,4},{7,5},{8,10},{9,11},{10,... | collective-permute-start | bytes 1671176 | tf_op jit(solution)/shard_map/ppermute | solution.py:71
  18.1 31.8 %collective-permute-start = (bf16[128,2176]{1,0:T(8,128)(2,1)}, bf16[128,2176]{1,0:T(8,128)(2,1)S(1)}, u32[]{:S(2)}, u32[]{:S(2)}) collective-permute-start(bf16[128,2176]{1,0:T(8,128)(2,1)} %constant_dynamic-slice_fusion.9), channel_id=1, source_target_pairs={{0,1},{1,0},{2,3},{3,2},{4,5},{5,4},{6,7},{7,6},{8,9},{9,8},{10,11... | collective-permute-start | bytes 1671176 | tf_op jit(solution)/shard_map/ppermute | solution.py:71
  18.9 29.2 %collective-permute-start.10 = (bf16[128,1024]{1,0:T(8,128)(2,1)}, bf16[128,1024]{1,0:T(8,128)(2,1)S(1)}, u32[]{:S(2)}, u32[]{:S(2)}) collective-permute-start(bf16[128,1024]{1,0:T(8,128)(2,1)} %constant_dynamic-slice_fusion.8), channel_id=1, source_target_pairs={{0,3},{1,2},{2,1},{3,0},{4,7},{5,6},{6,5},{7,4},{8,11},{9,10},{10,... | collective-permute-start | bytes 786440 | tf_op jit(solution)/shard_map/ppermute | solution.py:71
  53.6 30.4 %collective-permute-start.11 = (bf16[128,1024]{1,0:T(8,128)(2,1)S(1)}, bf16[128,1024]{1,0:T(8,128)(2,1)}, u32[]{:S(2)}, u32[]{:S(2)}) collective-permute-start(bf16[128,1024]{1,0:T(8,128)(2,1)S(1)} %collective-permute-done.10.refs_5_.refs_7_), channel_id=1, source_target_pairs={{0,4},{4,0},{8,12},{12,8},{16,20},{20,16},{24,28},{28,24},{1,5},{5... | collective-permute-start | bytes 786440 | tf_op jit(solution)/shard_map/ppermute | solution.py:57
  56.0 28.0 %collective-permute-start.9 = (bf16[128,1024]{1,0:T(8,128)(2,1)S(1)}, bf16[128,1024]{1,0:T(8,128)(2,1)}, u32[]{:S(2)}, u32[]{:S(2)}) collective-permute-start(bf16[128,1024]{1,0:T(8,128)(2,1)S(1)} %collective-permute-done.8.refs_3_.refs_5_), channel_id=1, source_target_pairs={{0,4},{4,0},{8,12},{12,8},{16,20},{20,16},{24,28},{28,24},{1,5},{5... | collective-permute-start | bytes 786440 | tf_op jit(solution)/shard_map/ppermute | solution.py:57
  56.0 28.0 %collective-permute-start.7 = (bf16[128,1024]{1,0:T(8,128)(2,1)}, bf16[128,1024]{1,0:T(8,128)(2,1)}, u32[]{:S(2)}, u32[]{:S(2)}) collective-permute-start(bf16[128,1024]{1,0:T(8,128)(2,1)} %collective-permute-done.6.refs_1_.refs_3_), channel_id=1, source_target_pairs={{0,4},{4,0},{8,12},{12,8},{16,20},{20,16},{24,28},{28,24},{1,5},{5... | collective-permute-start | bytes 786440 | tf_op jit(solution)/shard_map/ppermute | solution.py:57
  93.6 116.9 %all-gather.5.cloned.1.call-start = ((), (), s32[]{:S(2)}) async-start(), calls=%async_computation.5 | async-start | bytes 4718592 | tf_op jit(solution)/shard_map/all_gather | solution.py:770
  94.4 166.6 %reduce-scatter.7.cloned.1.call-start = ((), (), s32[]{:S(2)}) async-start(), calls=%async_computation.8 | async-start | bytes 4718592 | tf_op jit(solution)/shard_map/reduce_scatter | solution.py:778
  95.1 38.4 %collective-permute-start.14 = (bf16[2,384,1024]{2,1,0:T(8,128)(2,1)S(1)}, bf16[2,384,1024]{2,1,0:T(8,128)(2,1)}, u32[]{:S(2)}, u32[]{:S(2)}) collective-permute-start(bf16[2,384,1024]{2,1,0:T(8,128)(2,1)S(1)} %pad_maximum_fusion.refs_0_), channel_id=1, source_target_pairs={{0,3},{1,2},{2,1},{3,0},{4,7},{5,6},{6,5},{7,4},{8,11},{9,10},{10,... | collective-permute-start | bytes 4718600 | tf_op jit(solution)/shard_map/ppermute | solution.py:48
  97.5 68.6 %collective-permute-start.13 = (bf16[2,384,1024]{2,1,0:T(8,128)(2,1)S(1)}, bf16[2,384,1024]{2,1,0:T(8,128)(2,1)}, u32[]{:S(2)}, u32[]{:S(2)}) collective-permute-start(bf16[2,384,1024]{2,1,0:T(8,128)(2,1)S(1)} %pad_maximum_fusion.refs_0_), channel_id=1, source_target_pairs={{0,2},{1,3},{2,0},{3,1},{4,6},{5,7},{6,4},{7,5},{8,10},{9,11},{10,... | collective-permute-start | bytes 4718600 | tf_op jit(solution)/shard_map/ppermute | solution.py:48
  98.0 68.1 %collective-permute-start.12 = (bf16[2,384,1024]{2,1,0:T(8,128)(2,1)S(1)}, bf16[2,384,1024]{2,1,0:T(8,128)(2,1)}, u32[]{:S(2)}, u32[]{:S(2)}) collective-permute-start(bf16[2,384,1024]{2,1,0:T(8,128)(2,1)S(1)} %pad_maximum_fusion.refs_0_), channel_id=1, source_target_pairs={{0,1},{1,0},{2,3},{3,2},{4,5},{5,4},{6,7},{7,6},{8,9},{9,8},{10,11... | collective-permute-start | bytes 4718600 | tf_op jit(solution)/shard_map/ppermute | solution.py:48
  210.2 101.6 %reduce-scatter.5.cloned.1.call-start = ((), (), s32[]{:S(2)}) async-start(), calls=%async_computation.7 | async-start | bytes 4718592 | tf_op jit(solution)/shard_map/reduce_scatter | solution.py:778
  254.5 252.5 %reduce-scatter.9.cloned.1.call-start = ((), (), s32[]{:S(2)}) async-start(), calls=%async_computation.9 | async-start | bytes 4718592 | tf_op jit(solution)/shard_map/reduce_scatter | solution.py:795
  267.2 239.8 %reduce-scatter.11.cloned.1.call-start = ((), (), s32[]{:S(2)}) async-start(), calls=%async_computation.10 | async-start | bytes 4718592 | tf_op jit(solution)/shard_map/reduce_scatter | solution.py:795
  284.7 150.8 %collective-permute-start.42 = (bf16[2,128,1024]{2,1,0:T(8,128)(2,1)}, bf16[2,128,1024]{2,1,0:T(8,128)(2,1)}, u32[]{:S(2)}, u32[]{:S(2)}) collective-permute-start(bf16[2,128,1024]{2,1,0:T(8,128)(2,1)} %get-tuple-element.161), channel_id=1, source_target_pairs={{0,3},{1,2},{2,1},{3,0},{4,7},{5,6},{6,5},{7,4},{8,11},{9,10},{10,... | collective-permute-start | bytes 1572872 | tf_op jit(solution)/shard_map/ppermute | solution.py:92
  323.6 61.6 %collective-permute-start.26 = (bf16[4,128,1152]{2,1,0:T(8,128)(2,1)}, bf16[4,128,1152]{2,1,0:T(8,128)(2,1)S(1)}, u32[]{:S(2)}, u32[]{:S(2)}) collective-permute-start(bf16[4,128,1152]{2,1,0:T(8,128)(2,1)} %dynamic-slice_bitcast_fusion.1), channel_id=1, source_target_pairs={{0,4},{4,0},{8,12},{12,8},{16,20},{20,16},{24,28},{28,24},{1,5},{5... | collective-permute-start | bytes 3538952 | tf_op jit(solution)/shard_map/ppermute | solution.py:57
  353.7 32.2 %collective-permute-start.39 = (bf16[2,256,1024]{2,1,0:T(8,128)(2,1)}, bf16[2,256,1024]{2,1,0:T(8,128)(2,1)}, u32[]{:S(2)}, u32[]{:S(2)}) collective-permute-start(bf16[2,256,1024]{2,1,0:T(8,128)(2,1)} %get-tuple-element.154), channel_id=1, source_target_pairs={{0,3},{1,2},{2,1},{3,0},{4,7},{5,6},{6,5},{7,4},{8,11},{9,10},{10,... | collective-permute-start | bytes 3145736 | tf_op jit(solution)/shard_map/ppermute | solution.py:92
  356.1 46.9 %collective-permute-start.38 = (bf16[2,256,1024]{2,1,0:T(8,128)(2,1)}, bf16[2,256,1024]{2,1,0:T(8,128)(2,1)}, u32[]{:S(2)}, u32[]{:S(2)}) collective-permute-start(bf16[2,256,1024]{2,1,0:T(8,128)(2,1)} %get-tuple-element.155), channel_id=1, source_target_pairs={{0,2},{1,3},{2,0},{3,1},{4,6},{5,7},{6,4},{7,5},{8,10},{9,11},{10,... | collective-permute-start | bytes 3145736 | tf_op jit(solution)/shard_map/ppermute | solution.py:92
  356.6 48.1 %collective-permute-start.37 = (bf16[2,256,1024]{2,1,0:T(8,128)(2,1)}, bf16[2,256,1024]{2,1,0:T(8,128)(2,1)}, u32[]{:S(2)}, u32[]{:S(2)}) collective-permute-start(bf16[2,256,1024]{2,1,0:T(8,128)(2,1)} %get-tuple-element.156), channel_id=1, source_target_pairs={{0,1},{1,0},{2,3},{3,2},{4,5},{5,4},{6,7},{7,6},{8,9},{9,8},{10,11... | collective-permute-start | bytes 3145736 | tf_op jit(solution)/shard_map/ppermute | solution.py:92
  385.2 45.2 %collective-permute-start.15 = (bf16[4,128,2176]{2,1,0:T(8,128)(2,1)S(1)}, bf16[4,128,2176]{2,1,0:T(8,128)(2,1)}, u32[]{:S(2)}, u32[]{:S(2)}) collective-permute-start(bf16[4,128,2176]{2,1,0:T(8,128)(2,1)S(1)} %dynamic-slice_bitcast_fusion), channel_id=1, source_target_pairs={{0,4},{4,0},{8,12},{12,8},{16,20},{20,16},{24,28},{28,24},{1,5},{5... | collective-permute-start | bytes 6684680 | tf_op jit(solution)/shard_map/ppermute | solution.py:57
  435.5 27.7 %collective-permute-start.18 = (bf16[1,128,2176]{2,1,0:T(8,128)(2,1)S(1)}, bf16[1,128,2176]{2,1,0:T(8,128)(2,1)S(1)}, u32[]{:S(2)}, u32[]{:S(2)}) collective-permute-start(bf16[1,128,2176]{2,1,0:T(8,128)(2,1)S(1)} %get-tuple-element.151), channel_id=1, source_target_pairs={{0,3},{1,2},{2,1},{3,0},{4,7},{5,6},{6,5},{7,4},{8,11},{9,10},{10,... | collective-permute-start | bytes 1671176 | tf_op jit(solution)/shard_map/ppermute | solution.py:92
  447.5 40.4 %collective-permute-start.35 = (bf16[32,1152]{1,0:T(8,128)(2,1)S(1)}, bf16[32,1152]{1,0:T(8,128)(2,1)S(1)}, u32[]{:S(2)}, u32[]{:S(2)}) collective-permute-start(bf16[32,1152]{1,0:T(8,128)(2,1)S(1)} %get-tuple-element.147), channel_id=1, source_target_pairs={{0,24},{4,28},{8,0},{12,4},{16,8},{20,12},{24,16},{28,20},{1,25},{... | collective-permute-start | bytes 221192 | tf_op jit(solution)/shard_map/ppermute | solution.py:120
  (50 other events, 722.4 us)
Sparse Core Ops, SparseCore 0:
  11.0 86.9 all-gather.8
  100.1 45.6 all-gather.6
  148.0 45.8 all-gather.4
  210.3 50.5 reduce-scatter.6
  263.1 48.6 reduce-scatter.4
  314.0 48.1 reduce-scatter.8
  425.4 62.7 reduce-scatter.10

commit v4 on v3

--- a/solution.py
+++ b/solution.py
@@ -13,7 +13,6 @@
 HEAD_DIM = 64
 LANES = 128
 VMEM_LIMIT = 58 * 1024 * 1024
-CHUNKS = 2
 SMALL_COST = pl.CostEstimate(flops=0, bytes_accessed=0, transcendentals=0)
 F32 = jnp.float32
 BF16 = jnp.bfloat16
@@ -39,17 +38,13 @@
     return lax.dynamic_index_in_dim(blocks, index, 0, keepdims=False)
 
 
-def gather_pieces(piece):
-    count = lax.axis_size("shard")
-    if count == 4:
-        me = lax.axis_index("shard")
-        pieces = [(piece, me)]
-        for flip in (1, 2, 3):
-            got = lax.ppermute(piece, "shard", [(i, i ^ flip) for i in range(4)])
-            pieces.append((got, me ^ flip))
-        return pieces
-    every = lax.all_gather(piece, "shard", axis=0)
-    return [(every[i], jnp.int32(i)) for i in range(count)]
+def flip_shard(value, flip):
+    return lax.ppermute(value, "shard", [(i, i ^ flip) for i in range(4)])
+
+
+def flip_layer(value, flip):
+    size = lax.axis_size("expert")
+    return lax.ppermute(value, "expert", [(i, i ^ (2 * flip)) for i in range(size)])
 
 
 def swap_cores(value):
@@ -57,7 +52,13 @@
     return lax.ppermute(value, "expert", [(i, i ^ 1) for i in range(size)])
 
 
-def fetch_rows(rows):
+def both_ways(value, first, second):
+    half = value.shape[0] // 2
+    one, two = first(value), second(value)
+    return one, two, first(two[:half]), second(one[half:])
+
+
+def fetch_rows(rows, after=None):
     count = lax.axis_size("shard")
     size = rows.shape[0]
     if count != 4:
@@ -66,13 +67,71 @@
     core = lax.axis_index("expert") % 2
     half = size // 2
     mine = lax.dynamic_slice_in_dim(rows, core * half, half, 0)
+    if after is not None:
+        mine, _ = lax.optimization_barrier((mine, after))
+    one, two, low, high = both_ways(mine, lambda v: flip_shard(v, 1), lambda v: flip_shard(v, 2))
     pieces, places = [rows], [me * size]
-    for flip in (1, 2, 3):
-        got = lax.ppermute(mine, "shard", [(i, i ^ flip) for i in range(4)])
-        first = (me ^ flip) * size
+    for got, flip, skip in ((one, 1, 0), (two, 2, 0), (low, 3, 0), (high, 3, half // 2)):
+        first = (me ^ flip) * size + skip
         pieces += [got, swap_cores(got)]
         places += [first + core * half, first + (1 - core) * half]
     return pieces, jnp.stack(places).astype(jnp.int32)
+
+
+def fetch_experts(packed, after):
+    count = lax.axis_size("shard")
+    local = packed.shape[0]
+    if count != 4 or local != 2:
+        every = lax.all_gather(packed, "shard", axis=0)
+        arrays = [every[i] for i in range(count)]
+        sources = [[(i, j, i) for i in range(count)] for j in range(local)]
+        return arrays, sources, [jnp.int32(i) for i in range(count)]
+    me = lax.axis_index("shard")
+    sent, _ = lax.optimization_barrier((packed, after))
+    one, two, low, high = both_ways(sent, lambda v: flip_shard(v, 1), lambda v: flip_shard(v, 2))
+    arrays = [packed, one, two, low, high]
+    sources = [[(0, j, 0), (1, j, 1), (2, j, 2), (3 + j, 0, 3)] for j in range(2)]
+    return arrays, sources, [me, me ^ 1, me ^ 2, me ^ 3]
+
+
+def gather_layers(value):
+    layers = lax.axis_size("expert") // 2
+    if layers != 4:
+        every = lax.all_gather(value, "expert", axis=0)
+        me = lax.axis_index("expert")
+        return [value] + [pick(every, me ^ (2 * flip)) for flip in range(1, layers)]
+    one, three, low, high = both_ways(
+        value, lambda v: flip_layer(v, 1), lambda v: flip_layer(v, 3)
+    )
+    return [value, one, jnp.concatenate([low, high], axis=0), three]
+
+
+def sum_layers(mine, other):
+    layers = lax.axis_size("expert") // 2
+    arrived = [swap_cores(value) for value in other]
+    arrived = [piece for value in arrived for piece in jnp.split(value, value.shape[0] // mine[0].shape[0])]
+
+    def paired(flip):
+        return mine[flip].astype(F32) + arrived[flip].astype(F32)
+
+    if layers != 4:
+        me = lax.axis_index("expert") // 2
+        stack = jnp.stack([paired(flip).astype(BF16) for flip in range(layers)])
+        blocks = jnp.stack([pick(stack, me ^ place) for place in range(layers)])
+        groups = [[2 * i + core for i in range(layers)] for core in range(2)]
+        return [
+            lax.psum_scatter(
+                blocks, "expert", scatter_dimension=0, axis_index_groups=groups
+            )
+        ]
+    half = mine[0].shape[0] // 2
+    far = paired(2).astype(BF16)
+    low = flip_layer(far[:half], 1).astype(F32)
+    high = flip_layer(far[half:], 3).astype(F32)
+    three, one = paired(3), paired(1)
+    three = jnp.concatenate([three[:half] + low, three[half:]], axis=0).astype(BF16)
+    one = jnp.concatenate([one[:half], one[half:] + high], axis=0).astype(BF16)
+    return [mine[0], arrived[0], flip_layer(one, 1), flip_layer(three, 3)]
 
 
 def scatter_sum(values, axis, after=None):
@@ -89,78 +148,99 @@
     total = own.astype(F32)
     for flip in (1, 2, 3):
         sent = lax.dynamic_slice_in_dim(values, (me ^ flip) * size, size, axis).astype(BF16)
-        got = lax.ppermute(sent, "shard", [(i, i ^ flip) for i in range(4)])
-        total = total + got.astype(F32)
+        total = total + flip_shard(sent, flip).astype(F32)
     return total
 
 
 def sum_everywhere(grad):
     count = lax.axis_size("shard")
-    size = lax.axis_size("expert")
-    layers = size // 2
-    place = lax.axis_index("expert")
-    core, layer = place % 2, place // 2
+    layers = lax.axis_size("expert") // 2
+    core = lax.axis_index("expert") % 2
     width = grad.shape[1]
     half = grad.shape[0] // count // 2
     blocks = grad.reshape(count, 2, half, width)
     mine = lax.dynamic_index_in_dim(blocks, core, 1, keepdims=False)
     away = lax.dynamic_index_in_dim(blocks, 1 - core, 1, keepdims=False)
     paired = mine.astype(F32) + swap_cores(away).astype(F32)
-    local = scatter_sum(paired, 0).reshape(layers, half // layers, width)
-    total = pick(local, layer)
-    for step in range(1, layers):
-        perm = [(i, (i + 2 * step) % size) for i in range(size)]
-        sent = pick(local, (layer + step) % layers).astype(BF16)
-        total = total + lax.ppermute(sent, "expert", perm).astype(F32)
-    total = total.astype(BF16)
-    parts = jnp.zeros((layers, half // layers, width), BF16)
-    parts = lax.dynamic_update_index_in_dim(parts, total, layer, 0)
-    for step in range(1, layers):
-        perm = [(i, (i + 2 * step) % size) for i in range(size)]
-        got = lax.ppermute(total, "expert", perm)
-        parts = lax.dynamic_update_index_in_dim(parts, got, (layer - step) % layers, 0)
-    mine = parts.reshape(half, width)
-    other = swap_cores(mine)
-    low = jnp.where(core == 0, mine, other)
-    high = jnp.where(core == 0, other, mine)
+    local = scatter_sum(paired, 0).reshape(half, width).astype(BF16)
+    if layers != 4:
+        groups = [[2 * i + side for i in range(layers)] for side in range(2)]
+        total = lax.psum(local, "expert", axis_index_groups=groups)
+    else:
+        low, high = local[: half // 2], local[half // 2 :]
+        for order in ((1, 3), (3, 1)):
+            low, high = (
+                (low.astype(F32) + flip_layer(low, order[0]).astype(F32)).astype(BF16),
+                (high.astype(F32) + flip_layer(high, order[1]).astype(F32)).astype(BF16),
+            )
+        total = jnp.concatenate([low, high], axis=0)
+    other = swap_cores(total)
+    low = jnp.where(core == 0, total, other)
+    high = jnp.where(core == 0, other, total)
     return jnp.concatenate([low, high], axis=0).astype(F32)
 
 
-def expert_kernel(count, place_ref, x_ref, dy_ref, mask_ref, router_ref, *refs):
-    pieces = refs[:count]
-    out_ref, row_ref, act_ref, gate_ref, up_ref, score_ref, gu, down, sem = refs[count:]
+def expert_kernel(sources, pairs, arrays, place_ref, mask_ref, router_ref, *refs):
+    xs, refs = refs[: 2 * pairs], refs[2 * pairs :]
+    dys, refs = refs[: 2 * pairs], refs[2 * pairs :]
+    pieces, refs = refs[:arrays], refs[arrays:]
+    outs, rows_out = refs[0:2], refs[2:4]
+    act_ref, gate_ref, up_ref, score_ref, gu, down, x_in, dy_in, sem, in_sem = refs[4:]
     local, rows, width = pieces[0].shape
     third = rows // 3
     hidden = width // 2
-
-    @pl.when(pl.program_id(0) == 0)
-    def _():
+    step = pl.program_id(0)
+
+    def weight_copies(j):
         copies = []
-        for i in range(count):
-            at = place_ref[i]
+        for number, (array, index, slot) in enumerate(sources[j]):
+            at = place_ref[slot]
             copies.append(
                 pltpu.make_async_copy(
-                    pieces[i].at[:, pl.ds(0, 2 * third), :],
-                    gu.at[:, pl.ds(pl.multiple_of(at * (2 * third), 16), 2 * third), :],
-                    sem.at[2 * i],
+                    pieces[array].at[index, pl.ds(0, 2 * third), :],
+                    gu.at[j, pl.ds(pl.multiple_of(at * (2 * third), 16), 2 * third), :],
+                    sem.at[j, number, 0],
                 )
             )
             copies.append(
                 pltpu.make_async_copy(
-                    pieces[i].at[:, pl.ds(2 * third, third), :],
-                    down.at[:, pl.ds(pl.multiple_of(at * third, 16), third), :],
-                    sem.at[2 * i + 1],
+                    pieces[array].at[index, pl.ds(2 * third, third), :],
+                    down.at[j, pl.ds(pl.multiple_of(at * third, 16), third), :],
+                    sem.at[j, number, 1],
                 )
             )
-        for copy in copies:
+        return copies
+
+    def input_copies(i):
+        slot = i % 2
+        return [
+            pltpu.make_async_copy(xs[i], x_in.at[slot], in_sem.at[slot, 0]),
+            pltpu.make_async_copy(dys[i], dy_in.at[slot], in_sem.at[slot, 1]),
+        ]
+
+    @pl.when(step == 0)
+    def _():
+        for copy in input_copies(0):
             copy.start()
-        for copy in copies:
-            copy.wait()
-
-    x = x_ref[...]
+        for j in range(local):
+            for copy in weight_copies(j):
+                copy.start()
+
+    for i in range(2 * pairs):
+
+        @pl.when(step == i)
+        def _(i=i):
+            if i + 1 < 2 * pairs:
+                for copy in input_copies(i + 1):
+                    copy.start()
+            for copy in input_copies(i):
+                copy.wait()
+
+    slot = lax.rem(step, 2)
+    x = x_in[slot]
     tile = x.shape[0]
-    dy = dy_ref[...].reshape(tile, width)
-    mask = mask_ref[...].reshape(tile, LANES)
+    dy = dy_in[slot]
+    mask = mask_ref[...]
     lane = lax.broadcasted_iota(jnp.int32, (tile, LANES), 1)
     logits = jnp.where(mask > 0, jnp.dot(x, router_ref[...], preferred_element_type=F32), -1e30)
     powers = jnp.exp(logits - jnp.max(logits, axis=1, keepdims=True))
@@ -168,8 +248,15 @@
     out = None
     row = None
     scores = jnp.zeros((tile, LANES), F32)
+    own_slot = max(slot for per in sources for _, _, slot in per) + 1
     for j in range(local):
-        own = place_ref[count] * local + j
+
+        @pl.when(step == 0)
+        def _(j=j):
+            for copy in weight_copies(j):
+                copy.wait()
+
+        own = place_ref[own_slot] * local + j
         gate = jnp.sum(jnp.where(lane == own, chances, 0.0), axis=1, keepdims=True)
         left = gu[j, :, :hidden]
         right = gu[j, :, hidden:]
@@ -193,119 +280,140 @@
         out = part if out is None else out + part
         part = product_transposed_right(gate_back, left) + product_transposed_right(up_back, right)
         row = part if row is None else row + part
-    out_ref[...] = out.astype(BF16)
-    row_ref[...] = row.astype(BF16)
     score_ref[...] = scores
-
-
-def run_experts(every_x, every_dy, mask, router, pieces, chunk):
-    count = len(pieces)
-    total, width = every_x.shape
-    local, rows, _ = pieces[0][0].shape
+    out, row = out.astype(BF16), row.astype(BF16)
+    for side in range(2):
+
+        @pl.when(slot == side)
+        def _(side=side):
+            outs[side][...] = out
+            rows_out[side][...] = row
+
+
+def run_experts(flips, xs, dys, mask, router, weights):
+    arrays, sources, places = weights
+    pairs = len(flips)
+    size, width = xs[0].shape
+    local, rows, _ = arrays[0].shape
     third = rows // 3
-    peers = every_dy.shape[0]
-    rows_each = total // peers
-    group = 2
-    tile = group * rows_each
-    place = jnp.stack([index for _, index in pieces] + [lax.axis_index("expert")]).astype(jnp.int32)
-    block = pl.BlockSpec((tile, width), lambda i, p: (i, 0))
-    thin = pl.BlockSpec((tile, LANES), lambda i, p: (i, 0))
+    count = len(sources[0])
+    me = lax.axis_index("expert")
+    devices = [me ^ (2 * flip + side) for flip in flips for side in range(2)]
+    place = jnp.stack([*places, me, *devices]).astype(jnp.int32)
+    skip = len(places) + 1
+    block = pl.BlockSpec((size, width), lambda i, p: (i, 0))
+    pair = pl.BlockSpec((size, width), lambda i, p: (i // 2, 0))
+    anywhere = pl.BlockSpec(memory_space=pl.ANY)
+    total = 2 * pairs * size
     return pl.pallas_call(
-        functools.partial(expert_kernel, count),
+        functools.partial(expert_kernel, sources, pairs, len(arrays)),
         grid_spec=pltpu.PrefetchScalarGridSpec(
             num_scalar_prefetch=1,
-            grid=(peers // group,),
+            grid=(2 * pairs,),
             in_specs=[
-                block,
-                pl.BlockSpec((group, rows_each, width), lambda i, p: (i, chunk, 0)),
-                pl.BlockSpec((group, rows_each, LANES), lambda i, p: (i, chunk, 0)),
+                pl.BlockSpec((None, size, LANES), lambda i, p: (p[skip + i], 0, 0)),
                 pl.BlockSpec((width, LANES), lambda i, p: (0, 0)),
             ]
-            + [pl.BlockSpec(memory_space=pl.ANY)] * count,
-            out_specs=[block, block, block, block, block, thin],
+            + [anywhere] * (4 * pairs + len(arrays)),
+            out_specs=[pair] * 4
+            + [block, block, block, pl.BlockSpec((size, LANES), lambda i, p: (i, 0))],
             scratch_shapes=[
                 pltpu.VMEM((local, 2 * third * count, width), BF16),
                 pltpu.VMEM((local, third * count, width), BF16),
-                pltpu.SemaphoreType.DMA((2 * count,)),
+                pltpu.VMEM((2, size, width), BF16),
+                pltpu.VMEM((2, size, width), BF16),
+                pltpu.SemaphoreType.DMA((local, count, 2)),
+                pltpu.SemaphoreType.DMA((2, 2)),
             ],
         ),
-        out_shape=[jax.ShapeDtypeStruct((total, width), BF16)] * 5
+        out_shape=[jax.ShapeDtypeStruct((pairs * size, width), BF16)] * 4
+        + [jax.ShapeDtypeStruct((total, width), BF16)] * 3
         + [jax.ShapeDtypeStruct((total, LANES), F32)],
         compiler_params=pltpu.CompilerParams(vmem_limit_bytes=VMEM_LIMIT),
         cost_estimate=pl.CostEstimate(
             flops=2 * total * width * width * 6, bytes_accessed=total * width * 14, transcendentals=0
         ),
         name="experts",
-    )(place, every_x, every_dy, mask, router, *[piece for piece, _ in pieces])
-
-
-def columns_kernel(chunks, local, *refs):
-    xs, gates, ups = refs[:chunks], refs[chunks : 2 * chunks], refs[2 * chunks : 3 * chunks]
-    out_ref = refs[3 * chunks]
+    )(place, mask, router, *xs, *dys, *arrays)
+
+
+def grouped(refs, groups):
+    at = 0
+    for group in groups:
+        rows = 0
+        taken = []
+        while rows < group.shape[0]:
+            taken.append(refs[at][...])
+            rows += refs[at].shape[0]
+            at += 1
+        yield jnp.concatenate(taken, axis=0)
+
+
+def columns_kernel(chunks, groups, local, *refs):
+    xs, gates = refs[:chunks], refs[chunks : chunks + groups]
+    ups, out_ref = refs[chunks + groups : chunks + 2 * groups], refs[chunks + 2 * groups]
     hidden = out_ref.shape[2] // 2
+    totals = [None] * (2 * local)
+    for x, gate_ref, up_ref in zip(grouped(xs, gates), gates, ups):
+        for j in range(local):
+            for side, value_ref in ((0, gate_ref), (1, up_ref)):
+                part = product_tn(x, value_ref[:, j * hidden : (j + 1) * hidden])
+                at = 2 * j + side
+                totals[at] = part if totals[at] is None else totals[at] + part
     for j in range(local):
-        for side, values in ((0, gates), (1, ups)):
-            total = None
-            for x_ref, value_ref in zip(xs, values):
-                part = product_tn(x_ref[...], value_ref[:, j * hidden : (j + 1) * hidden])
-                total = part if total is None else total + part
-            out_ref[j, :, side * hidden : (side + 1) * hidden] = total.astype(BF16)
+        for side in range(2):
+            out_ref[j, :, side * hidden : (side + 1) * hidden] = totals[2 * j + side].astype(BF16)
+
+
+def held(value):
+    return pl.BlockSpec(value.shape, lambda i: (0, 0), pipeline_mode=pl.Buffered(1))
 
 
 def gate_up_gradient(xs, gates, ups, local):
-    rows, width = xs[0].shape
-    chunks = len(xs)
+    width = xs[0].shape[1]
     piece = width // 4
-    whole = pl.BlockSpec((rows, width), lambda i: (0, 0), pipeline_mode=pl.Buffered(1))
+    rows = sum(x.shape[0] for x in xs)
     return pl.pallas_call(
-        functools.partial(columns_kernel, chunks, local),
+        functools.partial(columns_kernel, len(xs), len(gates), local),
         grid=(4,),
-        in_specs=[pl.BlockSpec((rows, piece), lambda i: (0, i))] * chunks + [whole] * (2 * chunks),
+        in_specs=[pl.BlockSpec((x.shape[0], piece), lambda i: (0, i)) for x in xs]
+        + [held(value) for value in (*gates, *ups)],
         out_specs=pl.BlockSpec((local, piece, width), lambda i: (0, i, 0)),
         out_shape=jax.ShapeDtypeStruct((local, width, width), BF16),
         compiler_params=pltpu.CompilerParams(vmem_limit_bytes=VMEM_LIMIT),
         cost_estimate=pl.CostEstimate(
-            flops=4 * chunks * rows * width * width, bytes_accessed=chunks * rows * width * 6, transcendentals=0
+            flops=4 * rows * width * width, bytes_accessed=rows * width * 6, transcendentals=0
         ),
         name="gate_up_gradient",
     )(*xs, *gates, *ups)
 
 
-def down_kernel(chunks, *refs):
+def down_kernel(groups, chunks, *refs):
+    acts, dys, out_ref = refs[:groups], refs[groups : groups + chunks], refs[groups + chunks]
     total = None
-    for act_ref, dy_ref in zip(refs[:chunks], refs[chunks : 2 * chunks]):
-        dy = dy_ref[...].reshape(act_ref.shape[0], dy_ref.shape[2])
+    for act_ref, dy in zip(acts, grouped(dys, acts)):
         part = product_tn(act_ref[...], dy)
         total = part if total is None else total + part
-    refs[2 * chunks][...] = total.astype(BF16)
-
-
-def down_gradient(acts, every_dy, local):
-    rows, width = acts[0].shape
-    chunks = len(acts)
-    peers = every_dy.shape[0]
+    out_ref[...] = total.astype(BF16)
+
+
+def down_gradient(acts, dys, local):
+    width = acts[0].shape[1]
     piece = width // 4
-
-    def spec(chunk):
-        return pl.BlockSpec(
-            (peers, rows // peers, width),
-            lambda i: (0, chunk, 0),
-            pipeline_mode=pl.Buffered(1),
-        )
-
+    rows = sum(act.shape[0] for act in acts)
     return pl.pallas_call(
-        functools.partial(down_kernel, chunks),
+        functools.partial(down_kernel, len(acts), len(dys)),
         grid=(4,),
-        in_specs=[pl.BlockSpec((rows, piece), lambda i: (0, i))] * chunks
-        + [spec(chunk) for chunk in range(chunks)],
+        in_specs=[pl.BlockSpec((act.shape[0], piece), lambda i: (0, i)) for act in acts]
+        + [held(dy) for dy in dys],
         out_specs=pl.BlockSpec((piece, width), lambda i: (i, 0)),
         out_shape=jax.ShapeDtypeStruct((width, width), BF16),
         compiler_params=pltpu.CompilerParams(vmem_limit_bytes=VMEM_LIMIT),
         cost_estimate=pl.CostEstimate(
-            flops=2 * chunks * rows * width * width, bytes_accessed=chunks * rows * width * 4, transcendentals=0
+            flops=2 * rows * width * width, bytes_accessed=rows * width * 4, transcendentals=0
         ),
         name="down_gradient",
-    )(*acts, *([every_dy] * chunks)).reshape(local, width // local, width)
+    )(*acts, *dys).reshape(local, width // local, width)
 
 
 def row_copies(place_ref, pieces, target, sem):
@@ -589,7 +697,7 @@
     logit_grad = (
         gates * (gate_grad - jnp.sum(gates * gate_grad, axis=1, keepdims=True))
     ).astype(BF16)
-    rows = jnp.concatenate([part[...] for part in sums], axis=0).astype(F32)
+    rows = sum(part[...].astype(F32) for part in sums)
     mixed_grad = product_transposed_right(logit_grad, router_ref[...]) + rows
     state = state_ref[...]
     scale = scale_of(state)
@@ -687,34 +795,19 @@
     first_pieces, first_places = fetch_rows(
         jnp.concatenate([w_query, key_weight, value_weight, small], axis=1)
     )
-    out_pieces, out_places = fetch_rows(w_out)
+    out_pieces, out_places = fetch_rows(w_out, first_pieces[-1])
     packed = jnp.concatenate([jnp.concatenate([w_gate, w_up], axis=2), w_down], axis=1)
-    pieces = gather_pieces(packed)
-
+    weights = fetch_experts(packed, out_pieces[-1])
+
+    every_dy = gather_layers(cotangent)
+    every_dy = [value for mine in every_dy for value in (mine, swap_cores(mine))]
     expert_ids = jnp.arange(experts, dtype=jnp.int32)
-    chosen = jnp.any(routes[:, :, None] == expert_ids[None, None, :], axis=1)
-    mask_rows = total_rows * experts // model_width
-    mask_space = -(-mask_rows // 16) * 16
-    every_dy = lax.all_gather(
-        jnp.concatenate(
-            [
-                cotangent,
-                jnp.pad(
-                    chosen.astype(BF16).reshape(mask_rows, model_width),
-                    ((0, mask_space - mask_rows), (0, 0)),
-                ),
-            ],
-            axis=0,
-        ),
-        "expert",
-        axis=0,
-    )
+    chosen = jnp.any(routes[:, :, None] == expert_ids[None, None, :], axis=1).astype(BF16)
+    every_mask = lax.all_gather(chosen.reshape(-1, model_width), "expert", axis=0)
     every_mask = jnp.pad(
-        every_dy[:, total_rows : total_rows + mask_rows].reshape(peers, total_rows, experts),
-        ((0, 0), (0, 0), (0, LANES - experts)),
-    )
-
-    own_mask = jnp.pad(chosen.astype(BF16), ((0, 0), (0, LANES - experts)))
+        every_mask.reshape(peers, total_rows, experts), ((0, 0), (0, 0), (0, LANES - experts))
+    )
+    own_mask = jnp.pad(chosen, ((0, 0), (0, LANES - experts)))
 
     doc_ends = jnp.cumsum(lengths[0])
     token_index = jnp.arange(total_rows, dtype=jnp.int32)
@@ -764,41 +857,49 @@
         SMALL_COST,
     )
 
-    part = total_rows // CHUNKS
-    every_x, out_part, row_part, act, gate_back, up_back, scores_part = [], [], [], [], [], [], []
-    for chunk in range(CHUNKS):
-        gathered = lax.all_gather(
-            mixed_in[chunk * part : (chunk + 1) * part], "expert", axis=0, tiled=True
+    mixed_in, tied_dy, tied_weights = lax.optimization_barrier((mixed_in, every_dy, weights[0]))
+    every_dy, weights = tied_dy, (tied_weights, *weights[1:])
+    every_x = gather_layers(mixed_in)
+    every_x = [value for mine in every_x for value in (mine, swap_cores(mine))]
+    layers = peers // 2
+    groups = [[0], [1], list(range(2, layers))]
+    out_mine, out_other, row_mine, row_other, acts, gate_back, up_back, scores = (
+        [] for _ in range(8)
+    )
+    kept = (out_mine, out_other, row_mine, row_other, acts, gate_back, up_back, scores)
+    for flips in groups:
+        here = slice(2 * flips[0], 2 * flips[-1] + 2)
+        results = run_experts(
+            flips, every_x[here], every_dy[here], every_mask, router_lanes, weights
         )
-        results = run_experts(gathered, every_dy, every_mask, router_lanes, pieces, chunk)
-        every_x.append(gathered)
-        for kept, result in zip((out_part, row_part, act, gate_back, up_back, scores_part), results):
-            kept.append(result)
-    row_sum = [
-        lax.psum_scatter(rows, "expert", scatter_dimension=0, tiled=True) for rows in row_part
-    ]
-    sent_scores = jnp.concatenate(
-        [
-            values[:, :local_experts].reshape(peers, -1, LANES)
-            for values in scores_part
-        ],
-        axis=1,
-    )
+        for values, result in zip(kept, results):
+            values.append(result)
+
+    def by_flip(values):
+        return [piece for value in values for piece in jnp.split(value, value.shape[0] // total_rows)]
+
+    row_terms = sum_layers(by_flip(row_mine), row_other)
+    sent_scores = jnp.concatenate([value[:, :local_experts] for value in scores], axis=0)
+    sent_scores = sent_scores.reshape(peers, -1, LANES)
+    me = lax.axis_index("expert")
+    for bit in range(peers.bit_length() - 1):
+        split = sent_scores.reshape(peers >> (bit + 1), 2, 1 << bit, -1, LANES)
+        split = jnp.where((me >> bit) % 2 == 1, split[:, ::-1], split)
+        sent_scores = split.reshape(peers, -1, LANES)
     gate_grad = lax.all_to_all(sent_scores, "expert", split_axis=0, concat_axis=0, tiled=True)
     gate_grad = (
         gate_grad.reshape(peers, total_rows, local_experts)
         .transpose(1, 0, 2)
         .reshape(total_rows, experts)
     )
-    *out_part, row_last = lax.optimization_barrier((*out_part, row_sum[-1]))
-    row_sum[-1] = row_last
-    out_sum = [lax.psum_scatter(rows, "expert", scatter_dimension=0, tiled=True) for rows in out_part]
-
-    down_grad = down_gradient(act, every_dy, local_experts)
+    down_grad = down_gradient(acts, every_dy, local_experts)
     gu_grad = gate_up_gradient(every_x, gate_back, up_back, local_experts)
+    row_terms, gate_grad, _ = lax.optimization_barrier((row_terms, gate_grad, gu_grad))
+    out_mine, out_other, _ = lax.optimization_barrier((out_mine, out_other, row_terms[-1]))
+    out_terms = sum_layers(by_flip(out_mine), out_other)
 
     state_grad, attended_grad, pack = simple_call(
-        functools.partial(mix_back_kernel, len(out_pieces), CHUNKS, experts),
+        functools.partial(mix_back_kernel, len(out_pieces), len(row_terms), experts),
         "mix_back",
         out_places,
         [
@@ -810,7 +911,7 @@
             jnp.pad(gate_grad, ((0, 0), (0, LANES - experts))),
             router_lanes,
             gains,
-            *row_sum,
+            *row_terms,
         ],
         out_pieces,
         [
@@ -845,7 +946,7 @@
     expert_up_sum = gu_sum[:, :, hidden:]
     late = sum_everywhere(late_pack)
     state, _ = lax.optimization_barrier((state, value_back))
-    output = state + jnp.concatenate(out_sum, axis=0).astype(F32)
+    output = state + sum(value.astype(F32) for value in out_terms)
     q_end = q_width
     return (
         output.astype(BF16),

time: 525 us -> 707 us (1.35)
  starting transfers between devices: 52.9 us -> 149 us
  blocking collectives: 0 us -> 29 us
  waiting for transfers between devices: 200 us -> 223 us
  Pallas kernels: 192 us -> 214 us
  local copies, waits for them, and re-layouts: 30.9 us -> 45.3 us
  between operations: 15.5 us -> 2.23 us
  other arithmetic: 25.1 us -> 35.1 us
    ppermute x33 -> x48, starting transfers between devices: 47 us -> 141 us  [the longest x24 112 us: flip_layer(): lax.ppermute(value, 'expert', [(i, i ^ 2 * flip) for i in range(size)])]
    ppermute x33 -> x48, waiting for transfers between devices: 170 us -> 221 us  [the longest x24 148 us: flip_layer(): lax.ppermute(value, 'expert', [(i, i ^ 2 * flip) for i in range(size)])]
    reduce_scatter x4 -> x0, waiting for transfers between devices: 29.8 us -> none  [per_device(): lax.psum_scatter(rows, 'expert', scatter_dimension=0, tiled=True)]
    all_gather x0 -> x1, blocking collectives: none -> 29 us  [per_device(): lax.all_gather(chosen.reshape(-1, model_width), 'expert', axis=0)]
    pallas_call x4 -> x5, Pallas kernels: 128 us -> 149 us  [the longest x3 109 us: run_experts(): pl.pallas_call(functools.partial(expert_kernel, sources, pairs, len(array...]
    unnamed x48 -> x107, local copies, waits for them, and re-layouts: 2.13 us -> 10.3 us
  transfers between devices with their start and end apart: 51 -> 75, of which waited for: 24 -> 27; matrix products, arithmetic and copies ran while one was open for 9% -> 9% of each run, Pallas kernels for 37% -> 31%
where the time goes in v4:
time: 707 us; the launch traced here: 698 us
  waiting for transfers between devices  223 us (32%)
  Pallas kernels  214 us (30%)
  starting transfers between devices  149 us (21%)
  local copies, waits for them, and re-layouts  45.3 us (6%)
  other arithmetic  35.1 us (5%)
  blocking collectives  29 us (4%)
    ppermute x24, waiting for transfers between devices, flip_layer(): lax.ppermute(value, 'expert', [(i, i ^ 2 * flip) for i in range(size)])  148 us
    ppermute x24, starting transfers between devices, flip_layer(): lax.ppermute(value, 'expert', [(i, i ^ 2 * flip) for i in range(size)])  112 us
    pallas_call x3, Pallas kernels, run_experts(): pl.pallas_call(functools.partial(expert_kernel, sources, pairs, len(array...  109 us
    ppermute x24, waiting for transfers between devices, flip_shard(): return lax.ppermute(value, 'shard', [(i, i ^ flip) for i in range(4)])  73.3 us
    pallas_call x4, Pallas kernels, simple_call(): pl.pallas_call(kernel, grid_spec=pltpu.PrefetchScalarGridSpec(num_scalar_...  36.7 us
    ppermute x24, starting transfers between devices, flip_shard(): return lax.ppermute(value, 'shard', [(i, i ^ flip) for i in range(4)])  29.2 us
    all_gather x1, blocking collectives, per_device(): lax.all_gather(chosen.reshape(-1, model_width), 'expert', axis=0)  29 us
    pallas_call x1, Pallas kernels, gate_up_gradient(): pl.pallas_call(functools.partial(columns_kernel, len(xs), len(gates), loc...  26 us
  transfers between devices with their start and end apart: 75, of which 27 were waited for; matrix products, arithmetic and copies ran while one was open for 9% of the time, Pallas kernels for 31%

profile of v4, /device:TPU:0, one launch (start us, length us, event | category | flops | bytes accessed | tf_op | source)
XLA Modules:
  0.0 698.5 jit_solution(3701944596574425474)
XLA Ops:
  8.6 12.6 %collective-permute-done.refs_1_ = bf16[128,2176]{1,0:T(8,128)(2,1)S(1)} collective-permute-done((bf16[128,2176]{1,0:T(8,128)(2,1)S(1)}, bf16[128,2176]{1,0:T(8,128)(2,1)S(1)}, u32[]{:S(2)}, u32[]{:S(2)}) %collective-permute-start) | collective-permute-done | bytes 557088 | tf_op jit(solution)/shard_map/ppermute | solution.py:42
  57.1 24.5 %collective-permute-done.19.refs_6_.refs_9_ = bf16[512,1024]{1,0:T(8,128)(2,1)} collective-permute-done((bf16[512,1024]{1,0:T(8,128)(2,1)S(1)}, bf16[512,1024]{1,0:T(8,128)(2,1)}, u32[]{:S(2)}, u32[]{:S(2)}) %collective-permute-start.19) | collective-permute-done | bytes 1048608 | tf_op jit(solution)/shard_map/ppermute | solution.py:47
  82.8 9.8 %collective-permute-start.20 = (bf16[256,1024]{1,0:T(8,128)(2,1)S(1)}, bf16[256,1024]{1,0:T(8,128)(2,1)S(1)}, u32[]{:S(2)}, u32[]{:S(2)}) collective-permute-start(bf16[256,1024]{1,0:T(8,128)(2,1)S(1)} %slice.176), channel_id=1, source_target_pairs={{0,8},{4,12},{8,0},{12,4},{16,24},{20,28},{24,16},{28,20},{1,9},{5... | collective-permute-start | bytes 1572872 | tf_op jit(solution)/shard_map/ppermute | solution.py:47
  107.5 10.9 %collective-permute-done.21 = bf16[256,1024]{1,0:T(8,128)(2,1)S(1)} collective-permute-done((bf16[256,1024]{1,0:T(8,128)(2,1)S(1)}, bf16[256,1024]{1,0:T(8,128)(2,1)S(1)}, u32[]{:S(2)}, u32[]{:S(2)}) %collective-permute-start.21) | collective-permute-done | bytes 524320 | tf_op jit(solution)/shard_map/ppermute | solution.py:47
  137.9 13.6 %attend.1 = (bf16[512,1024]{1,0:T(8,128)(2,1)}, f32[32,512]{1,0:T(8,128)}) custom-call(s32[1,512]{1,0:T(1,128)} %bitcast.80, bf16[512,1024]{1,0:T(8,128)(2,1)} %get-tuple-element.85.q_ref, bf16[512,512]{1,0:T(8,128)(2,1)} %get-tuple-element.86.k_ref, bf16[512,512]{1,0:T(8,128)(2,1)} %get-tuple-element.87.v_ref), custom_call_target="tpu_custom_call" | custom-call | tf_op jit(solution)/shard_map/attend/pallas_call | solution.py:625
  161.3 25.7 %collective-permute-done.33.refs_2_.refs_6_ = bf16[512,1024]{1,0:T(8,128)(2,1)S(1)} collective-permute-done((bf16[512,1024]{1,0:T(8,128)(2,1)}, bf16[512,1024]{1,0:T(8,128)(2,1)S(1)}, u32[]{:S(2)}, u32[]{:S(2)}) %collective-permute-start.33) | collective-permute-done | bytes 1048608 | tf_op jit(solution)/shard_map/ppermute | solution.py:47
  187.0 20.7 %collective-permute-start.34 = (bf16[256,1024]{1,0:T(8,128)(2,1)S(1)}, bf16[256,1024]{1,0:T(8,128)(2,1)S(1)}, u32[]{:S(2)}, u32[]{:S(2)}) collective-permute-start(bf16[256,1024]{1,0:T(8,128)(2,1)S(1)} %slice.182), channel_id=1, source_target_pairs={{0,8},{4,12},{8,0},{12,4},{16,24},{20,28},{24,16},{28,20},{1,9},{5... | collective-permute-start | bytes 1572872 | tf_op jit(solution)/shard_map/ppermute | solution.py:47
  211.5 29.0 %all_gather.3 = bf16[8,8,1024]{2,1,0:T(8,128)(2,1)S(1)} all-gather(bf16[1,8,1024]{2,1,0:T(8,128)(2,1)S(1)} %reshape.116), channel_id=1, replica_groups=mesh['expert'=8,'shard'=4] {'expert'}, dimensions={0}, use_global_device_ids=true | all-gather | bytes 147456 | tf_op jit(solution)/shard_map/all_gather | solution.py:806
  245.0 29.0 %experts.3 = (bf16[512,1024]{1,0:T(8,128)(2,1)}, bf16[512,1024]{1,0:T(8,128)(2,1)}, bf16[512,1024]{1,0:T(8,128)(2,1)}, bf16[512,1024]{1,0:T(8,128)(2,1)}, bf16[1...) custom-call(s32[7]{0:T(128)} %stack.112.place_ref, ...), custom_call_target="tpu_custom_call" | custom-call | flops 12884901888 | bytes 14680064 | tf_op jit(solution)/shard_map/experts/pallas_call | solution.py:308
  276.6 50.1 %experts.5 = (bf16[1024,1024]{1,0:T(8,128)(2,1)}, bf16[1024,1024]{1,0:T(8,128)(2,1)}, bf16[1024,1024]{1,0:T(8,128)(2,1)}, bf16[1024,1024]{1,0:T(8,128)(2,1)}, bf...) custom-call(s32[9]{0:T(128)} %stack.120.place_ref, ...), custom_call_target="tpu_custom_call" | custom-call | flops 25769803776 | bytes 29360128 | tf_op jit(solution)/shard_map/experts/pallas_call | solution.py:308
  327.2 29.4 %experts.4 = (bf16[512,1024]{1,0:T(8,128)(2,1)}, bf16[512,1024]{1,0:T(8,128)(2,1)}, bf16[512,1024]{1,0:T(8,128)(2,1)}, bf16[512,1024]{1,0:T(8,128)(2,1)}, bf16[1...) custom-call(s32[7]{0:T(128)} %stack.115.place_ref, ...), custom_call_target="tpu_custom_call" | custom-call | flops 12884901888 | bytes 14680064 | tf_op jit(solution)/shard_map/experts/pallas_call | solution.py:308
  382.6 9.0 %collective-permute-start.40 = (bf16[512,1024]{1,0:T(8,128)(2,1)}, bf16[512,1024]{1,0:T(8,128)(2,1)}, u32[]{:S(2)}, u32[]{:S(2)}) collective-permute-start(bf16[512,1024]{1,0:T(8,128)(2,1)} %pad_maximum_fusion.2), channel_id=1, source_target_pairs={{0,8},{4,12},{8,0},{12,4},{16,24},{20,28},{24,16},{28,20},{1,9},{5... | collective-permute-start | bytes 3145736 | tf_op jit(solution)/shard_map/ppermute | solution.py:47
  395.2 26.0 %gate_up_gradient.1 = bf16[2,1024,1024]{2,1,0:T(8,128)(2,1)} custom-call(bf16[512,1024]{1,0:T(8,128)(2,1)} %get-tuple-element.95.refs_0_.mixed_ref, bf16[512,1024]{1,0:T(8,128)(2,1)} %collective-permute-done.28.refs_1_, bf16[512,1024]{1,0:T(8,128)(2,1)} %copy-done.36, bf16[512,1024]{1,0:T(8,128)(2,1)} %collective-permute-done.31.refs_1_.refs_3_, ...), custom_call_target="tpu_custom_call" | custom-call | flops 17179869184 | bytes 25165824 | tf_op jit(solution)/shard_map/gate_up_gradient/pallas_call | solution.py:376
  429.3 9.9 %collective-permute-done.42.refs_3_ = bf16[512,1024]{1,0:T(8,128)(2,1)} collective-permute-done((bf16[512,1024]{1,0:T(8,128)(2,1)}, bf16[512,1024]{1,0:T(8,128)(2,1)}, u32[]{:S(2)}, u32[]{:S(2)}) %collective-permute-start.42) | collective-permute-done | bytes 1048608 | tf_op jit(solution)/shard_map/ppermute | solution.py:47
  440.1 10.5 %mix_back.1 = (f32[512,1024]{1,0:T(8,128)}, bf16[512,1024]{1,0:T(8,128)(2,1)}, bf16[1024,1152]{1,0:T(8,128)(2,1)}) custom-call(s32[9]{0:T(128)} %stack.105.place_ref, bf16[512,1024]{1,0:T(8,128)(2,1)} %get-tuple-element.88.attended_ref, f32[512,1024]{1,0:T(8,128)} %get-tuple-element.133.state_ref, bf16[512,1024]{1,0:T(8,128)(2,1)} %get-tuple-element.95.refs_0_.mixed_ref, ...), custom_call_target="tpu_custom_call" | custom-call | tf_op jit(solution)/shard_map/mix_back/pallas_call | solution.py:487
  453.9 14.6 %down_gradient.1 = bf16[1024,1024]{1,0:T(8,128)(2,1)} custom-call(bf16[1024,1024]{1,0:T(8,128)(2,1)} %get-tuple-element.154.refs_0_, bf16[1024,1024]{1,0:T(8,128)(2,1)} %get-tuple-element.155.refs_1_, bf16[2048,1024]{1,0:T(8,128)(2,1)} %get-tuple-element.156.refs_2_, bf16[512,1024]{1,0:T(8,128)(2,1)} %refs_3_, bf16[512,1024]{1,0:T(8,128)(2,1)} %copy-done.43, ...), custom_call_target="tpu_custom_call" | custom-call | flops 8589934592 | bytes 16777216 | tf_op jit(solution)/shard_map/down_gradient/pallas_call | solution.py:404
  473.0 14.7 %attend_back.1 = (bf16[512,1024]{1,0:T(8,128)(2,1)}, bf16[512,512]{1,0:T(8,128)(2,1)}, bf16[512,512]{1,0:T(8,128)(2,1)}) custom-call(s32[1,512]{1,0:T(1,128)} %bitcast.81, bf16[512,1024]{1,0:T(8,128)(2,1)} %get-tuple-element.85.q_ref, bf16[512,512]{1,0:T(8,128)(2,1)} %get-tuple-element.86.k_ref, bf16[512,512]{1,0:T(8,128)(2,1)} %get-tuple-element.87.v_ref, ...), custom_call_target="tpu_custom_call" | custom-call | tf_op jit(solution)/shard_map/attend_back/pallas_call | solution.py:643
  487.6 11.3 %project_back.1 = (bf16[512,1024]{1,0:T(8,128)(2,1)}, bf16[1024,2176]{1,0:T(8,128)(2,1)}) custom-call(s32[9]{0:T(128)} %stack.105.place_ref, bf16[512,1024]{1,0:T(8,128)(2,1)} %get-tuple-element.146.normed_ref, bf16[512,1024]{1,0:T(8,128)(2,1)} %x_ref.5, f32[512,1024]{1,0:T(8,128)} %get-tuple-element.147.state_grad_ref, ...), custom_call_target="tpu_custom_call" | custom-call | tf_op jit(solution)/shard_map/project_back/pallas_call | solution.py:487
  517.7 12.4 %collective-permute-done.61 = bf16[1,128,1152]{1,2,0:T(8,128)(2,1)S(1)} collective-permute-done((bf16[1,128,1152]{1,2,0:T(8,128)(2,1)S(1)}, bf16[1,128,1152]{1,2,0:T(8,128)(2,1)S(1)}, u32[]{:S(2)}, u32[]{:S(2)}) %collective-permute-start.61) | collective-permute-done | bytes 294944 | tf_op jit(solution)/shard_map/ppermute | solution.py:42
  558.3 8.8 %collective-permute-done.64 = bf16[64,1152]{0,1:T(8,128)(2,1)S(1)} collective-permute-done((bf16[64,1152]{0,1:T(8,128)(2,1)S(1)}, bf16[64,1152]{0,1:T(8,128)(2,1)S(1)}, u32[]{:S(2)}, u32[]{:S(2)}) %collective-permute-start.64) | collective-permute-done | bytes 147488 | tf_op jit(solution)/shard_map/ppermute | solution.py:47
  588.1 9.2 %collective-permute-done.52 = bf16[1,128,2176]{2,1,0:T(8,128)(2,1)S(1)} collective-permute-done((bf16[1,128,2176]{2,1,0:T(8,128)(2,1)S(1)}, bf16[1,128,2176]{2,1,0:T(8,128)(2,1)S(1)}, u32[]{:S(2)}, u32[]{:S(2)}) %collective-permute-start.52) | collective-permute-done | bytes 557088 | tf_op jit(solution)/shard_map/ppermute | solution.py:42
  609.7 8.1 %collective-permute-done.56 = bf16[64,2176]{1,0:T(8,128)(2,1)S(1)} collective-permute-done((bf16[64,2176]{1,0:T(8,128)(2,1)S(1)}, bf16[64,2176]{1,0:T(8,128)(2,1)S(1)}, u32[]{:S(2)}, u32[]{:S(2)}) %collective-permute-start.56) | collective-permute-done | bytes 278560 | tf_op jit(solution)/shard_map/ppermute | solution.py:47
  617.9 32.0 %collective-permute-start.57 = (bf16[64,2176]{1,0:T(8,128)(2,1)S(1)}, bf16[64,2176]{1,0:T(8,128)(2,1)S(1)}, u32[]{:S(2)}, u32[]{:S(2)}) collective-permute-start(bf16[64,2176]{1,0:T(8,128)(2,1)S(1)} %get-tuple-element.263), channel_id=1, source_target_pairs={{0,8},{4,12},{8,0},{12,4},{16,24},{20,28},{24,16},{28,20},{1,9},{5... | collective-permute-start | bytes 835592 | tf_op jit(solution)/shard_map/ppermute | solution.py:47
  657.5 26.3 %collective-permute-done.55 = bf16[64,2176]{1,0:T(8,128)(2,1)S(1)} collective-permute-done((bf16[64,2176]{1,0:T(8,128)(2,1)S(1)}, bf16[64,2176]{1,0:T(8,128)(2,1)S(1)}, u32[]{:S(2)}, u32[]{:S(2)}) %collective-permute-start.55) | collective-permute-done | bytes 278560 | tf_op jit(solution)/shard_map/ppermute | solution.py:47
  (346 shorter events, 248.0 us)
Async XLA Ops:
  43.1 38.6 %collective-permute-start.19 = (bf16[512,1024]{1,0:T(8,128)(2,1)S(1)}, bf16[512,1024]{1,0:T(8,128)(2,1)}, u32[]{:S(2)}, u32[]{:S(2)}) collective-permute-start(bf16[512,1024]{1,0:T(8,128)(2,1)S(1)} %copy-done.17), channel_id=1, source_target_pairs={{0,24},{4,28},{8,16},{12,20},{16,8},{20,12},{24,0},{28,4},{1,25},{... | collective-permute-start | bytes 3145736 | tf_op jit(solution)/shard_map/ppermute | solution.py:47
  49.6 70.3 %collective-permute-start.24 = (bf16[2,384,1024]{2,1,0:T(8,128)(2,1)S(1)}, bf16[2,384,1024]{2,1,0:T(8,128)(2,1)S(1)}, u32[]{:S(2)}, u32[]{:S(2)}) collective-permute-start(bf16[2,384,1024]{2,1,0:T(8,128)(2,1)S(1)} %pad_maximum_fusion.1.refs_4_.refs_8_), channel_id=1, source_target_pairs={{0,1},{1,0},{2,3},{3,2},{4,5},{5,4},{6,7},{7,6},{8,9},{9,8},{10,11... | collective-permute-start | bytes 4718600 | tf_op jit(solution)/shard_map/ppermute | solution.py:42
  55.9 64.4 %collective-permute-start.25 = (bf16[2,384,1024]{2,1,0:T(8,128)(2,1)S(1)}, bf16[2,384,1024]{2,1,0:T(8,128)(2,1)S(1)}, u32[]{:S(2)}, u32[]{:S(2)}) collective-permute-start(bf16[2,384,1024]{2,1,0:T(8,128)(2,1)S(1)} %pad_maximum_fusion.1.refs_4_.refs_8_), channel_id=1, source_target_pairs={{0,2},{1,3},{2,0},{3,1},{4,6},{5,7},{6,4},{7,5},{8,10},{9,11},{10,... | collective-permute-start | bytes 4718600 | tf_op jit(solution)/shard_map/ppermute | solution.py:42
  119.3 39.5 %collective-permute-start.18 = (bf16[512,1024]{1,0:T(8,128)(2,1)}, bf16[512,1024]{1,0:T(8,128)(2,1)}, u32[]{:S(2)}, u32[]{:S(2)}) collective-permute-start(bf16[512,1024]{1,0:T(8,128)(2,1)} %collective-permute-done.17.refs_2_.refs_5_), channel_id=1, source_target_pairs={{0,4},{4,0},{8,12},{12,8},{16,20},{20,16},{24,28},{28,24},{1,5},{5... | collective-permute-start | bytes 3145736 | tf_op jit(solution)/shard_map/ppermute | solution.py:52
  119.9 38.9 %collective-permute-start.23 = (bf16[512,1024]{1,0:T(8,128)(2,1)}, bf16[512,1024]{1,0:T(8,128)(2,1)}, u32[]{:S(2)}, u32[]{:S(2)}) collective-permute-start(bf16[512,1024]{1,0:T(8,128)(2,1)} %collective-permute-done.19.refs_6_.refs_9_), channel_id=1, source_target_pairs={{0,4},{4,0},{8,12},{12,8},{16,20},{20,16},{24,28},{28,24},{1,5},{5... | collective-permute-start | bytes 3145736 | tf_op jit(solution)/shard_map/ppermute | solution.py:52
  160.6 47.6 %collective-permute-start.30 = (bf16[512,1024]{1,0:T(8,128)(2,1)}, bf16[512,1024]{1,0:T(8,128)(2,1)S(1)}, u32[]{:S(2)}, u32[]{:S(2)}) collective-permute-start(bf16[512,1024]{1,0:T(8,128)(2,1)} %get-tuple-element.95.refs_0_.mixed_ref), channel_id=1, source_target_pairs={{0,8},{4,12},{8,0},{12,4},{16,24},{20,28},{24,16},{28,20},{1,9},{5... | collective-permute-start | bytes 3145736 | tf_op jit(solution)/shard_map/ppermute | solution.py:47
  161.3 83.8 %collective-permute-start.28 = (bf16[512,1024]{1,0:T(8,128)(2,1)}, bf16[512,1024]{1,0:T(8,128)(2,1)}, u32[]{:S(2)}, u32[]{:S(2)}) collective-permute-start(bf16[512,1024]{1,0:T(8,128)(2,1)} %get-tuple-element.95.refs_0_.mixed_ref), channel_id=1, source_target_pairs={{0,4},{4,0},{8,12},{12,8},{16,20},{20,16},{24,28},{28,24},{1,5},{5... | collective-permute-start | bytes 3145736 | tf_op jit(solution)/shard_map/ppermute | solution.py:52
  187.0 57.6 %collective-permute-start.34 = (bf16[256,1024]{1,0:T(8,128)(2,1)S(1)}, bf16[256,1024]{1,0:T(8,128)(2,1)S(1)}, u32[]{:S(2)}, u32[]{:S(2)}) collective-permute-start(bf16[256,1024]{1,0:T(8,128)(2,1)S(1)} %slice.182), channel_id=1, source_target_pairs={{0,8},{4,12},{8,0},{12,4},{16,24},{20,28},{24,16},{28,20},{1,9},{5... | collective-permute-start | bytes 1572872 | tf_op jit(solution)/shard_map/ppermute | solution.py:47
  274.0 153.7 %collective-permute-start.29 = (bf16[512,1024]{1,0:T(8,128)(2,1)}, bf16[512,1024]{1,0:T(8,128)(2,1)S(1)}, u32[]{:S(2)}, u32[]{:S(2)}) collective-permute-start(bf16[512,1024]{1,0:T(8,128)(2,1)} %get-tuple-element.105), channel_id=1, source_target_pairs={{0,4},{4,0},{8,12},{12,8},{16,20},{20,16},{24,28},{28,24},{1,5},{5... | collective-permute-start | bytes 3145736 | tf_op jit(solution)/shard_map/ppermute | solution.py:52
  274.4 52.7 %collective-permute-start.31 = (bf16[512,1024]{1,0:T(8,128)(2,1)S(1)}, bf16[512,1024]{1,0:T(8,128)(2,1)}, u32[]{:S(2)}, u32[]{:S(2)}) collective-permute-start(bf16[512,1024]{1,0:T(8,128)(2,1)S(1)} %copy-done.37), channel_id=1, source_target_pairs={{0,4},{4,0},{8,12},{12,8},{16,20},{20,16},{24,28},{28,24},{1,5},{5... | collective-permute-start | bytes 3145736 | tf_op jit(solution)/shard_map/ppermute | solution.py:52
  365.5 61.8 %all-to-all-start = ((f32[8,8,128]{2,1,0:T(8,128)}), f32[8,8,128]{2,1,0:T(8,128)S(1)}, u32[]{:S(2)}, u32[]{:S(2)}) async-start(f32[8,8,128]{2,1,0:T(8,128)} %bitcast.27), calls=%async_computation | async-start | bytes 65536 | tf_op jit(solution)/shard_map/all_to_all | solution.py:889
  382.6 46.7 %collective-permute-start.40 = (bf16[512,1024]{1,0:T(8,128)(2,1)}, bf16[512,1024]{1,0:T(8,128)(2,1)}, u32[]{:S(2)}, u32[]{:S(2)}) collective-permute-start(bf16[512,1024]{1,0:T(8,128)(2,1)} %pad_maximum_fusion.2), channel_id=1, source_target_pairs={{0,8},{4,12},{8,0},{12,4},{16,24},{20,28},{24,16},{28,20},{1,9},{5... | collective-permute-start | bytes 3145736 | tf_op jit(solution)/shard_map/ppermute | solution.py:47
  392.8 46.4 %collective-permute-start.42 = (bf16[512,1024]{1,0:T(8,128)(2,1)}, bf16[512,1024]{1,0:T(8,128)(2,1)}, u32[]{:S(2)}, u32[]{:S(2)}) collective-permute-start(bf16[512,1024]{1,0:T(8,128)(2,1)} %pad_maximum_fusion.3), channel_id=1, source_target_pairs={{0,24},{4,28},{8,16},{12,20},{16,8},{20,12},{24,0},{28,4},{1,25},{... | collective-permute-start | bytes 3145736 | tf_op jit(solution)/shard_map/ppermute | solution.py:47
  425.3 80.1 %collective-permute-start.70 = (bf16[2,256,1024]{2,1,0:T(8,128)(2,1)}, bf16[2,256,1024]{2,1,0:T(8,128)(2,1)}, u32[]{:S(2)}, u32[]{:S(2)}) collective-permute-start(bf16[2,256,1024]{2,1,0:T(8,128)(2,1)} %get-tuple-element.234), channel_id=1, source_target_pairs={{0,3},{1,2},{2,1},{3,0},{4,7},{5,6},{6,5},{7,4},{8,11},{9,10},{10,... | collective-permute-start | bytes 3145736 | tf_op jit(solution)/shard_map/ppermute | solution.py:42
  426.8 81.1 %collective-permute-start.69 = (bf16[2,256,1024]{2,1,0:T(8,128)(2,1)}, bf16[2,256,1024]{2,1,0:T(8,128)(2,1)}, u32[]{:S(2)}, u32[]{:S(2)}) collective-permute-start(bf16[2,256,1024]{2,1,0:T(8,128)(2,1)} %get-tuple-element.235), channel_id=1, source_target_pairs={{0,2},{1,3},{2,0},{3,1},{4,6},{5,7},{6,4},{7,5},{8,10},{9,11},{10,... | collective-permute-start | bytes 3145736 | tf_op jit(solution)/shard_map/ppermute | solution.py:42
  427.8 80.6 %collective-permute-start.68 = (bf16[2,256,1024]{2,1,0:T(8,128)(2,1)}, bf16[2,256,1024]{2,1,0:T(8,128)(2,1)}, u32[]{:S(2)}, u32[]{:S(2)}) collective-permute-start(bf16[2,256,1024]{2,1,0:T(8,128)(2,1)} %get-tuple-element.236), channel_id=1, source_target_pairs={{0,1},{1,0},{2,3},{3,2},{4,5},{5,4},{6,7},{7,6},{8,9},{9,8},{10,11... | collective-permute-start | bytes 3145736 | tf_op jit(solution)/shard_map/ppermute | solution.py:42
  453.9 49.2 %collective-permute-start.59 = (bf16[4,128,1152]{1,2,0:T(8,128)(2,1)}, bf16[4,128,1152]{1,2,0:T(8,128)(2,1)}, u32[]{:S(2)}, u32[]{:S(2)}) collective-permute-start(bf16[4,128,1152]{1,2,0:T(8,128)(2,1)} %bitcast.74), channel_id=1, source_target_pairs={{0,4},{4,0},{8,12},{12,8},{16,20},{20,16},{24,28},{28,24},{1,5},{5... | collective-permute-start | bytes 3538952 | tf_op jit(solution)/shard_map/ppermute | solution.py:52
  471.5 75.1 %collective-permute-start.73 = (bf16[2,128,1024]{2,1,0:T(8,128)(2,1)}, bf16[2,128,1024]{2,1,0:T(8,128)(2,1)}, u32[]{:S(2)}, u32[]{:S(2)}) collective-permute-start(bf16[2,128,1024]{2,1,0:T(8,128)(2,1)} %get-tuple-element.247), channel_id=1, source_target_pairs={{0,3},{1,2},{2,1},{3,0},{4,7},{5,6},{6,5},{7,4},{8,11},{9,10},{10,... | collective-permute-start | bytes 1572872 | tf_op jit(solution)/shard_map/ppermute | solution.py:42
  503.1 44.0 %collective-permute-start.72 = (bf16[2,128,1024]{2,1,0:T(8,128)(2,1)}, bf16[2,128,1024]{2,1,0:T(8,128)(2,1)S(1)}, u32[]{:S(2)}, u32[]{:S(2)}) collective-permute-start(bf16[2,128,1024]{2,1,0:T(8,128)(2,1)} %get-tuple-element.248), channel_id=1, source_target_pairs={{0,2},{1,3},{2,0},{3,1},{4,6},{5,7},{6,4},{7,5},{8,10},{9,11},{10,... | collective-permute-start | bytes 1572872 | tf_op jit(solution)/shard_map/ppermute | solution.py:42
  546.6 143.0 %collective-permute-start.43 = (bf16[512,1024]{1,0:T(8,128)(2,1)}, bf16[512,1024]{1,0:T(8,128)(2,1)}, u32[]{:S(2)}, u32[]{:S(2)}) collective-permute-start(bf16[512,1024]{1,0:T(8,128)(2,1)} %get-tuple-element.141), channel_id=1, source_target_pairs={{0,4},{4,0},{8,12},{12,8},{16,20},{20,16},{24,28},{28,24},{1,5},{5... | collective-permute-start | bytes 3145736 | tf_op jit(solution)/shard_map/ppermute | solution.py:52
  586.5 63.3 %collective-permute-start.46 = (bf16[256,1024]{1,0:T(8,128)(2,1)S(1)}, bf16[256,1024]{1,0:T(8,128)(2,1)S(1)}, u32[]{:S(2)}, u32[]{:S(2)}) collective-permute-start(bf16[256,1024]{1,0:T(8,128)(2,1)S(1)} %get-tuple-element.256), channel_id=1, source_target_pairs={{0,24},{4,28},{8,16},{12,20},{16,8},{20,12},{24,0},{28,4},{1,25},{... | collective-permute-start | bytes 1572872 | tf_op jit(solution)/shard_map/ppermute | solution.py:47
  605.4 84.2 %collective-permute-start.49 = (bf16[512,1024]{1,0:T(8,128)(2,1)}, bf16[512,1024]{1,0:T(8,128)(2,1)}, u32[]{:S(2)}, u32[]{:S(2)}) collective-permute-start(bf16[512,1024]{1,0:T(8,128)(2,1)} %pad_maximum_fusion.5), channel_id=1, source_target_pairs={{0,24},{4,28},{8,16},{12,20},{16,8},{20,12},{24,0},{28,4},{1,25},{... | collective-permute-start | bytes 3145736 | tf_op jit(solution)/shard_map/ppermute | solution.py:47
  617.9 39.5 %collective-permute-start.57 = (bf16[64,2176]{1,0:T(8,128)(2,1)S(1)}, bf16[64,2176]{1,0:T(8,128)(2,1)S(1)}, u32[]{:S(2)}, u32[]{:S(2)}) collective-permute-start(bf16[64,2176]{1,0:T(8,128)(2,1)S(1)} %get-tuple-element.263), channel_id=1, source_target_pairs={{0,8},{4,12},{8,0},{12,4},{16,24},{20,28},{24,16},{28,20},{1,9},{5... | collective-permute-start | bytes 835592 | tf_op jit(solution)/shard_map/ppermute | solution.py:47
  651.1 38.5 %collective-permute-start.47 = (bf16[512,1024]{1,0:T(8,128)(2,1)}, bf16[512,1024]{1,0:T(8,128)(2,1)}, u32[]{:S(2)}, u32[]{:S(2)}) collective-permute-start(bf16[512,1024]{1,0:T(8,128)(2,1)} %pad_maximum_fusion.4), channel_id=1, source_target_pairs={{0,8},{4,12},{8,0},{12,4},{16,24},{20,28},{24,16},{28,20},{1,9},{5... | collective-permute-start | bytes 3145736 | tf_op jit(solution)/shard_map/ppermute | solution.py:47
  (102 other events, 2405.1 us)

commit v5 on v3

--- a/solution.py
+++ b/solution.py
@@ -13,8 +13,14 @@
 HEAD_DIM = 64
 LANES = 128
 VMEM_LIMIT = 58 * 1024 * 1024
-CHUNKS = 2
-SMALL_COST = pl.CostEstimate(flops=0, bytes_accessed=0, transcendentals=0)
+
+
+def cost(microseconds):
+    return pl.CostEstimate(
+        flops=int(microseconds * 1.15e9), bytes_accessed=0, transcendentals=0
+    )
+
+
 F32 = jnp.float32
 BF16 = jnp.bfloat16
 
@@ -39,17 +45,13 @@
     return lax.dynamic_index_in_dim(blocks, index, 0, keepdims=False)
 
 
-def gather_pieces(piece):
-    count = lax.axis_size("shard")
-    if count == 4:
-        me = lax.axis_index("shard")
-        pieces = [(piece, me)]
-        for flip in (1, 2, 3):
-            got = lax.ppermute(piece, "shard", [(i, i ^ flip) for i in range(4)])
-            pieces.append((got, me ^ flip))
-        return pieces
-    every = lax.all_gather(piece, "shard", axis=0)
-    return [(every[i], jnp.int32(i)) for i in range(count)]
+def flip_shard(value, flip):
+    return lax.ppermute(value, "shard", [(i, i ^ flip) for i in range(4)])
+
+
+def flip_layer(value, flip):
+    size = lax.axis_size("expert")
+    return lax.ppermute(value, "expert", [(i, i ^ (2 * flip)) for i in range(size)])
 
 
 def swap_cores(value):
@@ -57,7 +59,15 @@
     return lax.ppermute(value, "expert", [(i, i ^ 1) for i in range(size)])
 
 
-def fetch_rows(rows):
+def both_ways(value, first, second, after=None):
+    half = value.shape[0] // 2
+    one, two = first(value), second(value)
+    if after is not None:
+        one, two, _ = lax.optimization_barrier((one, two, after))
+    return one, two, first(two[:half]), second(one[half:])
+
+
+def fetch_rows(rows, before_first=None, before_second=None):
     count = lax.axis_size("shard")
     size = rows.shape[0]
     if count != 4:
@@ -66,92 +76,136 @@
     core = lax.axis_index("expert") % 2
     half = size // 2
     mine = lax.dynamic_slice_in_dim(rows, core * half, half, 0)
+    if before_first is not None:
+        mine, _ = lax.optimization_barrier((mine, before_first))
+    one, two, low, high = both_ways(
+        mine, lambda v: flip_shard(v, 1), lambda v: flip_shard(v, 2), before_second
+    )
     pieces, places = [rows], [me * size]
-    for flip in (1, 2, 3):
-        got = lax.ppermute(mine, "shard", [(i, i ^ flip) for i in range(4)])
-        first = (me ^ flip) * size
+    for got, flip, skip in ((one, 1, 0), (two, 2, 0), (low, 3, 0), (high, 3, half // 2)):
+        first = (me ^ flip) * size + skip
         pieces += [got, swap_cores(got)]
         places += [first + core * half, first + (1 - core) * half]
     return pieces, jnp.stack(places).astype(jnp.int32)
 
 
-def scatter_sum(values, axis, after=None):
+def fetch_experts(packed, before_first, before_second):
     count = lax.axis_size("shard")
-    if count != 4:
-        return lax.psum_scatter(
-            values.astype(BF16), "shard", scatter_dimension=axis, tiled=True
-        ).astype(F32)
+    local = packed.shape[0]
+    if count != 4 or local != 2:
+        every = lax.all_gather(packed, "shard", axis=0)
+        arrays = [every[i] for i in range(count)]
+        sources = [[(i, j, i) for i in range(count)] for j in range(local)]
+        return arrays, sources, [jnp.int32(i) for i in range(count)]
     me = lax.axis_index("shard")
-    size = values.shape[axis] // count
-    own = lax.dynamic_slice_in_dim(values, me * size, size, axis)
-    if after is not None:
-        own, _ = lax.optimization_barrier((own, after))
-    total = own.astype(F32)
-    for flip in (1, 2, 3):
-        sent = lax.dynamic_slice_in_dim(values, (me ^ flip) * size, size, axis).astype(BF16)
-        got = lax.ppermute(sent, "shard", [(i, i ^ flip) for i in range(4)])
-        total = total + got.astype(F32)
-    return total
-
-
-def sum_everywhere(grad):
+    sent, _ = lax.optimization_barrier((packed, before_first))
+    one, two, low, high = both_ways(
+        sent, lambda v: flip_shard(v, 1), lambda v: flip_shard(v, 2), before_second
+    )
+    arrays = [packed, one, two, low, high]
+    sources = [[(0, j, 0), (1, j, 1), (2, j, 2), (3 + j, 0, 3)] for j in range(2)]
+    return arrays, sources, [me, me ^ 1, me ^ 2, me ^ 3]
+
+
+def split_parts(values, axis):
+    me = lax.axis_index("shard")
+    size = values.shape[axis] // lax.axis_size("shard")
+    return [
+        lax.dynamic_slice_in_dim(values, (me ^ flip) * size, size, axis) for flip in range(4)
+    ]
+
+
+def send_far(far):
+    half = far.shape[0] // 2
+    return flip_shard(far[:half], 1), flip_shard(far[half:], 2)
+
+
+def send_near(one, two, low, high):
+    half = one.shape[0] // 2
+    two = jnp.concatenate([(two[:half].astype(F32) + low.astype(F32)).astype(BF16), two[half:]], axis=0)
+    one = jnp.concatenate([one[:half], (one[half:].astype(F32) + high.astype(F32)).astype(BF16)], axis=0)
+    return flip_shard(one, 1), flip_shard(two, 2)
+
+
+def add_up(values):
+    return sum(value.astype(F32) for value in values)
+
+
+def plain_scatter_sum(values, axis):
+    return lax.psum_scatter(values, "shard", scatter_dimension=axis, tiled=True).astype(F32)
+
+
+def pair_cores(grad):
     count = lax.axis_size("shard")
-    size = lax.axis_size("expert")
-    layers = size // 2
-    place = lax.axis_index("expert")
-    core, layer = place % 2, place // 2
+    core = lax.axis_index("expert") % 2
     width = grad.shape[1]
     half = grad.shape[0] // count // 2
     blocks = grad.reshape(count, 2, half, width)
     mine = lax.dynamic_index_in_dim(blocks, core, 1, keepdims=False)
     away = lax.dynamic_index_in_dim(blocks, 1 - core, 1, keepdims=False)
-    paired = mine.astype(F32) + swap_cores(away).astype(F32)
-    local = scatter_sum(paired, 0).reshape(layers, half // layers, width)
-    total = pick(local, layer)
-    for step in range(1, layers):
-        perm = [(i, (i + 2 * step) % size) for i in range(size)]
-        sent = pick(local, (layer + step) % layers).astype(BF16)
-        total = total + lax.ppermute(sent, "expert", perm).astype(F32)
-    total = total.astype(BF16)
-    parts = jnp.zeros((layers, half // layers, width), BF16)
-    parts = lax.dynamic_update_index_in_dim(parts, total, layer, 0)
-    for step in range(1, layers):
-        perm = [(i, (i + 2 * step) % size) for i in range(size)]
-        got = lax.ppermute(total, "expert", perm)
-        parts = lax.dynamic_update_index_in_dim(parts, got, (layer - step) % layers, 0)
-    mine = parts.reshape(half, width)
-    other = swap_cores(mine)
-    low = jnp.where(core == 0, mine, other)
-    high = jnp.where(core == 0, other, mine)
+    return (mine.astype(F32) + swap_cores(away).astype(F32)).astype(BF16)
+
+
+def sum_near(paired):
+    count, half, width = paired.shape
+    if count != 4:
+        return plain_scatter_sum(paired, 0).reshape(half, width).astype(BF16)
+    own, one, two, far = (part.reshape(half, width) for part in split_parts(paired, 0))
+    total = own.astype(F32)
+    for flip, sent in ((1, one), (2, two), (3, far)):
+        total = total + flip_shard(sent, flip).astype(F32)
+    return total.astype(BF16)
+
+
+def sum_far(local):
+    layers = lax.axis_size("expert") // 2
+    core = lax.axis_index("expert") % 2
+    if layers != 4:
+        groups = [[2 * i + side for i in range(layers)] for side in range(2)]
+        total = lax.psum(local, "expert", axis_index_groups=groups)
+    else:
+        half = local.shape[0] // 2
+        low, high = local[:half], local[half:]
+        for order in ((1, 3), (3, 1)):
+            low, high = (
+                (low.astype(F32) + flip_layer(low, order[0]).astype(F32)).astype(BF16),
+                (high.astype(F32) + flip_layer(high, order[1]).astype(F32)).astype(BF16),
+            )
+        total = jnp.concatenate([low, high], axis=0)
+    other = swap_cores(total)
+    low = jnp.where(core == 0, total, other)
+    high = jnp.where(core == 0, other, total)
     return jnp.concatenate([low, high], axis=0).astype(F32)
 
 
-def expert_kernel(count, place_ref, x_ref, dy_ref, mask_ref, router_ref, *refs):
-    pieces = refs[:count]
-    out_ref, row_ref, act_ref, gate_ref, up_ref, score_ref, gu, down, sem = refs[count:]
+def expert_kernel(sources, arrays, place_ref, x_ref, dy_ref, mask_ref, router_ref, *refs):
+    pieces = refs[:arrays]
+    out_ref, row_ref, act_ref, gate_ref, up_ref, score_ref, gu, down, sem = refs[arrays:]
     local, rows, width = pieces[0].shape
     third = rows // 3
     hidden = width // 2
+    count = len(sources[0])
 
     @pl.when(pl.program_id(0) == 0)
     def _():
         copies = []
-        for i in range(count):
-            at = place_ref[i]
-            copies.append(
-                pltpu.make_async_copy(
-                    pieces[i].at[:, pl.ds(0, 2 * third), :],
-                    gu.at[:, pl.ds(pl.multiple_of(at * (2 * third), 16), 2 * third), :],
-                    sem.at[2 * i],
+        for j in range(local):
+            for number, (array, index, slot) in enumerate(sources[j]):
+                at = place_ref[slot]
+                copies.append(
+                    pltpu.make_async_copy(
+                        pieces[array].at[index, pl.ds(0, 2 * third), :],
+                        gu.at[j, pl.ds(pl.multiple_of(at * (2 * third), 16), 2 * third), :],
+                        sem.at[j, number, 0],
+                    )
                 )
-            )
-            copies.append(
-                pltpu.make_async_copy(
-                    pieces[i].at[:, pl.ds(2 * third, third), :],
-                    down.at[:, pl.ds(pl.multiple_of(at * third, 16), third), :],
-                    sem.at[2 * i + 1],
+                copies.append(
+                    pltpu.make_async_copy(
+                        pieces[array].at[index, pl.ds(2 * third, third), :],
+                        down.at[j, pl.ds(pl.multiple_of(at * third, 16), third), :],
+                        sem.at[j, number, 1],
+                    )
                 )
-            )
         for copy in copies:
             copy.start()
         for copy in copies:
@@ -198,20 +252,21 @@
     score_ref[...] = scores
 
 
-def run_experts(every_x, every_dy, mask, router, pieces, chunk):
-    count = len(pieces)
+def run_experts(every_x, every_dy, mask, router, weights, chunk):
+    arrays, sources, places = weights
+    count = len(sources[0])
     total, width = every_x.shape
-    local, rows, _ = pieces[0][0].shape
+    local, rows, _ = arrays[0].shape
     third = rows // 3
     peers = every_dy.shape[0]
     rows_each = total // peers
     group = 2
     tile = group * rows_each
-    place = jnp.stack([index for _, index in pieces] + [lax.axis_index("expert")]).astype(jnp.int32)
+    place = jnp.stack([*places, lax.axis_index("expert")]).astype(jnp.int32)
     block = pl.BlockSpec((tile, width), lambda i, p: (i, 0))
     thin = pl.BlockSpec((tile, LANES), lambda i, p: (i, 0))
     return pl.pallas_call(
-        functools.partial(expert_kernel, count),
+        functools.partial(expert_kernel, sources, len(arrays)),
         grid_spec=pltpu.PrefetchScalarGridSpec(
             num_scalar_prefetch=1,
             grid=(peers // group,),
@@ -221,12 +276,12 @@
                 pl.BlockSpec((group, rows_each, LANES), lambda i, p: (i, chunk, 0)),
                 pl.BlockSpec((width, LANES), lambda i, p: (0, 0)),
             ]
-            + [pl.BlockSpec(memory_space=pl.ANY)] * count,
+            + [pl.BlockSpec(memory_space=pl.ANY)] * len(arrays),
             out_specs=[block, block, block, block, block, thin],
             scratch_shapes=[
                 pltpu.VMEM((local, 2 * third * count, width), BF16),
                 pltpu.VMEM((local, third * count, width), BF16),
-                pltpu.SemaphoreType.DMA((2 * count,)),
+                pltpu.SemaphoreType.DMA((local, count, 2)),
             ],
         ),
         out_shape=[jax.ShapeDtypeStruct((total, width), BF16)] * 5
@@ -236,7 +291,7 @@
             flops=2 * total * width * width * 6, bytes_accessed=total * width * 14, transcendentals=0
         ),
         name="experts",
-    )(place, every_x, every_dy, mask, router, *[piece for piece, _ in pieces])
+    )(place, every_x, every_dy, mask, router, *arrays)
 
 
 def columns_kernel(chunks, local, *refs):
@@ -372,7 +427,7 @@
     ).astype(BF16)
 
 
-def simple_call(kernel, name, prefetch, inputs, pieces, outputs, scratch, cost=None):
+def simple_call(kernel, name, prefetch, inputs, pieces, outputs, scratch, time):
     def whole(shape):
         return pl.BlockSpec(shape, lambda i, p: (0,) * len(shape))
 
@@ -388,7 +443,7 @@
         ),
         out_shape=[jax.ShapeDtypeStruct(shape, kind) for shape, kind in outputs],
         compiler_params=pltpu.CompilerParams(vmem_limit_bytes=VMEM_LIMIT),
-        cost_estimate=cost,
+        cost_estimate=cost(time),
         name=name,
     )(prefetch, *inputs, *pieces)
 
@@ -524,7 +579,7 @@
             jax.ShapeDtypeStruct((8 * steps, rows), F32),
         ],
         compiler_params=pltpu.CompilerParams(vmem_limit_bytes=VMEM_LIMIT),
-        cost_estimate=SMALL_COST,
+        cost_estimate=cost(13),
         name="attend",
     )(start, q, k, v)
 
@@ -543,13 +598,14 @@
             jax.ShapeDtypeStruct(v.shape, BF16),
         ],
         compiler_params=pltpu.CompilerParams(vmem_limit_bytes=VMEM_LIMIT),
+        cost_estimate=cost(15),
         name="attend_back",
     )(start, q, k, v, grad, logs, cosine, sine)
 
 
 def mix_kernel(count, place_ref, attended_ref, x_ref, mask_ref, router_ref, gains_ref, *refs):
     pieces = refs[:count]
-    state_ref, mixed_ref, gates_ref, weight, sem = refs[count:]
+    state_ref, low_ref, high_ref, gates_ref, weight, sem = refs[count:]
     copies = row_copies(place_ref, pieces, weight, sem)
     for copy in copies:
         copy.wait()
@@ -558,7 +614,8 @@
     )
     state_ref[...] = state
     mixed = (state * scale_of(state) * gains_ref[1:2, :]).astype(BF16)
-    mixed_ref[...] = mixed
+    low_ref[...] = mixed[: low_ref.shape[0]]
+    high_ref[...] = mixed[low_ref.shape[0] :]
     logits = jnp.dot(mixed, router_ref[...], preferred_element_type=F32)
     logits = jnp.where(mask_ref[...] > 0, logits, -1e30)
     powers = jnp.exp(logits - jnp.max(logits, axis=1, keepdims=True))
@@ -572,7 +629,8 @@
     place_ref,
     attended_ref,
     state_ref,
-    mixed_ref,
+    low_ref,
+    high_ref,
     dy_ref,
     gates_ref,
     gate_grad_ref,
@@ -606,30 +664,24 @@
     pack_ref[:, :width] = product_tn(attended_ref[...], branch).astype(BF16)
     line = lax.broadcasted_iota(jnp.int32, (LANES, width), 0)
     column = jnp.where(line == experts, gain_grad, 0.0).T
-    pack_ref[:, width:] = (product_tn(mixed_ref[...], logit_grad) + column).astype(BF16)
-
-
-def project_back_kernel(
-    count,
-    place_ref,
-    normed_ref,
-    x_ref,
-    state_grad_ref,
-    gains_ref,
-    qb_ref,
-    kb_ref,
-    vb_ref,
-    *refs,
-):
-    pieces = refs[:count]
-    out_ref, pack_ref, weight, sem = refs[count:]
-    copies = row_copies(place_ref, pieces, weight, sem)
+    pack_ref[:, width:] = (product_tn(jnp.concatenate([low_ref[...], high_ref[...]], axis=0), logit_grad) + column).astype(BF16)
+
+
+def project_weights_kernel(place_ref, normed_ref, qb_ref, kb_ref, vb_ref, pack_ref):
     normed = normed_ref[...]
     at = 0
     for back_ref in (qb_ref, kb_ref, vb_ref):
         width = back_ref.shape[1]
         pack_ref[:, at : at + width] = product_tn(normed, back_ref[...]).astype(BF16)
         at += width
+
+
+def project_back_kernel(
+    count, place_ref, x_ref, state_grad_ref, gains_ref, qb_ref, kb_ref, vb_ref, *refs
+):
+    pieces = refs[:count]
+    out_ref, weight, sem = refs[count:]
+    copies = row_copies(place_ref, pieces, weight, sem)
     for copy in copies:
         copy.wait()
     grad = None
@@ -641,14 +693,11 @@
         first += width
     x = x_ref[...].astype(F32)
     scale = scale_of(x)
-    gain_grad = jnp.sum(grad * (x * scale), axis=0, keepdims=True)
     scaled = gains_ref[0:1, :] * grad
     mean = jnp.mean(scaled * x, axis=1, keepdims=True)
     out_ref[...] = (
         state_grad_ref[...] + scale * scaled - x * (scale * scale * scale * mean)
     ).astype(BF16)
-    line = lax.broadcasted_iota(jnp.int32, (LANES, x.shape[1]), 0)
-    pack_ref[:, at:] = jnp.where(line == 0, gain_grad, 0.0).T.astype(BF16)
 
 
 def per_device(
@@ -687,12 +736,8 @@
     first_pieces, first_places = fetch_rows(
         jnp.concatenate([w_query, key_weight, value_weight, small], axis=1)
     )
-    out_pieces, out_places = fetch_rows(w_out)
-    packed = jnp.concatenate([jnp.concatenate([w_gate, w_up], axis=2), w_down], axis=1)
-    pieces = gather_pieces(packed)
-
     expert_ids = jnp.arange(experts, dtype=jnp.int32)
-    chosen = jnp.any(routes[:, :, None] == expert_ids[None, None, :], axis=1)
+    chosen = jnp.any(routes[:, :, None] == expert_ids[None, None, :], axis=1).astype(BF16)
     mask_rows = total_rows * experts // model_width
     mask_space = -(-mask_rows // 16) * 16
     every_dy = lax.all_gather(
@@ -700,8 +745,7 @@
             [
                 cotangent,
                 jnp.pad(
-                    chosen.astype(BF16).reshape(mask_rows, model_width),
-                    ((0, mask_space - mask_rows), (0, 0)),
+                    chosen.reshape(mask_rows, model_width), ((0, mask_space - mask_rows), (0, 0))
                 ),
             ],
             axis=0,
@@ -713,8 +757,7 @@
         every_dy[:, total_rows : total_rows + mask_rows].reshape(peers, total_rows, experts),
         ((0, 0), (0, 0), (0, LANES - experts)),
     )
-
-    own_mask = jnp.pad(chosen.astype(BF16), ((0, 0), (0, LANES - experts)))
+    own_mask = jnp.pad(chosen, ((0, 0), (0, LANES - experts)))
 
     doc_ends = jnp.cumsum(lengths[0])
     token_index = jnp.arange(total_rows, dtype=jnp.int32)
@@ -747,30 +790,35 @@
             pltpu.VMEM((model_width, first_width), BF16),
             pltpu.SemaphoreType.DMA((len(first_pieces),)),
         ],
-        SMALL_COST,
-    )
+        8,
+    )
+    out_pieces, out_places = fetch_rows(w_out, first_pieces[-1], normed)
     attended, logs = attend(start, q, k, v)
-    state, mixed_in, gates = simple_call(
+    state, mixed_low, mixed_high, gates = simple_call(
         functools.partial(mix_kernel, len(out_pieces)),
         "mix",
         out_places,
         [attended, tokens, own_mask, router_lanes, gains],
         out_pieces,
-        [(tokens.shape, F32), (tokens.shape, BF16), ((total_rows, LANES), F32)],
+        [
+            (tokens.shape, F32),
+            ((total_rows // 2, model_width), BF16),
+            ((total_rows // 2, model_width), BF16),
+            ((total_rows, LANES), F32),
+        ],
         [
             pltpu.VMEM((q_width, model_width), BF16),
             pltpu.SemaphoreType.DMA((len(out_pieces),)),
         ],
-        SMALL_COST,
-    )
-
-    part = total_rows // CHUNKS
+        7,
+    )
+
+    packed = jnp.concatenate([jnp.concatenate([w_gate, w_up], axis=2), w_down], axis=1)
+    weights = fetch_experts(packed, out_pieces[1:2], mixed_low)
     every_x, out_part, row_part, act, gate_back, up_back, scores_part = [], [], [], [], [], [], []
-    for chunk in range(CHUNKS):
-        gathered = lax.all_gather(
-            mixed_in[chunk * part : (chunk + 1) * part], "expert", axis=0, tiled=True
-        )
-        results = run_experts(gathered, every_dy, every_mask, router_lanes, pieces, chunk)
+    for chunk, mixed in enumerate((mixed_low, mixed_high)):
+        gathered = lax.all_gather(mixed, "expert", axis=0, tiled=True)
+        results = run_experts(gathered, every_dy, every_mask, router_lanes, weights, chunk)
         every_x.append(gathered)
         for kept, result in zip((out_part, row_part, act, gate_back, up_back, scores_part), results):
             kept.append(result)
@@ -778,11 +826,7 @@
         lax.psum_scatter(rows, "expert", scatter_dimension=0, tiled=True) for rows in row_part
     ]
     sent_scores = jnp.concatenate(
-        [
-            values[:, :local_experts].reshape(peers, -1, LANES)
-            for values in scores_part
-        ],
-        axis=1,
+        [values[:, :local_experts].reshape(peers, -1, LANES) for values in scores_part], axis=1
     )
     gate_grad = lax.all_to_all(sent_scores, "expert", split_axis=0, concat_axis=0, tiled=True)
     gate_grad = (
@@ -790,21 +834,34 @@
         .transpose(1, 0, 2)
         .reshape(total_rows, experts)
     )
-    *out_part, row_last = lax.optimization_barrier((*out_part, row_sum[-1]))
-    row_sum[-1] = row_last
-    out_sum = [lax.psum_scatter(rows, "expert", scatter_dimension=0, tiled=True) for rows in out_part]
-
     down_grad = down_gradient(act, every_dy, local_experts)
     gu_grad = gate_up_gradient(every_x, gate_back, up_back, local_experts)
+    four = lax.axis_size("shard") == 4 and local_experts % 2 == 0
+    if four:
+        gu_own, gu_one, gu_two, gu_far = split_parts(gu_grad, 1)
+        gu_low, gu_high = send_far(gu_far)
+        (row_sum, gate_grad, down_grad, gu_own, gu_one, gu_two, gu_low, gu_high) = (
+            lax.optimization_barrier(
+                (row_sum, gate_grad, down_grad, gu_own, gu_one, gu_two, gu_low, gu_high)
+            )
+        )
+        gu_one, gu_two = send_near(gu_one, gu_two, gu_low, gu_high)
+    else:
+        row_sum, gate_grad, gu_grad, down_grad = lax.optimization_barrier(
+            (row_sum, gate_grad, gu_grad, down_grad)
+        )
+    out_part, _ = lax.optimization_barrier((out_part, row_sum[-1]))
+    out_sum = [lax.psum_scatter(rows, "expert", scatter_dimension=0, tiled=True) for rows in out_part]
 
     state_grad, attended_grad, pack = simple_call(
-        functools.partial(mix_back_kernel, len(out_pieces), CHUNKS, experts),
+        functools.partial(mix_back_kernel, len(out_pieces), 2, experts),
         "mix_back",
         out_places,
         [
             attended,
             state,
-            mixed_in,
+            mixed_low,
+            mixed_high,
             cotangent,
             gates,
             jnp.pad(gate_grad, ((0, 0), (0, LANES - experts))),
@@ -822,35 +879,70 @@
             pltpu.VMEM((q_width, model_width), BF16),
             pltpu.SemaphoreType.DMA((len(out_pieces),)),
         ],
-    )
-    early = sum_everywhere(pack)
-    query_back, key_back, value_back = attend_back(
-        start, q, k, v, attended_grad, logs, cosine, sine
-    )
-    input_grad, late_pack = simple_call(
+        10,
+    )
+    backs = attend_back(start, q, k, v, attended_grad, logs, cosine, sine)
+    early = sum_near(pair_cores(pack))
+    (late_pack,) = simple_call(
+        project_weights_kernel,
+        "project_weights",
+        first_places,
+        [normed, *backs],
+        [],
+        [((model_width, first_width - LANES), BF16)],
+        [],
+        6,
+    )
+    late = pair_cores(late_pack)
+    if four:
+        late, early, gu_one, gu_two = lax.optimization_barrier((late, early, gu_one, gu_two))
+    backs, state_grad, late, down_grad = lax.optimization_barrier(
+        (backs, state_grad, late, down_grad)
+    )
+    late = sum_near(late)
+    if four:
+        down_own, down_one, down_two, down_far = split_parts(down_grad, 1)
+        down_low, down_high = send_far(down_far)
+    (input_grad,) = simple_call(
         functools.partial(project_back_kernel, len(first_pieces)),
         "project_back",
         first_places,
-        [normed, tokens, state_grad, gains, query_back, key_back, value_back],
+        [tokens, state_grad, gains, *backs],
         first_pieces,
-        [(tokens.shape, BF16), ((model_width, first_width), BF16)],
+        [(tokens.shape, BF16)],
         [
             pltpu.VMEM((model_width, first_width), BF16),
             pltpu.SemaphoreType.DMA((len(first_pieces),)),
         ],
-    )
-    expert_down_sum = scatter_sum(down_grad, 1, value_back)
-    gu_sum = scatter_sum(gu_grad, 1, value_back)
+        7,
+    )
+    late, early, input_grad = lax.optimization_barrier((late, early, input_grad))
+    if four:
+        down_low, down_high, _ = lax.optimization_barrier((down_low, down_high, late))
+        down_one, down_two = send_near(down_one, down_two, down_low, down_high)
+        gu_parts, state, _ = lax.optimization_barrier(((gu_own, gu_one, gu_two), state, late))
+        gu_sum, expert_down_sum = add_up(gu_parts), add_up((down_own, down_one, down_two))
+    else:
+        expert_down_sum = plain_scatter_sum(down_grad, 1)
+        gu_sum = plain_scatter_sum(gu_grad, 1)
     expert_gate_sum = gu_sum[:, :, :hidden]
     expert_up_sum = gu_sum[:, :, hidden:]
-    late = sum_everywhere(late_pack)
-    state, _ = lax.optimization_barrier((state, value_back))
+    whole = sum_far(jnp.concatenate([late, early], axis=1))
+    late, early = whole[:, : late.shape[1]], whole[:, late.shape[1] :]
     output = state + jnp.concatenate(out_sum, axis=0).astype(F32)
+    projections = (
+        (w_query, late[:, :q_width]),
+        (key_weight, late[:, q_width : q_width + kv_width]),
+        (value_weight, late[:, q_width + kv_width :]),
+    )
+    gain_sum = add_up(
+        jnp.sum(weight.astype(F32) * grad, axis=1) for weight, grad in projections
+    ) / gain_attn.astype(F32)
     q_end = q_width
     return (
         output.astype(BF16),
         input_grad,
-        late[:, q_end + 2 * kv_width],
+        gain_sum,
         late[:, :q_end],
         late[:, q_end : q_end + kv_width],
         late[:, q_end + kv_width : q_end + 2 * kv_width],

time: 525 us -> 474 us (0.903)
  waiting for transfers between devices: 200 us -> 138 us
  Pallas kernels: 192 us -> 198 us
    ppermute x33 -> x30, waiting for transfers between devices: 170 us -> 128 us  [the longest x26 116 us: flip_shard(): return lax.ppermute(value, 'shard', [(i, i ^ flip) for i in range(4)])]
    reduce_scatter x4, waiting for transfers between devices: 29.8 us -> 0.62 us  [per_device(): lax.psum_scatter(rows, 'expert', scatter_dimension=0, tiled=True)]
    convert_element_type x2 -> x11, other arithmetic: 0.22 us -> 11.7 us  [the longest x2 4.32 us: pair_cores(): return (mine.astype(F32) + swap_cores(away).astype(F32)).astype(BF16)]
    all_gather x3, waiting for transfers between devices: 0.02 us -> 8.13 us  [the longest x2 8.13 us: per_device(): gathered = lax.all_gather(mixed, 'expert', axis=0, tiled=True)]
    add x6 -> x2, other arithmetic: 8.78 us -> 3.04 us  [add_up(): return sum((value.astype(F32) for value in values))]
    pallas_call x4 -> x5, Pallas kernels: 35.4 us -> 40.9 us  [simple_call(): pl.pallas_call(kernel, grid_spec=pltpu.PrefetchScalarGridSpec(num_scalar_...]
    ppermute x33 -> x30, starting transfers between devices: 47 us -> 44.8 us  [the longest x26 33.2 us: flip_shard(): return lax.ppermute(value, 'shard', [(i, i ^ flip) for i in range(4)])]
  transfers between devices with their start and end apart: 51 -> 49, of which waited for: 24 -> 25; matrix products, arithmetic and copies ran while one was open for 9% -> 12% of each run, Pallas kernels for 37% -> 43%
where the time goes in v5:
time: 474 us; the launch traced here: 465 us
  Pallas kernels  198 us (42%)
  waiting for transfers between devices  138 us (29%)
  starting transfers between devices  50.9 us (11%)
  local copies, waits for them, and re-layouts  33 us (7%)
  other arithmetic  30.1 us (6%)
  between operations  15.5 us (3%)
    ppermute x26, waiting for transfers between devices, flip_shard(): return lax.ppermute(value, 'shard', [(i, i ^ flip) for i in range(4)])  116 us
    pallas_call x2, Pallas kernels, run_experts(): pl.pallas_call(functools.partial(expert_kernel, sources, len(arrays)), gr...  88.3 us
    pallas_call x5, Pallas kernels, simple_call(): pl.pallas_call(kernel, grid_spec=pltpu.PrefetchScalarGridSpec(num_scalar_...  40.9 us
    ppermute x26, starting transfers between devices, flip_shard(): return lax.ppermute(value, 'shard', [(i, i ^ flip) for i in range(4)])  33.2 us
    pallas_call x1, Pallas kernels, gate_up_gradient(): pl.pallas_call(functools.partial(columns_kernel, chunks, local), grid=(4,...  25.7 us
    pallas_call x1, Pallas kernels, attend_back(): pl.pallas_call(attend_back_kernel, grid=(k.shape[1] // LANES,), in_specs=...  14.7 us
    pallas_call x1, Pallas kernels, down_gradient(): pl.pallas_call(functools.partial(down_kernel, chunks), grid=(4,), in_spec...  14.5 us
    pallas_call x1, Pallas kernels, attend(): pl.pallas_call(attend_kernel, grid=(steps,), in_specs=[one, wide, thin, t...  13.5 us
  transfers between devices with their start and end apart: 49, of which 25 were waited for; matrix products, arithmetic and copies ran while one was open for 12% of the time, Pallas kernels for 43%

profile of v5, /device:TPU:0, one launch (start us, length us, event | category | flops | bytes accessed | tf_op | source)
XLA Modules:
  0.0 464.9 jit_solution(7285010882372719139)
XLA Ops:
  17.6 10.9 %collective-permute-done.2.refs_3_ = bf16[128,2176]{1,0:T(8,128)(2,1)S(1)} collective-permute-done((bf16[128,2176]{1,0:T(8,128)(2,1)S(1)}, bf16[128,2176]{1,0:T(8,128)(2,1)S(1)}, u32[]{:S(2)}, u32[]{:S(2)}) %collective-permute-start.2) | collective-permute-done | bytes 557088 | tf_op jit(solution)/shard_map/ppermute | solution.py:49
  32.4 4.2 collective-permute-done.4.refs_5_
  44.0 7.8 %project.1 = (bf16[512,1024]{1,0:T(8,128)(2,1)}, bf16[512,1024]{1,0:T(8,128)(2,1)}, bf16[512,512]{1,0:T(8,128)(2,1)}, bf16[512,512]{1,0:T(8,128)(2,1)}, f32[8,1024]{1,0:T(8,128)}, /*index=5*/bf16[1024,128]{1,0:T(8,128)(2,1)}) custom-call(s32[9]{0:T(128)} %stack.79.place_ref, bf16[512,1024]{1,0:T(8,128)(2,1)} %x_ref.5, ...), custom_call_target="tpu_custom_call" | custom-call | flops 9200000000 | tf_op jit(solution)/shard_map/project/pallas_call | solution.py:434
  58.0 13.5 %attend.1 = (bf16[512,1024]{1,0:T(8,128)(2,1)}, f32[32,512]{1,0:T(8,128)}) custom-call(s32[1,512]{1,0:T(1,128)} %bitcast.71, bf16[512,1024]{1,0:T(8,128)(2,1)} %get-tuple-element.78.q_ref, bf16[512,512]{1,0:T(8,128)(2,1)} %get-tuple-element.79.k_ref, bf16[512,512]{1,0:T(8,128)(2,1)} %get-tuple-element.80.v_ref), custom_call_target="tpu_custom_call" | custom-call | flops 14949999616 | tf_op jit(solution)/shard_map/attend/pallas_call | solution.py:572
  72.5 7.4 %mix.1 = (f32[512,1024]{1,0:T(8,128)}, bf16[256,1024]{1,0:T(8,128)(2,1)}, bf16[256,1024]{1,0:T(8,128)(2,1)}, f32[512,128]{1,0:T(8,128)}) custom-call(s32[9]{0:T(128)} %stack.79.place_ref, bf16[512,1024]{1,0:T(8,128)(2,1)} %get-tuple-element.81.attended_ref, bf16[512,1024]{1,0:T(8,128)(2,1)} %x_ref.5, bf16[512,128]{1,0:T(8,128)(2,1)} %pad_convert_fusion.mask_ref, ...), custom_call_target="tpu_custom_call" | custom-call | flops 8049999872 | tf_op jit(solution)/shard_map/mix/pallas_call | solution.py:434
  83.9 34.3 %collective-permute-done.17.refs_2_ = bf16[2,384,1024]{2,1,0:T(8,128)(2,1)S(1)} collective-permute-done((bf16[2,384,1024]{2,1,0:T(8,128)(2,1)S(1)}, bf16[2,384,1024]{2,1,0:T(8,128)(2,1)S(1)}, u32[]{:S(2)}, u32[]{:S(2)}) %collective-permute-start.17) | collective-permute-done | bytes 1572896 | tf_op jit(solution)/shard_map/ppermute | solution.py:49
  125.8 13.6 %collective-permute-done.18.refs_3_ = bf16[1,384,1024]{2,1,0:T(8,128)(2,1)} collective-permute-done((bf16[1,384,1024]{2,1,0:T(8,128)(2,1)}, bf16[1,384,1024]{2,1,0:T(8,128)(2,1)}, u32[]{:S(2)}, u32[]{:S(2)}) %collective-permute-start.18) | collective-permute-done | bytes 786464 | tf_op jit(solution)/shard_map/ppermute | solution.py:49
  140.2 5.0 %all-gather.7.cloned.1.call-done.x_ref.refs_1_ = bf16[2048,1024]{1,0:T(8,128)(2,1)} async-done(((bf16[256,1024]{1,0:T(8,128)(2,1)}), bf16[2048,1024]{1,0:T(8,128)(2,1)}) %all-gather.7.cloned.1.call-update) | async-done | bytes 4194320 | tf_op jit(solution)/shard_map/all_gather | solution.py:820
  145.2 44.2 %experts.3 = (bf16[2048,1024]{1,0:T(8,128)(2,1)}, bf16[2048,1024]{1,0:T(8,128)(2,1)}, bf16[2048,1024]{1,0:T(8,128)(2,1)}, bf16[2048,1024]{1,0:T(8,128)(2,1)}, bf...) custom-call(s32[5]{0:T(128)} %stack.69.place_ref, bf16[2048,1024]{1,0:T(8,128)(2,1)} %all-gather.7.cloned.1.call-done.x_ref.refs_1_, ...), custom_call_target="tpu_custom_call" | custom-call | flops 25769803776 | bytes 29360128 | tf_op jit(solution)/shard_map/experts/pallas_call | solution.py:268
  192.7 44.2 %experts.2 = (bf16[2048,1024]{1,0:T(8,128)(2,1)}, bf16[2048,1024]{1,0:T(8,128)(2,1)}, bf16[2048,1024]{1,0:T(8,128)(2,1)}, bf16[2048,1024]{1,0:T(8,128)(2,1)}, bf...) custom-call(s32[5]{0:T(128)} %stack.69.place_ref, bf16[2048,1024]{1,0:T(8,128)(2,1)} %all-gather.5.cloned.1.call-done.x_ref.refs_0_, ...), custom_call_target="tpu_custom_call" | custom-call | flops 25769803776 | bytes 29360128 | tf_op jit(solution)/shard_map/experts/pallas_call | solution.py:268
  243.4 25.7 %gate_up_gradient.1 = bf16[2,1024,1024]{2,1,0:T(8,128)(2,1)} custom-call(bf16[2048,1024]{1,0:T(8,128)(2,1)} %all-gather.5.cloned.1.call-done.x_ref.refs_0_, bf16[2048,1024]{1,0:T(8,128)(2,1)} %all-gather.7.cloned.1.call-done.x_ref.refs_1_, bf16[2048,1024]{1,0:T(8,128)(2,1)} %get-tuple-element.99.refs_2_, bf16[2048,1024]{1,0:T(8,128)(2,1)} %get-tuple-element.100.refs_3_, ...), custom_call_target="tpu_custom_call" | custom-call | flops 17179869184 | bytes 25165824 | tf_op jit(solution)/shard_map/gate_up_gradient/pallas_call | solution.py:315
  274.3 14.5 %down_gradient.1 = bf16[1024,1024]{1,0:T(8,128)(2,1)} custom-call(bf16[2048,1024]{1,0:T(8,128)(2,1)} %get-tuple-element.97.refs_0_, bf16[2048,1024]{1,0:T(8,128)(2,1)} %get-tuple-element.98.refs_1_, bf16[8,528,1024]{2,1,0:T(8,128)(2,1)} %bitcast.76, bf16[8,528,1024]{2,1,0:T(8,128)(2,1)} %bitcast.77), custom_call_target="tpu_custom_call" | custom-call | flops 8589934592 | bytes 16777216 | tf_op jit(solution)/shard_map/down_gradient/pallas_call | solution.py:351
  295.8 9.5 %mix_back.1 = (f32[512,1024]{1,0:T(8,128)}, bf16[512,1024]{1,0:T(8,128)(2,1)}, bf16[1024,1152]{1,0:T(8,128)(2,1)}) custom-call(s32[9]{0:T(128)} %stack.79.place_ref, bf16[512,1024]{1,0:T(8,128)(2,1)} %get-tuple-element.81.attended_ref, f32[512,1024]{1,0:T(8,128)} %get-tuple-element.131.state_ref, bf16[256,1024]{1,0:T(8,128)(2,1)} %get-tuple-element.88.low_ref, ...), custom_call_target="tpu_custom_call" | custom-call | flops 11500000256 | tf_op jit(solution)/shard_map/mix_back/pallas_call | solution.py:434
  307.7 14.7 %attend_back.1 = (bf16[512,1024]{1,0:T(8,128)(2,1)}, bf16[512,512]{1,0:T(8,128)(2,1)}, bf16[512,512]{1,0:T(8,128)(2,1)}) custom-call(s32[1,512]{1,0:T(1,128)} %bitcast.72, bf16[512,1024]{1,0:T(8,128)(2,1)} %get-tuple-element.78.q_ref, bf16[512,512]{1,0:T(8,128)(2,1)} %get-tuple-element.79.k_ref, bf16[512,512]{1,0:T(8,128)(2,1)} %get-tuple-element.80.v_ref, ...), custom_call_target="tpu_custom_call" | custom-call | flops 17250000896 | tf_op jit(solution)/shard_map/attend_back/pallas_call | solution.py:590
  322.4 6.9 %project_weights.1 = bf16[1024,2048]{1,0:T(8,128)(2,1)} custom-call(s32[9]{0:T(128)} %stack.79.place_ref, bf16[512,1024]{1,0:T(8,128)(2,1)} %get-tuple-element.85.normed_ref, bf16[512,1024]{1,0:T(8,128)(2,1)} %get-tuple-element.127.qb_ref, bf16[512,512]{1,0:T(8,128)(2,1)} %get-tuple-element.128.kb_ref, bf16[512,512]{1,0:T(8,128)(2,1)} %get-tuple-element.129.vb_ref), custom_call_target="tpu_custom_call" | custom-call | flops 6899999744 | tf_op jit(solution)/shard_map/project_weights/pallas_call | solution.py:434
  344.1 4.9 %collective-permute-done.24 = bf16[128,1152]{1,0:T(8,128)(2,1)S(1)} collective-permute-done((bf16[128,1152]{1,0:T(8,128)(2,1)S(1)}, bf16[128,1152]{1,0:T(8,128)(2,1)S(1)}, u32[]{:S(2)}, u32[]{:S(2)}) %collective-permute-start.24) | collective-permute-done | bytes 294944 | tf_op jit(solution)/shard_map/ppermute | solution.py:49
  350.5 4.8 %collective-permute-done.26 = bf16[128,1152]{1,0:T(8,128)(2,1)S(1)} collective-permute-done((bf16[128,1152]{1,0:T(8,128)(2,1)S(1)}, bf16[128,1152]{1,0:T(8,128)(2,1)S(1)}, u32[]{:S(2)}, u32[]{:S(2)}) %collective-permute-start.26) | collective-permute-done | bytes 294944 | tf_op jit(solution)/shard_map/ppermute | solution.py:49
  355.2 18.1 %collective-permute-done.25 = bf16[128,1152]{1,0:T(8,128)(2,1)S(1)} collective-permute-done((bf16[128,1152]{1,0:T(8,128)(2,1)S(1)}, bf16[128,1152]{1,0:T(8,128)(2,1)S(1)}, u32[]{:S(2)}, u32[]{:S(2)}) %collective-permute-start.25) | collective-permute-done | bytes 294944 | tf_op jit(solution)/shard_map/ppermute | solution.py:49
  381.1 9.2 %project_back.1 = bf16[512,1024]{1,0:T(8,128)(2,1)} custom-call(s32[9]{0:T(128)} %stack.79.place_ref, bf16[512,1024]{1,0:T(8,128)(2,1)} %x_ref.5, f32[512,1024]{1,0:T(8,128)} %get-tuple-element.126.state_grad_ref, f32[8,1024]{1,0:T(8,128)} %get-tuple-element.83.gains_ref, bf16[512,1024]{1,0:T(8,128)(2,1)} %get-tuple-element.127.qb_ref, ...), custom_call_target="tpu_custom_call" | custom-call | flops 8049999872 | tf_op jit(solution)/shard_map/project_back/pallas_call | solution.py:434
  392.8 9.8 %collective-permute-done.31 = bf16[128,2048]{1,0:T(8,128)(2,1)} collective-permute-done((bf16[128,2048]{1,0:T(8,128)(2,1)S(1)}, bf16[128,2048]{1,0:T(8,128)(2,1)}, u32[]{:S(2)}, u32[]{:S(2)}) %collective-permute-start.31) | collective-permute-done | bytes 524320 | tf_op jit(solution)/shard_map/ppermute | solution.py:49
  413.1 5.1 %collective-permute-done.37 = bf16[1,128,1024]{2,1,0:T(8,128)(2,1)} collective-permute-done((bf16[1,128,1024]{2,1,0:T(8,128)(2,1)}, bf16[1,128,1024]{2,1,0:T(8,128)(2,1)}, u32[]{:S(2)}, u32[]{:S(2)}) %collective-permute-start.37) | collective-permute-done | bytes 262176 | tf_op jit(solution)/shard_map/ppermute | solution.py:49
  419.1 5.5 %collective-permute-done.34 = bf16[64,3200]{1,0:T(8,128)(2,1)} collective-permute-done((bf16[64,3200]{1,0:T(8,128)(2,1)}, bf16[64,3200]{1,0:T(8,128)(2,1)}, u32[]{:S(2)}, u32[]{:S(2)}) %collective-permute-start.34) | collective-permute-done | bytes 409632 | tf_op jit(solution)/shard_map/ppermute | solution.py:54
  431.0 7.0 %collective-permute-start.35 = (bf16[64,3200]{1,0:T(8,128)(2,1)S(1)}, bf16[64,3200]{1,0:T(8,128)(2,1)S(1)}, u32[]{:S(2)}, u32[]{:S(2)}) collective-permute-start(bf16[64,3200]{1,0:T(8,128)(2,1)S(1)} %get-tuple-element.247), channel_id=1, source_target_pairs={{0,8},{4,12},{8,0},{12,4},{16,24},{20,28},{24,16},{28,20},{1,9},{5... | collective-permute-start | bytes 1228808 | tf_op jit(solution)/shard_map/ppermute | solution.py:54
  439.6 4.4 collective-permute-done.35
  (240 shorter events, 124.0 us)
Async XLA Ops:
  7.2 115.6 %all-gather.9.cloned.1.call-start = ((), (), s32[]{:S(2)}) async-start(), calls=%async_computation.11 | async-start | bytes 9732096 | tf_op jit(solution)/shard_map/all_gather | solution.py:743
  10.8 134.4 %all-gather.7.cloned.1.call-start = ((), (), s32[]{:S(2)}) async-start(), calls=%async_computation.7 | async-start | bytes 4718592 | tf_op jit(solution)/shard_map/all_gather | solution.py:820
  54.5 17.1 %collective-permute-start.10 = (bf16[128,1024]{1,0:T(8,128)(2,1)S(1)}, bf16[128,1024]{1,0:T(8,128)(2,1)S(1)}, u32[]{:S(2)}, u32[]{:S(2)}) collective-permute-start(bf16[128,1024]{1,0:T(8,128)(2,1)S(1)} %collective-permute-done.8.refs_1_.refs_3_), channel_id=1, source_target_pairs={{0,4},{4,0},{8,12},{12,8},{16,20},{20,16},{24,28},{28,24},{1,5},{5... | collective-permute-start | bytes 786440 | tf_op jit(solution)/shard_map/ppermute | solution.py:59
  80.0 112.7 %all-gather.5.cloned.1.call-start = ((), (), s32[]{:S(2)}) async-start(), calls=%async_computation.5 | async-start | bytes 4718592 | tf_op jit(solution)/shard_map/all_gather | solution.py:820
  80.7 212.6 %reduce-scatter.7.cloned.1.call-start = ((), (), s32[]{:S(2)}) async-start(), calls=%async_computation.8 | async-start | bytes 4718592 | tf_op jit(solution)/shard_map/reduce_scatter | solution.py:826
  81.5 36.8 %collective-permute-start.17 = (bf16[2,384,1024]{2,1,0:T(8,128)(2,1)S(1)}, bf16[2,384,1024]{2,1,0:T(8,128)(2,1)S(1)}, u32[]{:S(2)}, u32[]{:S(2)}) collective-permute-start(bf16[2,384,1024]{2,1,0:T(8,128)(2,1)S(1)} %pad_maximum_fusion.refs_0_), channel_id=1, source_target_pairs={{0,2},{1,3},{2,0},{3,1},{4,6},{5,7},{6,4},{7,5},{8,10},{9,11},{10,... | collective-permute-start | bytes 4718600 | tf_op jit(solution)/shard_map/ppermute | solution.py:49
  82.6 36.4 %collective-permute-start.16 = (bf16[2,384,1024]{2,1,0:T(8,128)(2,1)S(1)}, bf16[2,384,1024]{2,1,0:T(8,128)(2,1)S(1)}, u32[]{:S(2)}, u32[]{:S(2)}) collective-permute-start(bf16[2,384,1024]{2,1,0:T(8,128)(2,1)S(1)} %pad_maximum_fusion.refs_0_), channel_id=1, source_target_pairs={{0,1},{1,0},{2,3},{3,2},{4,5},{5,4},{6,7},{7,6},{8,9},{9,8},{10,11... | collective-permute-start | bytes 4718600 | tf_op jit(solution)/shard_map/ppermute | solution.py:49
  120.1 19.3 %collective-permute-start.18 = (bf16[1,384,1024]{2,1,0:T(8,128)(2,1)}, bf16[1,384,1024]{2,1,0:T(8,128)(2,1)}, u32[]{:S(2)}, u32[]{:S(2)}) collective-permute-start(bf16[1,384,1024]{2,1,0:T(8,128)(2,1)} %slice.109), channel_id=1, source_target_pairs={{0,1},{1,0},{2,3},{3,2},{4,5},{5,4},{6,7},{7,6},{8,9},{9,8},{10,11... | collective-permute-start | bytes 2359304 | tf_op jit(solution)/shard_map/ppermute | solution.py:49
  121.5 18.7 %collective-permute-start.19 = (bf16[1,384,1024]{2,1,0:T(8,128)(2,1)S(1)}, bf16[1,384,1024]{2,1,0:T(8,128)(2,1)}, u32[]{:S(2)}, u32[]{:S(2)}) collective-permute-start(bf16[1,384,1024]{2,1,0:T(8,128)(2,1)S(1)} %slice.110), channel_id=1, source_target_pairs={{0,2},{1,3},{2,0},{3,1},{4,6},{5,7},{6,4},{7,5},{8,10},{9,11},{10,... | collective-permute-start | bytes 2359304 | tf_op jit(solution)/shard_map/ppermute | solution.py:49
  189.4 104.5 %reduce-scatter.5.cloned.1.call-start = ((), (), s32[]{:S(2)}) async-start(), calls=%async_computation.6 | async-start | bytes 4718592 | tf_op jit(solution)/shard_map/reduce_scatter | solution.py:826
  239.8 51.2 %all-to-all-start = ((f32[8,8,128]{2,1,0:T(8,128)}), f32[8,8,128]{2,1,0:T(8,128)S(1)}, u32[]{:S(2)}, u32[]{:S(2)}) async-start(f32[8,8,128]{2,1,0:T(8,128)} %pad_maximum_fusion.9), calls=%async_computation.2 | async-start | bytes 65536 | tf_op jit(solution)/shard_map/all_to_all | solution.py:831
  243.1 211.7 %reduce-scatter.9.cloned.1.call-start = ((), (), s32[]{:S(2)}) async-start(), calls=%async_computation.9 | async-start | bytes 4718592 | tf_op jit(solution)/shard_map/reduce_scatter | solution.py:854
  271.4 21.9 %collective-permute-start.21 = (bf16[1,256,1024]{2,1,0:T(8,128)(2,1)}, bf16[1,256,1024]{2,1,0:T(8,128)(2,1)}, u32[]{:S(2)}, u32[]{:S(2)}) collective-permute-start(bf16[1,256,1024]{2,1,0:T(8,128)(2,1)} %get-tuple-element.222), channel_id=1, source_target_pairs={{0,2},{1,3},{2,0},{3,1},{4,6},{5,7},{6,4},{7,5},{8,10},{9,11},{10,... | collective-permute-start | bytes 1572872 | tf_op jit(solution)/shard_map/ppermute | solution.py:49
  272.8 20.5 %collective-permute-start.20 = (bf16[1,256,1024]{2,1,0:T(8,128)(2,1)}, bf16[1,256,1024]{2,1,0:T(8,128)(2,1)}, u32[]{:S(2)}, u32[]{:S(2)}) collective-permute-start(bf16[1,256,1024]{2,1,0:T(8,128)(2,1)} %get-tuple-element.223), channel_id=1, source_target_pairs={{0,1},{1,0},{2,3},{3,2},{4,5},{5,4},{6,7},{7,6},{8,9},{9,8},{10,11... | collective-permute-start | bytes 1572872 | tf_op jit(solution)/shard_map/ppermute | solution.py:49
  293.9 160.9 %reduce-scatter.11.cloned.1.call-start = ((), (), s32[]{:S(2)}) async-start(), calls=%async_computation.10 | async-start | bytes 4718592 | tf_op jit(solution)/shard_map/reduce_scatter | solution.py:854
  307.7 29.3 %collective-permute-start.23 = (bf16[4,128,1152]{2,1,0:T(8,128)(2,1)}, bf16[4,128,1152]{2,1,0:T(8,128)(2,1)}, u32[]{:S(2)}, u32[]{:S(2)}) collective-permute-start(bf16[4,128,1152]{2,1,0:T(8,128)(2,1)} %dynamic-slice_bitcast_fusion.1), channel_id=1, source_target_pairs={{0,4},{4,0},{8,12},{12,8},{16,20},{20,16},{24,28},{28,24},{1,5},{5... | collective-permute-start | bytes 3538952 | tf_op jit(solution)/shard_map/ppermute | solution.py:59
  332.6 40.9 %collective-permute-start.22 = (bf16[4,128,2048]{2,1,0:T(8,128)(2,1)}, bf16[4,128,2048]{2,1,0:T(8,128)(2,1)}, u32[]{:S(2)}, u32[]{:S(2)}) collective-permute-start(bf16[4,128,2048]{2,1,0:T(8,128)(2,1)} %dynamic-slice_bitcast_fusion), channel_id=1, source_target_pairs={{0,4},{4,0},{8,12},{12,8},{16,20},{20,16},{24,28},{28,24},{1,5},{5... | collective-permute-start | bytes 6291464 | tf_op jit(solution)/shard_map/ppermute | solution.py:59
  335.4 40.5 %collective-permute-start.28 = (bf16[2,256,1024]{2,1,0:T(8,128)(2,1)}, bf16[2,256,1024]{2,1,0:T(8,128)(2,1)S(1)}, u32[]{:S(2)}, u32[]{:S(2)}) collective-permute-start(bf16[2,256,1024]{2,1,0:T(8,128)(2,1)} %pad_maximum_fusion.3), channel_id=1, source_target_pairs={{0,2},{1,3},{2,0},{3,1},{4,6},{5,7},{6,4},{7,5},{8,10},{9,11},{10,... | collective-permute-start | bytes 3145736 | tf_op jit(solution)/shard_map/ppermute | solution.py:49
  341.0 32.3 %collective-permute-start.25 = (bf16[128,1152]{1,0:T(8,128)(2,1)S(1)}, bf16[128,1152]{1,0:T(8,128)(2,1)S(1)}, u32[]{:S(2)}, u32[]{:S(2)}) collective-permute-start(bf16[128,1152]{1,0:T(8,128)(2,1)S(1)} %get-tuple-element.245), channel_id=1, source_target_pairs={{0,2},{1,3},{2,0},{3,1},{4,6},{5,7},{6,4},{7,5},{8,10},{9,11},{10,... | collective-permute-start | bytes 884744 | tf_op jit(solution)/shard_map/ppermute | solution.py:49
  349.0 27.7 %collective-permute-start.27 = (bf16[2,256,1024]{2,1,0:T(8,128)(2,1)S(1)}, bf16[2,256,1024]{2,1,0:T(8,128)(2,1)}, u32[]{:S(2)}, u32[]{:S(2)}) collective-permute-start(bf16[2,256,1024]{2,1,0:T(8,128)(2,1)S(1)} %pad_maximum_fusion.2), channel_id=1, source_target_pairs={{0,1},{1,0},{2,3},{3,2},{4,5},{5,4},{6,7},{7,6},{8,9},{9,8},{10,11... | collective-permute-start | bytes 3145736 | tf_op jit(solution)/shard_map/ppermute | solution.py:49
  379.1 23.6 %collective-permute-start.31 = (bf16[128,2048]{1,0:T(8,128)(2,1)S(1)}, bf16[128,2048]{1,0:T(8,128)(2,1)}, u32[]{:S(2)}, u32[]{:S(2)}) collective-permute-start(bf16[128,2048]{1,0:T(8,128)(2,1)S(1)} %get-tuple-element.237), channel_id=1, source_target_pairs={{0,3},{1,2},{2,1},{3,0},{4,7},{5,6},{6,5},{7,4},{8,11},{9,10},{10,... | collective-permute-start | bytes 1572872 | tf_op jit(solution)/shard_map/ppermute | solution.py:49
  379.9 23.9 %collective-permute-start.30 = (bf16[128,2048]{1,0:T(8,128)(2,1)S(1)}, bf16[128,2048]{1,0:T(8,128)(2,1)}, u32[]{:S(2)}, u32[]{:S(2)}) collective-permute-start(bf16[128,2048]{1,0:T(8,128)(2,1)S(1)} %get-tuple-element.238), channel_id=1, source_target_pairs={{0,2},{1,3},{2,0},{3,1},{4,6},{5,7},{6,4},{7,5},{8,10},{9,11},{10,... | collective-permute-start | bytes 1572872 | tf_op jit(solution)/shard_map/ppermute | solution.py:49
  407.1 17.6 %collective-permute-start.34 = (bf16[64,3200]{1,0:T(8,128)(2,1)}, bf16[64,3200]{1,0:T(8,128)(2,1)}, u32[]{:S(2)}, u32[]{:S(2)}) collective-permute-start(bf16[64,3200]{1,0:T(8,128)(2,1)} %get-tuple-element.249), channel_id=1, source_target_pairs={{0,24},{4,28},{8,16},{12,20},{16,8},{20,12},{24,0},{28,4},{1,25},{... | collective-permute-start | bytes 1228808 | tf_op jit(solution)/shard_map/ppermute | solution.py:54
  429.0 18.6 %collective-permute-start.40 = (bf16[2,128,1024]{2,1,0:T(8,128)(2,1)S(1)}, bf16[2,128,1024]{2,1,0:T(8,128)(2,1)S(1)}, u32[]{:S(2)}, u32[]{:S(2)}) collective-permute-start(bf16[2,128,1024]{2,1,0:T(8,128)(2,1)S(1)} %pad_maximum_fusion.6), channel_id=1, source_target_pairs={{0,2},{1,3},{2,0},{3,1},{4,6},{5,7},{6,4},{7,5},{8,10},{9,11},{10,... | collective-permute-start | bytes 1572872 | tf_op jit(solution)/shard_map/ppermute | solution.py:49
  (60 other events, 600.3 us)
Sparse Core Ops, SparseCore 0:
  10.9 86.9 all-gather.8
  99.5 45.6 all-gather.6
  146.8 45.8 all-gather.4
  194.9 48.7 reduce-scatter.6
  245.8 48.1 reduce-scatter.4
  296.1 48.1 reduce-scatter.8
  346.5 48.1 reduce-scatter.10

commit v6 on v5

--- a/solution.py
+++ b/solution.py
@@ -120,10 +120,14 @@
     return flip_shard(far[:half], 1), flip_shard(far[half:], 2)
 
 
-def send_near(one, two, low, high):
+def join_near(one, two, low, high):
     half = one.shape[0] // 2
     two = jnp.concatenate([(two[:half].astype(F32) + low.astype(F32)).astype(BF16), two[half:]], axis=0)
     one = jnp.concatenate([one[:half], (one[half:].astype(F32) + high.astype(F32)).astype(BF16)], axis=0)
+    return one, two
+
+
+def send_near(one, two):
     return flip_shard(one, 1), flip_shard(two, 2)
 
 
@@ -146,18 +150,20 @@
     return (mine.astype(F32) + swap_cores(away).astype(F32)).astype(BF16)
 
 
-def sum_near(paired):
+def sum_near(paired, after=None):
     count, half, width = paired.shape
     if count != 4:
         return plain_scatter_sum(paired, 0).reshape(half, width).astype(BF16)
     own, one, two, far = (part.reshape(half, width) for part in split_parts(paired, 0))
+    if after is not None:
+        own, _ = lax.optimization_barrier((own, after))
     total = own.astype(F32)
     for flip, sent in ((1, one), (2, two), (3, far)):
         total = total + flip_shard(sent, flip).astype(F32)
     return total.astype(BF16)
 
 
-def sum_far(local):
+def sum_far(local, beside, last):
     layers = lax.axis_size("expert") // 2
     core = lax.axis_index("expert") % 2
     if layers != 4:
@@ -171,15 +177,18 @@
                 (low.astype(F32) + flip_layer(low, order[0]).astype(F32)).astype(BF16),
                 (high.astype(F32) + flip_layer(high, order[1]).astype(F32)).astype(BF16),
             )
+            if order == (1, 3):
+                low, high, beside = lax.optimization_barrier((low, high, beside))
         total = jnp.concatenate([low, high], axis=0)
+    total, last = lax.optimization_barrier((total, last))
     other = swap_cores(total)
     low = jnp.where(core == 0, total, other)
     high = jnp.where(core == 0, other, total)
-    return jnp.concatenate([low, high], axis=0).astype(F32)
-
-
-def expert_kernel(sources, arrays, place_ref, x_ref, dy_ref, mask_ref, router_ref, *refs):
-    pieces = refs[:arrays]
+    return jnp.concatenate([low, high], axis=0).astype(F32), beside, last
+
+
+def expert_kernel(sources, arrays, earlier, place_ref, x_ref, dy_ref, mask_ref, router_ref, *refs):
+    pieces, refs = refs[:arrays], refs[earlier:]
     out_ref, row_ref, act_ref, gate_ref, up_ref, score_ref, gu, down, sem = refs[arrays:]
     local, rows, width = pieces[0].shape
     third = rows // 3
@@ -247,12 +256,12 @@
         out = part if out is None else out + part
         part = product_transposed_right(gate_back, left) + product_transposed_right(up_back, right)
         row = part if row is None else row + part
-    out_ref[...] = out.astype(BF16)
+    out_ref[...] = out.astype(BF16).reshape(out_ref.shape)
     row_ref[...] = row.astype(BF16)
     score_ref[...] = scores
 
 
-def run_experts(every_x, every_dy, mask, router, weights, chunk):
+def run_experts(every_x, every_dy, mask, router, weights, chunk, earlier):
     arrays, sources, places = weights
     count = len(sources[0])
     total, width = every_x.shape
@@ -266,7 +275,7 @@
     block = pl.BlockSpec((tile, width), lambda i, p: (i, 0))
     thin = pl.BlockSpec((tile, LANES), lambda i, p: (i, 0))
     return pl.pallas_call(
-        functools.partial(expert_kernel, sources, len(arrays)),
+        functools.partial(expert_kernel, sources, len(arrays), len(earlier)),
         grid_spec=pltpu.PrefetchScalarGridSpec(
             num_scalar_prefetch=1,
             grid=(peers // group,),
@@ -276,22 +285,31 @@
                 pl.BlockSpec((group, rows_each, LANES), lambda i, p: (i, chunk, 0)),
                 pl.BlockSpec((width, LANES), lambda i, p: (0, 0)),
             ]
-            + [pl.BlockSpec(memory_space=pl.ANY)] * len(arrays),
-            out_specs=[block, block, block, block, block, thin],
+            + [pl.BlockSpec(memory_space=pl.ANY)] * (len(arrays) + len(earlier)),
+            out_specs=[
+                pl.BlockSpec((group, rows_each, width), lambda i, p: (i, chunk, 0)),
+                block,
+                block,
+                block,
+                block,
+                thin,
+            ],
             scratch_shapes=[
                 pltpu.VMEM((local, 2 * third * count, width), BF16),
                 pltpu.VMEM((local, third * count, width), BF16),
                 pltpu.SemaphoreType.DMA((local, count, 2)),
             ],
         ),
-        out_shape=[jax.ShapeDtypeStruct((total, width), BF16)] * 5
+        out_shape=[jax.ShapeDtypeStruct((peers, 2 * rows_each, width), BF16)]
+        + [jax.ShapeDtypeStruct((total, width), BF16)] * 4
         + [jax.ShapeDtypeStruct((total, LANES), F32)],
         compiler_params=pltpu.CompilerParams(vmem_limit_bytes=VMEM_LIMIT),
         cost_estimate=pl.CostEstimate(
             flops=2 * total * width * width * 6, bytes_accessed=total * width * 14, transcendentals=0
         ),
+        input_output_aliases={5 + len(arrays): 0} if earlier else {},
         name="experts",
-    )(place, every_x, every_dy, mask, router, *arrays)
+    )(place, every_x, every_dy, mask, router, *arrays, *earlier)
 
 
 def columns_kernel(chunks, local, *refs):
@@ -818,7 +836,9 @@
     every_x, out_part, row_part, act, gate_back, up_back, scores_part = [], [], [], [], [], [], []
     for chunk, mixed in enumerate((mixed_low, mixed_high)):
         gathered = lax.all_gather(mixed, "expert", axis=0, tiled=True)
-        results = run_experts(gathered, every_dy, every_mask, router_lanes, weights, chunk)
+        results = run_experts(
+            gathered, every_dy, every_mask, router_lanes, weights, chunk, out_part[-1:]
+        )
         every_x.append(gathered)
         for kept, result in zip((out_part, row_part, act, gate_back, up_back, scores_part), results):
             kept.append(result)
@@ -834,24 +854,27 @@
         .transpose(1, 0, 2)
         .reshape(total_rows, experts)
     )
+    gate_grad = jnp.pad(gate_grad, ((0, 0), (0, LANES - experts)))
+    act, gate_grad = lax.optimization_barrier((act, gate_grad))
     down_grad = down_gradient(act, every_dy, local_experts)
     gu_grad = gate_up_gradient(every_x, gate_back, up_back, local_experts)
     four = lax.axis_size("shard") == 4 and local_experts % 2 == 0
     if four:
         gu_own, gu_one, gu_two, gu_far = split_parts(gu_grad, 1)
         gu_low, gu_high = send_far(gu_far)
-        (row_sum, gate_grad, down_grad, gu_own, gu_one, gu_two, gu_low, gu_high) = (
+        down_own, down_one, down_two, down_far = split_parts(down_grad, 1)
+        (row_sum, gate_grad, gu_own, gu_one, gu_two, gu_low, gu_high, down_far) = (
             lax.optimization_barrier(
-                (row_sum, gate_grad, down_grad, gu_own, gu_one, gu_two, gu_low, gu_high)
+                (row_sum, gate_grad, gu_own, gu_one, gu_two, gu_low, gu_high, down_far)
             )
         )
-        gu_one, gu_two = send_near(gu_one, gu_two, gu_low, gu_high)
+        down_low, down_high = send_far(down_far)
     else:
         row_sum, gate_grad, gu_grad, down_grad = lax.optimization_barrier(
             (row_sum, gate_grad, gu_grad, down_grad)
         )
-    out_part, _ = lax.optimization_barrier((out_part, row_sum[-1]))
-    out_sum = [lax.psum_scatter(rows, "expert", scatter_dimension=0, tiled=True) for rows in out_part]
+    out_whole, _ = lax.optimization_barrier((out_part[-1], row_sum[-1]))
+    out_sum = lax.psum_scatter(out_whole, "expert", scatter_dimension=0)
 
     state_grad, attended_grad, pack = simple_call(
         functools.partial(mix_back_kernel, len(out_pieces), 2, experts),
@@ -864,7 +887,7 @@
             mixed_high,
             cotangent,
             gates,
-            jnp.pad(gate_grad, ((0, 0), (0, LANES - experts))),
+            gate_grad,
             router_lanes,
             gains,
             *row_sum,
@@ -882,7 +905,8 @@
         10,
     )
     backs = attend_back(start, q, k, v, attended_grad, logs, cosine, sine)
-    early = sum_near(pair_cores(pack))
+    early = pair_cores(pack)
+    backs, early = lax.optimization_barrier((backs, early))
     (late_pack,) = simple_call(
         project_weights_kernel,
         "project_weights",
@@ -894,15 +918,20 @@
         6,
     )
     late = pair_cores(late_pack)
+    backs, state_grad, late = lax.optimization_barrier((backs, state_grad, late))
     if four:
-        late, early, gu_one, gu_two = lax.optimization_barrier((late, early, gu_one, gu_two))
-    backs, state_grad, late, down_grad = lax.optimization_barrier(
-        (backs, state_grad, late, down_grad)
-    )
+        gu_low, gu_high, down_low, down_high, late = lax.optimization_barrier(
+            (gu_low, gu_high, down_low, down_high, late)
+        )
+    sent = late
     late = sum_near(late)
+    early = sum_near(early, late)
     if four:
-        down_own, down_one, down_two, down_far = split_parts(down_grad, 1)
-        down_low, down_high = send_far(down_far)
+        gu_low, gu_high, down_low, down_high, _ = lax.optimization_barrier(
+            (gu_low, gu_high, down_low, down_high, sent)
+        )
+        gu_one, gu_two = send_near(*join_near(gu_one, gu_two, gu_low, gu_high))
+        down_one, down_two = send_near(*join_near(down_one, down_two, down_low, down_high))
     (input_grad,) = simple_call(
         functools.partial(project_back_kernel, len(first_pieces)),
         "project_back",
@@ -917,19 +946,21 @@
         7,
     )
     late, early, input_grad = lax.optimization_barrier((late, early, input_grad))
+    state, _ = lax.optimization_barrier((state, late))
+    output = (state + out_sum.astype(F32)).astype(BF16)
     if four:
-        down_low, down_high, _ = lax.optimization_barrier((down_low, down_high, late))
-        down_one, down_two = send_near(down_one, down_two, down_low, down_high)
-        gu_parts, state, _ = lax.optimization_barrier(((gu_own, gu_one, gu_two), state, late))
+        gu_parts, _ = lax.optimization_barrier(((gu_own, gu_one, gu_two), late))
         gu_sum, expert_down_sum = add_up(gu_parts), add_up((down_own, down_one, down_two))
     else:
-        expert_down_sum = plain_scatter_sum(down_grad, 1)
-        gu_sum = plain_scatter_sum(gu_grad, 1)
+        gu_sum, expert_down_sum = plain_scatter_sum(gu_grad, 1), plain_scatter_sum(down_grad, 1)
     expert_gate_sum = gu_sum[:, :, :hidden]
     expert_up_sum = gu_sum[:, :, hidden:]
-    whole = sum_far(jnp.concatenate([late, early], axis=1))
+    whole, output, (expert_gate_sum, expert_up_sum, expert_down_sum) = sum_far(
+        jnp.concatenate([late, early], axis=1),
+        output,
+        (expert_gate_sum, expert_up_sum, expert_down_sum),
+    )
     late, early = whole[:, : late.shape[1]], whole[:, late.shape[1] :]
-    output = state + jnp.concatenate(out_sum, axis=0).astype(F32)
     projections = (
         (w_query, late[:, :q_width]),
         (key_weight, late[:, q_width : q_width + kv_width]),
@@ -940,7 +971,7 @@
     ) / gain_attn.astype(F32)
     q_end = q_width
     return (
-        output.astype(BF16),
+        output,
         input_grad,
         gain_sum,
         late[:, :q_end],

time: 474 us -> 466 us (0.983)
  starting transfers between devices: 50.9 us -> 42.1 us
  waiting for transfers between devices: 138 us -> 133 us
    ppermute x26, waiting for transfers between devices: 116 us -> 101 us  [flip_shard(): return lax.ppermute(value, 'shard', [(i, i ^ flip) for i in range(4)])]
    ppermute x4, waiting for transfers between devices: 11.7 us -> 21.7 us  [flip_layer(): lax.ppermute(value, 'expert', [(i, i ^ 2 * flip) for i in range(size)])]
  transfers between devices with their start and end apart: 49 -> 48, of which waited for: 25 -> 23; matrix products, arithmetic and copies ran while one was open for 12% -> 11% of each run, Pallas kernels for 43% -> 44%
where the time goes in v6:
time: 466 us; the launch traced here: 457 us
  Pallas kernels  201 us (43%)
  waiting for transfers between devices  133 us (29%)
  starting transfers between devices  42.1 us (9%)
  other arithmetic  33.1 us (7%)
  local copies, waits for them, and re-layouts  32.2 us (7%)
  between operations  15.5 us (3%)
    ppermute x26, waiting for transfers between devices, flip_shard(): return lax.ppermute(value, 'shard', [(i, i ^ flip) for i in range(4)])  101 us
    pallas_call x2, Pallas kernels, run_experts(): pl.pallas_call(functools.partial(expert_kernel, sources, len(arrays), len...  90.7 us
    pallas_call x5, Pallas kernels, simple_call(): pl.pallas_call(kernel, grid_spec=pltpu.PrefetchScalarGridSpec(num_scalar_...  41.2 us
    ppermute x26, starting transfers between devices, flip_shard(): return lax.ppermute(value, 'shard', [(i, i ^ flip) for i in range(4)])  29 us
    pallas_call x1, Pallas kernels, gate_up_gradient(): pl.pallas_call(functools.partial(columns_kernel, chunks, local), grid=(4,...  26.1 us
    ppermute x4, waiting for transfers between devices, flip_layer(): lax.ppermute(value, 'expert', [(i, i ^ 2 * flip) for i in range(size)])  21.7 us
    pallas_call x1, Pallas kernels, attend_back(): pl.pallas_call(attend_back_kernel, grid=(k.shape[1] // LANES,), in_specs=...  14.9 us
    pallas_call x1, Pallas kernels, down_gradient(): pl.pallas_call(functools.partial(down_kernel, chunks), grid=(4,), in_spec...  14.5 us
  transfers between devices with their start and end apart: 48, of which 23 were waited for; matrix products, arithmetic and copies ran while one was open for 11% of the time, Pallas kernels for 44%

profile of v6, /device:TPU:0, one launch (start us, length us, event | category | flops | bytes accessed | tf_op | source)
XLA Modules:
  0.0 456.7 jit_solution(3195696715070282686)
XLA Ops:
  17.6 10.9 %collective-permute-done.2.refs_3_ = bf16[128,2176]{1,0:T(8,128)(2,1)S(1)} collective-permute-done((bf16[128,2176]{1,0:T(8,128)(2,1)S(1)}, bf16[128,2176]{1,0:T(8,128)(2,1)S(1)}, u32[]{:S(2)}, u32[]{:S(2)}) %collective-permute-start.2) | collective-permute-done | bytes 557088 | tf_op jit(solution)/shard_map/ppermute | solution.py:49
  32.4 4.2 collective-permute-done.4.refs_5_
  43.9 7.8 %project.1 = (bf16[512,1024]{1,0:T(8,128)(2,1)}, bf16[512,1024]{1,0:T(8,128)(2,1)}, bf16[512,512]{1,0:T(8,128)(2,1)}, bf16[512,512]{1,0:T(8,128)(2,1)}, f32[8,1024]{1,0:T(8,128)}, /*index=5*/bf16[1024,128]{1,0:T(8,128)(2,1)}) custom-call(s32[9]{0:T(128)} %stack.79.place_ref, bf16[512,1024]{1,0:T(8,128)(2,1)} %x_ref.5, ...), custom_call_target="tpu_custom_call" | custom-call | flops 9200000000 | tf_op jit(solution)/shard_map/project/pallas_call | solution.py:452
  58.0 13.5 %attend.1 = (bf16[512,1024]{1,0:T(8,128)(2,1)}, f32[32,512]{1,0:T(8,128)}) custom-call(s32[1,512]{1,0:T(1,128)} %bitcast.72, bf16[512,1024]{1,0:T(8,128)(2,1)} %get-tuple-element.98.q_ref, bf16[512,512]{1,0:T(8,128)(2,1)} %get-tuple-element.99.k_ref, bf16[512,512]{1,0:T(8,128)(2,1)} %get-tuple-element.100.v_ref), custom_call_target="tpu_custom_call" | custom-call | flops 14949999616 | tf_op jit(solution)/shard_map/attend/pallas_call | solution.py:590
  72.5 7.5 %mix.1 = (f32[512,1024]{1,0:T(8,128)}, bf16[256,1024]{1,0:T(8,128)(2,1)}, bf16[256,1024]{1,0:T(8,128)(2,1)}, f32[512,128]{1,0:T(8,128)}) custom-call(s32[9]{0:T(128)} %stack.79.place_ref, bf16[512,1024]{1,0:T(8,128)(2,1)} %get-tuple-element.101.attended_ref, bf16[512,1024]{1,0:T(8,128)(2,1)} %x_ref.5, bf16[512,128]{1,0:T(8,128)(2,1)} %pad_convert_fusion.mask_ref, ...), custom_call_target="tpu_custom_call" | custom-call | flops 8049999872 | tf_op jit(solution)/shard_map/mix/pallas_call | solution.py:452
  83.9 34.3 %collective-permute-done.17.refs_2_ = bf16[2,384,1024]{2,1,0:T(8,128)(2,1)S(1)} collective-permute-done((bf16[2,384,1024]{2,1,0:T(8,128)(2,1)S(1)}, bf16[2,384,1024]{2,1,0:T(8,128)(2,1)S(1)}, u32[]{:S(2)}, u32[]{:S(2)}) %collective-permute-start.17) | collective-permute-done | bytes 1572896 | tf_op jit(solution)/shard_map/ppermute | solution.py:49
  125.7 13.5 %collective-permute-done.18.refs_3_ = bf16[1,384,1024]{2,1,0:T(8,128)(2,1)} collective-permute-done((bf16[1,384,1024]{2,1,0:T(8,128)(2,1)}, bf16[1,384,1024]{2,1,0:T(8,128)(2,1)}, u32[]{:S(2)}, u32[]{:S(2)}) %collective-permute-start.18) | collective-permute-done | bytes 786464 | tf_op jit(solution)/shard_map/ppermute | solution.py:49
  140.1 5.1 %all-gather.5.cloned.1.call-done.x_ref.refs_0_ = bf16[2048,1024]{1,0:T(8,128)(2,1)} async-done(((bf16[256,1024]{1,0:T(8,128)(2,1)}), bf16[2048,1024]{1,0:T(8,128)(2,1)}) %all-gather.5.cloned.1.call-update) | async-done | bytes 4194320 | tf_op jit(solution)/shard_map/all_gather | solution.py:838
  145.2 45.3 %experts.2 = (bf16[8,512,1024]{2,1,0:T(8,128)(2,1)}, bf16[2048,1024]{1,0:T(8,128)(2,1)}, bf16[2048,1024]{1,0:T(8,128)(2,1)}, bf16[2048,1024]{1,0:T(8,128)(2,1)},...) custom-call(s32[5]{0:T(128)} %stack.69.place_ref, bf16[2048,1024]{1,0:T(8,128)(2,1)} %all-gather.5.cloned.1.call-done.x_ref.refs_0_, ...), custom_call_target="tpu_custom_call" | custom-call | flops 25769803776 | bytes 29360128 | tf_op jit(solution)/shard_map/experts/pallas_call | solution.py:277
  192.7 45.4 %experts.3 = (bf16[8,512,1024]{2,1,0:T(8,128)(2,1)}, bf16[2048,1024]{1,0:T(8,128)(2,1)}, bf16[2048,1024]{1,0:T(8,128)(2,1)}, bf16[2048,1024]{1,0:T(8,128)(2,1)},...) custom-call(s32[5]{0:T(128)} %stack.69.place_ref, ...), custom_call_target="tpu_custom_call", output_to_operand_aliasing={{0}: (10, {})} | custom-call | flops 25769803776 | bytes 29360128 | tf_op jit(solution)/shard_map/experts/pallas_call | solution.py:277
  244.6 26.1 %gate_up_gradient.1 = bf16[2,1024,1024]{2,1,0:T(8,128)(2,1)} custom-call(bf16[2048,1024]{1,0:T(8,128)(2,1)} %all-gather.5.cloned.1.call-done.x_ref.refs_0_, bf16[2048,1024]{1,0:T(8,128)(2,1)} %all-gather.7.cloned.1.call-done.x_ref.refs_1_, bf16[2048,1024]{1,0:T(8,128)(2,1)} %get-tuple-element.121.refs_2_, bf16[2048,1024]{1,0:T(8,128)(2,1)} %get-tuple-element.122.refs_3_, ...), custom_call_target="tpu_custom_call" | custom-call | flops 17179869184 | bytes 25165824 | tf_op jit(solution)/shard_map/gate_up_gradient/pallas_call | solution.py:333
  280.5 14.5 %down_gradient.1 = bf16[1024,1024]{1,0:T(8,128)(2,1)} custom-call(bf16[2048,1024]{1,0:T(8,128)(2,1)} %get-tuple-element.125.refs_0_, bf16[2048,1024]{1,0:T(8,128)(2,1)} %get-tuple-element.126.refs_1_, bf16[8,528,1024]{2,1,0:T(8,128)(2,1)} %bitcast.77, bf16[8,528,1024]{2,1,0:T(8,128)(2,1)} %bitcast.78), custom_call_target="tpu_custom_call" | custom-call | flops 8589934592 | bytes 16777216 | tf_op jit(solution)/shard_map/down_gradient/pallas_call | solution.py:369
  297.7 9.7 %mix_back.1 = (f32[512,1024]{1,0:T(8,128)}, bf16[512,1024]{1,0:T(8,128)(2,1)}, bf16[1024,1152]{1,0:T(8,128)(2,1)}) custom-call(s32[9]{0:T(128)} %stack.79.place_ref, bf16[512,1024]{1,0:T(8,128)(2,1)} %get-tuple-element.101.attended_ref, f32[512,1024]{1,0:T(8,128)} %get-tuple-element.155.state_ref, bf16[256,1024]{1,0:T(8,128)(2,1)} %get-tuple-element.108.low_ref, ...), custom_call_target="tpu_custom_call" | custom-call | flops 11500000256 | tf_op jit(solution)/shard_map/mix_back/pallas_call | solution.py:452
  308.9 14.9 %attend_back.1 = (bf16[512,1024]{1,0:T(8,128)(2,1)}, bf16[512,512]{1,0:T(8,128)(2,1)}, bf16[512,512]{1,0:T(8,128)(2,1)}) custom-call(s32[1,512]{1,0:T(1,128)} %bitcast.73, bf16[512,1024]{1,0:T(8,128)(2,1)} %get-tuple-element.98.q_ref, bf16[512,512]{1,0:T(8,128)(2,1)} %get-tuple-element.99.k_ref, bf16[512,512]{1,0:T(8,128)(2,1)} %get-tuple-element.100.v_ref, ...), custom_call_target="tpu_custom_call" | custom-call | flops 17250000896 | tf_op jit(solution)/shard_map/attend_back/pallas_call | solution.py:608
  325.4 7.0 %project_weights.1 = bf16[1024,2048]{1,0:T(8,128)(2,1)} custom-call(s32[9]{0:T(128)} %stack.79.place_ref, bf16[512,1024]{1,0:T(8,128)(2,1)} %get-tuple-element.105.normed_ref, bf16[512,1024]{1,0:T(8,128)(2,1)} %get-tuple-element.150.qb_ref, bf16[512,512]{1,0:T(8,128)(2,1)} %get-tuple-element.151.kb_ref, bf16[512,512]{1,0:T(8,128)(2,1)} %get-tuple-element.152.vb_ref), custom_call_target="tpu_custom_call" | custom-call | flops 6899999744 | tf_op jit(solution)/shard_map/project_weights/pallas_call | solution.py:452
  357.7 9.2 %project_back.1 = bf16[512,1024]{1,0:T(8,128)(2,1)} custom-call(s32[9]{0:T(128)} %stack.79.place_ref, bf16[512,1024]{1,0:T(8,128)(2,1)} %x_ref.5, f32[512,1024]{1,0:T(8,128)} %get-tuple-element.149.state_grad_ref, f32[8,1024]{1,0:T(8,128)} %get-tuple-element.103.gains_ref, bf16[512,1024]{1,0:T(8,128)(2,1)} %get-tuple-element.150.qb_ref, ...), custom_call_target="tpu_custom_call" | custom-call | flops 8049999872 | tf_op jit(solution)/shard_map/project_back/pallas_call | solution.py:452
  367.6 10.2 %collective-permute-done.28 = bf16[128,2048]{1,0:T(8,128)(2,1)} collective-permute-done((bf16[128,2048]{1,0:T(8,128)(2,1)S(1)}, bf16[128,2048]{1,0:T(8,128)(2,1)}, u32[]{:S(2)}, u32[]{:S(2)}) %collective-permute-start.28) | collective-permute-done | bytes 524320 | tf_op jit(solution)/shard_map/ppermute | solution.py:49
  378.0 4.4 collective-permute-done.27
  386.4 3.8 collective-permute-start.33
  400.8 5.7 %collective-permute-done.32 = bf16[64,3200]{1,0:T(8,128)(2,1)S(1)} collective-permute-done((bf16[64,3200]{1,0:T(8,128)(2,1)S(1)}, bf16[64,3200]{1,0:T(8,128)(2,1)S(1)}, u32[]{:S(2)}, u32[]{:S(2)}) %collective-permute-start.32) | collective-permute-done | bytes 409632 | tf_op jit(solution)/shard_map/ppermute | solution.py:54
  407.4 8.1 %collective-permute-done.37 = bf16[2,256,1024]{2,1,0:T(8,128)(2,1)} collective-permute-done((bf16[2,256,1024]{2,1,0:T(8,128)(2,1)}, bf16[2,256,1024]{2,1,0:T(8,128)(2,1)}, u32[]{:S(2)}, u32[]{:S(2)}) %collective-permute-start.37) | collective-permute-done | bytes 1048608 | tf_op jit(solution)/shard_map/ppermute | solution.py:49
  420.4 3.4 collective-permute-start.34
  427.4 7.2 %collective-permute-done.34 = bf16[64,3200]{1,0:T(8,128)(2,1)S(1)} collective-permute-done((bf16[64,3200]{1,0:T(8,128)(2,1)S(1)}, bf16[64,3200]{1,0:T(8,128)(2,1)S(1)}, u32[]{:S(2)}, u32[]{:S(2)}) %collective-permute-start.34) | collective-permute-done | bytes 409632 | tf_op jit(solution)/shard_map/ppermute | solution.py:54
  434.7 5.8 %collective-permute-done.35 = bf16[64,3200]{1,0:T(8,128)(2,1)S(1)} collective-permute-done((bf16[64,3200]{1,0:T(8,128)(2,1)S(1)}, bf16[64,3200]{1,0:T(8,128)(2,1)S(1)}, u32[]{:S(2)}, u32[]{:S(2)}) %collective-permute-start.35) | collective-permute-done | bytes 409632 | tf_op jit(solution)/shard_map/ppermute | solution.py:54
  (251 shorter events, 123.8 us)
Async XLA Ops:
  7.2 115.5 %all-gather.9.cloned.1.call-start = ((), (), s32[]{:S(2)}) async-start(), calls=%async_computation.9 | async-start | bytes 9732096 | tf_op jit(solution)/shard_map/all_gather | solution.py:761
  10.8 134.4 %all-gather.5.cloned.1.call-start = ((), (), s32[]{:S(2)}) async-start(), calls=%async_computation.4 | async-start | bytes 4718592 | tf_op jit(solution)/shard_map/all_gather | solution.py:838
  54.5 17.1 %collective-permute-start.11 = (bf16[128,1024]{1,0:T(8,128)(2,1)S(1)}, bf16[128,1024]{1,0:T(8,128)(2,1)S(1)}, u32[]{:S(2)}, u32[]{:S(2)}) collective-permute-start(bf16[128,1024]{1,0:T(8,128)(2,1)S(1)} %collective-permute-done.9.refs_3_.refs_5_), channel_id=1, source_target_pairs={{0,4},{4,0},{8,12},{12,8},{16,20},{20,16},{24,28},{28,24},{1,5},{5... | collective-permute-start | bytes 786440 | tf_op jit(solution)/shard_map/ppermute | solution.py:59
  54.5 17.1 %collective-permute-start.10 = (bf16[128,1024]{1,0:T(8,128)(2,1)S(1)}, bf16[128,1024]{1,0:T(8,128)(2,1)S(1)}, u32[]{:S(2)}, u32[]{:S(2)}) collective-permute-start(bf16[128,1024]{1,0:T(8,128)(2,1)S(1)} %collective-permute-done.8.refs_1_.refs_3_), channel_id=1, source_target_pairs={{0,4},{4,0},{8,12},{12,8},{16,20},{20,16},{24,28},{28,24},{1,5},{5... | collective-permute-start | bytes 786440 | tf_op jit(solution)/shard_map/ppermute | solution.py:59
  80.0 112.7 %all-gather.7.cloned.1.call-start = ((), (), s32[]{:S(2)}) async-start(), calls=%async_computation.6 | async-start | bytes 4718592 | tf_op jit(solution)/shard_map/all_gather | solution.py:838
  80.7 216.3 %reduce-scatter.4.cloned.1.call-start = ((), (), s32[]{:S(2)}) async-start(), calls=%async_computation.5 | async-start | bytes 4718592 | tf_op jit(solution)/shard_map/reduce_scatter | solution.py:846
  81.4 36.7 %collective-permute-start.17 = (bf16[2,384,1024]{2,1,0:T(8,128)(2,1)S(1)}, bf16[2,384,1024]{2,1,0:T(8,128)(2,1)S(1)}, u32[]{:S(2)}, u32[]{:S(2)}) collective-permute-start(bf16[2,384,1024]{2,1,0:T(8,128)(2,1)S(1)} %pad_maximum_fusion.refs_0_), channel_id=1, source_target_pairs={{0,2},{1,3},{2,0},{3,1},{4,6},{5,7},{6,4},{7,5},{8,10},{9,11},{10,... | collective-permute-start | bytes 4718600 | tf_op jit(solution)/shard_map/ppermute | solution.py:49
  82.5 36.4 %collective-permute-start.16 = (bf16[2,384,1024]{2,1,0:T(8,128)(2,1)S(1)}, bf16[2,384,1024]{2,1,0:T(8,128)(2,1)S(1)}, u32[]{:S(2)}, u32[]{:S(2)}) collective-permute-start(bf16[2,384,1024]{2,1,0:T(8,128)(2,1)S(1)} %pad_maximum_fusion.refs_0_), channel_id=1, source_target_pairs={{0,1},{1,0},{2,3},{3,2},{4,5},{5,4},{6,7},{7,6},{8,9},{9,8},{10,11... | collective-permute-start | bytes 4718600 | tf_op jit(solution)/shard_map/ppermute | solution.py:49
  120.0 19.2 %collective-permute-start.18 = (bf16[1,384,1024]{2,1,0:T(8,128)(2,1)}, bf16[1,384,1024]{2,1,0:T(8,128)(2,1)}, u32[]{:S(2)}, u32[]{:S(2)}) collective-permute-start(bf16[1,384,1024]{2,1,0:T(8,128)(2,1)} %slice.109), channel_id=1, source_target_pairs={{0,1},{1,0},{2,3},{3,2},{4,5},{5,4},{6,7},{7,6},{8,9},{9,8},{10,11... | collective-permute-start | bytes 2359304 | tf_op jit(solution)/shard_map/ppermute | solution.py:49
  121.4 18.7 %collective-permute-start.19 = (bf16[1,384,1024]{2,1,0:T(8,128)(2,1)S(1)}, bf16[1,384,1024]{2,1,0:T(8,128)(2,1)}, u32[]{:S(2)}, u32[]{:S(2)}) collective-permute-start(bf16[1,384,1024]{2,1,0:T(8,128)(2,1)S(1)} %slice.110), channel_id=1, source_target_pairs={{0,2},{1,3},{2,0},{3,1},{4,6},{5,7},{6,4},{7,5},{8,10},{9,11},{10,... | collective-permute-start | bytes 2359304 | tf_op jit(solution)/shard_map/ppermute | solution.py:49
  190.5 106.5 %reduce-scatter.6.cloned.1.call-start = ((), (), s32[]{:S(2)}) async-start(), calls=%async_computation.7 | async-start | bytes 4718592 | tf_op jit(solution)/shard_map/reduce_scatter | solution.py:846
  241.0 38.1 %all-to-all-start = ((f32[8,8,128]{2,1,0:T(8,128)}), f32[8,8,128]{2,1,0:T(8,128)S(1)}, u32[]{:S(2)}, u32[]{:S(2)}) async-start(f32[8,8,128]{2,1,0:T(8,128)} %pad_maximum_fusion.9), calls=%async_computation.2 | async-start | bytes 65536 | tf_op jit(solution)/shard_map/all_to_all | solution.py:851
  244.3 173.4 %reduce-scatter.8.cloned.1.call-start = ((), (), s32[]{:S(2)}) async-start(), calls=%async_computation.8 | async-start | bytes 9437184 | tf_op jit(solution)/shard_map/reduce_scatter | solution.py:877
  273.0 24.0 %collective-permute-start.21 = (bf16[1,256,1024]{2,1,0:T(8,128)(2,1)}, bf16[1,256,1024]{2,1,0:T(8,128)(2,1)S(1)}, u32[]{:S(2)}, u32[]{:S(2)}) collective-permute-start(bf16[1,256,1024]{2,1,0:T(8,128)(2,1)} %get-tuple-element.258), channel_id=1, source_target_pairs={{0,2},{1,3},{2,0},{3,1},{4,6},{5,7},{6,4},{7,5},{8,10},{9,11},{10,... | collective-permute-start | bytes 1572872 | tf_op jit(solution)/shard_map/ppermute | solution.py:49
  274.4 22.5 %collective-permute-start.20 = (bf16[1,256,1024]{2,1,0:T(8,128)(2,1)}, bf16[1,256,1024]{2,1,0:T(8,128)(2,1)}, u32[]{:S(2)}, u32[]{:S(2)}) collective-permute-start(bf16[1,256,1024]{2,1,0:T(8,128)(2,1)} %get-tuple-element.259), channel_id=1, source_target_pairs={{0,1},{1,0},{2,3},{3,2},{4,5},{5,4},{6,7},{7,6},{8,9},{9,8},{10,11... | collective-permute-start | bytes 1572872 | tf_op jit(solution)/shard_map/ppermute | solution.py:49
  340.1 44.5 %collective-permute-start.31 = (bf16[128,1152]{1,0:T(8,128)(2,1)}, bf16[128,1152]{1,0:T(8,128)(2,1)S(1)}, u32[]{:S(2)}, u32[]{:S(2)}) collective-permute-start(bf16[128,1152]{1,0:T(8,128)(2,1)} %get-tuple-element.278), channel_id=1, source_target_pairs={{0,3},{1,2},{2,1},{3,0},{4,7},{5,6},{6,5},{7,4},{8,11},{9,10},{10,... | collective-permute-start | bytes 884744 | tf_op jit(solution)/shard_map/ppermute | solution.py:49
  342.7 42.5 %collective-permute-start.30 = (bf16[128,1152]{1,0:T(8,128)(2,1)}, bf16[128,1152]{1,0:T(8,128)(2,1)}, u32[]{:S(2)}, u32[]{:S(2)}) collective-permute-start(bf16[128,1152]{1,0:T(8,128)(2,1)} %get-tuple-element.279), channel_id=1, source_target_pairs={{0,2},{1,3},{2,0},{3,1},{4,6},{5,7},{6,4},{7,5},{8,10},{9,11},{10,... | collective-permute-start | bytes 884744 | tf_op jit(solution)/shard_map/ppermute | solution.py:49
  348.7 18.2 %collective-permute-start.26 = (bf16[128,2048]{1,0:T(8,128)(2,1)}, bf16[128,2048]{1,0:T(8,128)(2,1)}, u32[]{:S(2)}, u32[]{:S(2)}) collective-permute-start(bf16[128,2048]{1,0:T(8,128)(2,1)} %get-tuple-element.270), channel_id=1, source_target_pairs={{0,1},{1,0},{2,3},{3,2},{4,5},{5,4},{6,7},{7,6},{8,9},{9,8},{10,11... | collective-permute-start | bytes 1572872 | tf_op jit(solution)/shard_map/ppermute | solution.py:49
  349.2 28.6 %collective-permute-start.28 = (bf16[128,2048]{1,0:T(8,128)(2,1)S(1)}, bf16[128,2048]{1,0:T(8,128)(2,1)}, u32[]{:S(2)}, u32[]{:S(2)}) collective-permute-start(bf16[128,2048]{1,0:T(8,128)(2,1)S(1)} %get-tuple-element.271), channel_id=1, source_target_pairs={{0,3},{1,2},{2,1},{3,0},{4,7},{5,6},{6,5},{7,4},{8,11},{9,10},{10,... | collective-permute-start | bytes 1572872 | tf_op jit(solution)/shard_map/ppermute | solution.py:49
  351.7 30.8 %collective-permute-start.27 = (bf16[128,2048]{1,0:T(8,128)(2,1)S(1)}, bf16[128,2048]{1,0:T(8,128)(2,1)}, u32[]{:S(2)}, u32[]{:S(2)}) collective-permute-start(bf16[128,2048]{1,0:T(8,128)(2,1)S(1)} %get-tuple-element.272), channel_id=1, source_target_pairs={{0,2},{1,3},{2,0},{3,1},{4,6},{5,7},{6,4},{7,5},{8,10},{9,11},{10,... | collective-permute-start | bytes 1572872 | tf_op jit(solution)/shard_map/ppermute | solution.py:49
  367.0 18.2 %collective-permute-start.29 = (bf16[128,1152]{1,0:T(8,128)(2,1)S(1)}, bf16[128,1152]{1,0:T(8,128)(2,1)S(1)}, u32[]{:S(2)}, u32[]{:S(2)}) collective-permute-start(bf16[128,1152]{1,0:T(8,128)(2,1)S(1)} %copy-done.24), channel_id=1, source_target_pairs={{0,1},{1,0},{2,3},{3,2},{4,5},{5,4},{6,7},{7,6},{8,9},{9,8},{10,11... | collective-permute-start | bytes 884744 | tf_op jit(solution)/shard_map/ppermute | solution.py:49
  384.6 30.9 %collective-permute-start.37 = (bf16[2,256,1024]{2,1,0:T(8,128)(2,1)}, bf16[2,256,1024]{2,1,0:T(8,128)(2,1)}, u32[]{:S(2)}, u32[]{:S(2)}) collective-permute-start(bf16[2,256,1024]{2,1,0:T(8,128)(2,1)} %pad_maximum_fusion.3), channel_id=1, source_target_pairs={{0,2},{1,3},{2,0},{3,1},{4,6},{5,7},{6,4},{7,5},{8,10},{9,11},{10,... | collective-permute-start | bytes 3145736 | tf_op jit(solution)/shard_map/ppermute | solution.py:49
  390.2 16.2 %collective-permute-start.32 = (bf16[64,3200]{1,0:T(8,128)(2,1)S(1)}, bf16[64,3200]{1,0:T(8,128)(2,1)S(1)}, u32[]{:S(2)}, u32[]{:S(2)}) collective-permute-start(bf16[64,3200]{1,0:T(8,128)(2,1)S(1)} %get-tuple-element.284), channel_id=1, source_target_pairs={{0,8},{4,12},{8,0},{12,4},{16,24},{20,28},{24,16},{28,20},{1,9},{5... | collective-permute-start | bytes 1228808 | tf_op jit(solution)/shard_map/ppermute | solution.py:54
  393.6 24.2 %collective-permute-start.36 = (bf16[2,256,1024]{2,1,0:T(8,128)(2,1)S(1)}, bf16[2,256,1024]{2,1,0:T(8,128)(2,1)}, u32[]{:S(2)}, u32[]{:S(2)}) collective-permute-start(bf16[2,256,1024]{2,1,0:T(8,128)(2,1)S(1)} %pad_maximum_fusion.2), channel_id=1, source_target_pairs={{0,1},{1,0},{2,3},{3,2},{4,5},{5,4},{6,7},{7,6},{8,9},{9,8},{10,11... | collective-permute-start | bytes 3145736 | tf_op jit(solution)/shard_map/ppermute | solution.py:49
  (65 other events, 620.8 us)
Sparse Core Ops, SparseCore 0:
  10.9 86.9 all-gather.8
  99.5 45.6 all-gather.4
  146.8 45.8 all-gather.6
  194.8 48.7 reduce-scatter.3
  245.7 48.1 reduce-scatter.5
  297.2 89.1 reduce-scatter.7
